TPU v7x, 512 devices: a whole 4x8x8 slice. The times are simulated.
512 devices in a mesh: dp: 16 (over z_hi, y), tensor: 32 (over x, z_lo, core).
Axes of the slice: x: 4, y: 8, z: 8 (z_hi: 2, z_lo: 4; z = z_hi * 4 + z_lo), core: 2. Of those that a mesh axis runs over, the one named last changes fastest.
Arguments:
- inputs: bfloat16 [3072, 5120], P('dp', 'tensor'), may hold values from -6 to 6
- grad_out: bfloat16 [3072, 5120], P('dp', 'tensor'), may hold values from -6 to 6
- gate_codes: int32 [5120, 8192], P('dp', 'tensor'), may hold values from 0 to 127
- up_codes: int32 [5120, 8192], P('dp', 'tensor'), may hold values from 0 to 127
- down_codes: int32 [5120, 8192], P('dp', 'tensor'), may hold values from 0 to 127
Outputs:
- input_grad: bfloat16 [3072, 5120], P(('dp', 'tensor'))
- down_log_grad: float32 [5120, 8192], P('dp', 'tensor')
Inputs may be any that keep to these rules, and one draw needn't show every extreme that they name: `gate_codes`: each word holds a sign bit (bit 0, 1 meaning negative) and a log-magnitude code (the word divided by 2). `up_codes`: each word holds a sign bit (bit 0, 1 meaning negative) and a log-magnitude code (the word divided by 2). `down_codes`: each word holds a sign bit (bit 0, 1 meaning negative) and a log-magnitude code (the word divided by 2).
All inputs are finite; a program needn't handle non-finite values.
Results may differ from a plain program's by a relative error of at most 0.024.
Values may be sent and summed in bfloat16 or wider, within the bound.
No kernel may reach another device: no remote copies, remote signals or barrier semaphores. Data moves between devices by JAX's collectives and lax.ppermute only.
A program may use at most 64 MiB of HBM per device.

v0:
```python
import math

import jax
import jax.numpy as jnp
from jax import lax
from jax.sharding import PartitionSpec as P

D = 5120
FF_W = 8192


coef_one = 0.6931472
coef_two = 0.2402265
coef_three = 0.0555041


def decode(packed, fan):
    sign_bit = packed % 2
    level = packed // 2
    whole = level // 8
    frac = (level % 8).astype(jnp.float32) / 8.0
    power = jnp.where(whole % 2 == 1, 0.5, 1.0).astype(jnp.float32)
    power = power * jnp.where(whole // 2 % 2 == 1, 0.25, 1.0).astype(jnp.float32)
    power = power * jnp.where(whole // 4 % 2 == 1, 0.0625, 1.0).astype(jnp.float32)
    poly = 1.0 - frac * (coef_one - frac * (coef_two - coef_three * frac))
    factor = 1.0 - 2.0 * sign_bit.astype(jnp.float32)
    return factor * power * poly * (3.0 / math.sqrt(fan))


def on_device(inputs, grad_out, gate_codes, up_codes, down_codes):
    gate_local = decode(gate_codes, D).astype(jnp.bfloat16)
    up_local = decode(up_codes, D).astype(jnp.bfloat16)
    down_decoded = decode(down_codes, FF_W)
    down_local = down_decoded.astype(jnp.bfloat16)
    gate_full, up_full, down_full = (
        lax.all_gather(gate_local, "dp", axis=0, tiled=True),
        lax.all_gather(up_local, "dp", axis=0, tiled=True),
        lax.all_gather(down_local, "dp", axis=0, tiled=True),
    )
    acts, cotangent = (
        lax.all_gather(inputs, "tensor", axis=1, tiled=True),
        lax.all_gather(grad_out, "tensor", axis=1, tiled=True),
    )
    gate = jnp.dot(acts, gate_full, preferred_element_type=jnp.float32)
    up = jnp.dot(acts, up_full, preferred_element_type=jnp.float32)
    sig = jax.nn.sigmoid(gate)
    hidden = (gate * sig * up).astype(jnp.bfloat16)
    hidden_grad = jnp.dot(cotangent, down_full, preferred_element_type=jnp.float32)
    gate_grad = (hidden_grad * up * sig * (1.0 + gate * (1.0 - sig))).astype(jnp.bfloat16)
    up_grad = (hidden_grad * gate * sig).astype(jnp.bfloat16)
    dims = (((1,), (1,)), ((), ()))
    term = lax.dot_general(gate_grad, gate_full, dims, preferred_element_type=jnp.float32)
    input_grad = lax.psum_scatter(
        (term + lax.dot_general(up_grad, up_full, dims, preferred_element_type=jnp.float32)).astype(
            jnp.bfloat16
        ),
        "tensor",
        scatter_dimension=0,
        tiled=True,
    )
    down_grad = lax.psum_scatter(
        lax.dot_general(
            cotangent, hidden, (((0,), (0,)), ((), ())), preferred_element_type=jnp.float32
        ).astype(jnp.bfloat16),
        "dp",
        scatter_dimension=0,
        tiled=True,
    ).astype(jnp.float32)
    return (input_grad, down_grad * down_decoded)


def solution(mesh):
    in_specs = (
        P("dp", "tensor"),
        P("dp", "tensor"),
        P("dp", "tensor"),
        P("dp", "tensor"),
        P("dp", "tensor"),
    )
    out_specs = (P(("dp", "tensor"), None), P("dp", "tensor"))
    return jax.shard_map(
        on_device, mesh=mesh, in_specs=in_specs, out_specs=out_specs, check_vma=False
    )
```

profile of v0, /device:TPU:1, one launch (start us, length us, event | category | flops | bytes accessed | tf_op | source)
XLA Modules:
  0.0 842.0 jit_solution(1999338271359362980)
XLA Ops:
  7.2 0.0 all-gather.12.cloned.1.call-start
  7.2 0.7 all-gather.12.cloned.1.call-update
  7.9 0.0 all-gather.14.cloned.1.call-start
  7.9 3.1 fusion.36
  11.0 0.0 all-gather.14.cloned.1.call-update
  11.0 0.0 all-gather.10.cloned.1.call-start
  11.1 3.1 fusion.22
  14.1 0.0 all-gather.10.cloned.1.call-update
  14.2 0.0 all-gather.8.cloned.1.call-start
  14.2 0.5 all-gather.8.cloned.1.call-update
  14.7 0.0 reduce-scatter.6.cloned.1.call-start
  14.8 65.3 %all-gather.12.cloned.1.call-done = bf16[192,5120]{0,1:T(8,128)(2,1)} async-done(((bf16[192,160]{0,1:T(8,128)(2,1)}), bf16[192,5120]{0,1:T(8,128)(2,1)}) %all-gather.12.cloned.1.call-update) | async-done | bytes 1966096 | tf_op jit(solution)/shard_map/all_gather | solution.py:41
  80.1 112.0 %all-gather.14.cloned.1.call-done = bf16[5120,256]{1,0:T(8,128)(2,1)} async-done(((bf16[320,256]{1,0:T(8,128)(2,1)}), bf16[5120,256]{1,0:T(8,128)(2,1)}) %all-gather.14.cloned.1.call-update) | async-done | bytes 2621456 | tf_op jit(solution)/shard_map/all_gather | solution.py:36
  192.0 3.6 convolution_bitcast_fusion
  195.6 106.6 %all-gather.10.cloned.1.call-done = bf16[5120,256]{1,0:T(8,128)(2,1)} async-done(((bf16[320,256]{1,0:T(8,128)(2,1)}), bf16[5120,256]{1,0:T(8,128)(2,1)}) %all-gather.10.cloned.1.call-update) | async-done | bytes 2621456 | tf_op jit(solution)/shard_map/all_gather | solution.py:37
  302.2 2.8 convolution_bitcast_fusion.1
  305.0 60.7 %all-gather.8.cloned.1.call-done = bf16[192,5120]{0,1:T(8,128)(2,1)} async-done(((bf16[192,160]{0,1:T(8,128)(2,1)}), bf16[192,5120]{0,1:T(8,128)(2,1)}) %all-gather.8.cloned.1.call-update) | async-done | bytes 1966096 | tf_op jit(solution)/shard_map/all_gather | solution.py:42
  365.7 2.7 fusion.2
  368.4 2.6 copy.21
  371.0 0.0 reduce-scatter.6.cloned.1.call-update
  371.0 0.0 all-gather.6.cloned.1.call-start
  371.1 231.2 %reduce-scatter.6.cloned.1.call-done = bf16[320,256]{1,0:T(8,128)(2,1)} async-done(((bf16[5120,256]{1,0:T(8,128)(2,1)}), bf16[320,256]{1,0:T(8,128)(2,1)}) %reduce-scatter.6.cloned.1.call-update) | async-done | bytes 163856 | tf_op jit(solution)/shard_map/reduce_scatter | solution.py:61
  602.3 3.1 convert_multiply_fusion
  605.4 0.0 all-gather.6.cloned.1.call-update
  605.4 110.4 %all-gather.6.cloned.1.call-done = bf16[5120,256]{1,0:T(8,128)(2,1)} async-done(((bf16[320,256]{1,0:T(8,128)(2,1)}), bf16[5120,256]{1,0:T(8,128)(2,1)}) %all-gather.6.cloned.1.call-update) | async-done | bytes 2621456 | tf_op jit(solution)/shard_map/all_gather | solution.py:38
  715.8 3.6 convolution_bitcast_fusion.2
  719.4 1.0 fusion.59
  720.4 0.7 copy-done.2
  721.1 1.0 fusion.1
  722.2 83.0 %fusion = bf16[8,5120]{1,0:T(8,128)(2,1)S(1)} fusion(bf16[192,5120]{1,0:T(8,128)(2,1)S(1)} %fusion.1), kind=kCustom, calls=%all-reduce-scatter | all-reduce-scatter fusion | flops 1310721 | bytes 2050048
  805.1 2.1 collective-permute-start
  807.3 1.3 collective-permute-start.1
  808.6 1.3 collective-permute-start.7
  809.9 1.3 collective-permute-start.2
  811.2 1.8 collective-permute-start.3
  813.0 0.0 collective-permute-done.7
  813.0 5.8 collective-permute-start.4
  818.8 0.0 collective-permute-done
  818.8 5.0 collective-permute-start.5
  823.8 0.0 collective-permute-done.1
  823.8 5.7 collective-permute-start.6
  829.5 1.3 dynamic-slice.4
  831.4 0.0 collective-permute-done.2
  831.4 0.0 collective-permute-done.3
  831.4 0.0 collective-permute-done.4
  831.4 0.7 collective-permute-done.6
  832.1 2.3 concatenate
  834.5 0.7 constant_dynamic-slice_fusion
  (9 shorter events, 0.0 us)
Async XLA Ops:
  7.2 72.9 %all-gather.12.cloned.1.call-start = ((), (), s32[]{:S(2)}) async-start(), calls=%async_computation.4 | async-start | bytes 2703360 | tf_op jit(solution)/shard_map/all_gather | solution.py:41
  7.9 184.1 %all-gather.14.cloned.1.call-start = ((), (), s32[]{:S(2)}) async-start(), calls=%async_computation.5 | async-start | bytes 2785280 | tf_op jit(solution)/shard_map/all_gather | solution.py:36
  11.0 291.2 %all-gather.10.cloned.1.call-start = ((), (), s32[]{:S(2)}) async-start(), calls=%async_computation.3 | async-start | bytes 2785280 | tf_op jit(solution)/shard_map/all_gather | solution.py:37
  14.2 351.5 %all-gather.8.cloned.1.call-start = ((), (), s32[]{:S(2)}) async-start(), calls=%async_computation.2 | async-start | bytes 2703360 | tf_op jit(solution)/shard_map/all_gather | solution.py:42
  14.7 587.5 %reduce-scatter.6.cloned.1.call-start = ((), (), s32[]{:S(2)}) async-start(), calls=%async_computation.6 | async-start | bytes 2785280 | tf_op jit(solution)/shard_map/reduce_scatter | solution.py:61
  80.1 222.2 %copy-start.1 = (bf16[192,5120]{0,1:T(8,128)(2,1)S(1)}, bf16[192,5120]{0,1:T(8,128)(2,1)}, u32[]{:S(2)}) copy-start(bf16[192,5120]{0,1:T(8,128)(2,1)} %all-gather.12.cloned.1.call-done) | copy-start | bytes 5898244
  371.0 231.3 %copy-start.3 = (s32[320,256]{1,0:T(8,128)S(1)}, s32[320,256]{1,0:T(8,128)}, u32[]{:S(2)}) copy-start(s32[320,256]{1,0:T(8,128)} %param.9) | copy-start | bytes 983044
  371.0 344.8 %all-gather.6.cloned.1.call-start = ((), (), s32[]{:S(2)}) async-start(), calls=%async_computation.1 | async-start | bytes 2785280 | tf_op jit(solution)/shard_map/all_gather | solution.py:38
  605.4 114.0 %copy-start = (bf16[5120,256]{1,0:T(8,128)(2,1)S(1)}, bf16[5120,256]{1,0:T(8,128)(2,1)}, u32[]{:S(2)}) copy-start(bf16[5120,256]{1,0:T(8,128)(2,1)} %all-gather.14.cloned.1.call-done) | copy-start | bytes 7864324
  719.4 1.7 copy-start.2
  805.1 13.6 %collective-permute-start = (bf16[8,5120]{1,0:T(8,128)(2,1)S(1)}, bf16[8,5120]{1,0:T(8,128)(2,1)S(1)}, u32[]{:S(2)}, u32[]{:S(2)}) collective-permute-start(bf16[8,5120]{1,0:T(8,128)(2,1)S(1)} %fusion), channel_id=1, source_target_pairs={{0,1},{1,2},{2,3},{3,4},{4,5},{5,6},{6,7},{7,8},{8,9},{9,10},{10,1... | collective-permute-start | bytes 245768
  807.3 16.5 %collective-permute-start.1 = (bf16[8,5120]{1,0:T(8,128)(2,1)S(1)}, bf16[8,5120]{1,0:T(8,128)(2,1)S(1)}, u32[]{:S(2)}, u32[]{:S(2)}) collective-permute-start(bf16[8,5120]{1,0:T(8,128)(2,1)S(1)} %fusion), channel_id=1, source_target_pairs={{0,2},{1,3},{2,4},{3,5},{4,6},{5,7},{6,8},{7,9},{8,10},{9,11},{10,... | collective-permute-start | bytes 245768
  808.6 4.4 collective-permute-start.7
  809.9 21.5 %collective-permute-start.2 = (bf16[8,5120]{1,0:T(8,128)(2,1)S(1)}, bf16[8,5120]{1,0:T(8,128)(2,1)S(1)}, u32[]{:S(2)}, u32[]{:S(2)}) collective-permute-start(bf16[8,5120]{1,0:T(8,128)(2,1)S(1)} %fusion), channel_id=1, source_target_pairs={{0,3},{1,4},{2,5},{3,6},{4,7},{5,8},{6,9},{7,10},{8,11},{9,12},{10... | collective-permute-start | bytes 245768
  811.2 20.2 %collective-permute-start.3 = (bf16[8,5120]{1,0:T(8,128)(2,1)S(1)}, bf16[8,5120]{1,0:T(8,128)(2,1)S(1)}, u32[]{:S(2)}, u32[]{:S(2)}) collective-permute-start(bf16[8,5120]{1,0:T(8,128)(2,1)S(1)} %fusion), channel_id=1, source_target_pairs={{0,4},{1,5},{2,6},{3,7},{4,8},{5,9},{6,10},{7,11},{8,12},{9,13},{1... | collective-permute-start | bytes 245768
  813.0 18.4 %collective-permute-start.4 = (bf16[8,5120]{1,0:T(8,128)(2,1)S(1)}, bf16[8,5120]{1,0:T(8,128)(2,1)S(1)}, u32[]{:S(2)}, u32[]{:S(2)}) collective-permute-start(bf16[8,5120]{1,0:T(8,128)(2,1)S(1)} %fusion), channel_id=1, source_target_pairs={{0,5},{1,6},{2,7},{3,8},{4,9},{5,10},{6,11},{7,12},{8,13},{9,14},{... | collective-permute-start | bytes 245768
  818.8 12.6 %collective-permute-start.5 = (bf16[8,5120]{1,0:T(8,128)(2,1)S(1)}, bf16[8,5120]{1,0:T(8,128)(2,1)S(1)}, u32[]{:S(2)}, u32[]{:S(2)}) collective-permute-start(bf16[8,5120]{1,0:T(8,128)(2,1)S(1)} %fusion), channel_id=1, source_target_pairs={{0,6},{1,7},{2,8},{3,9},{4,10},{5,11},{6,12},{7,13},{8,14},{9,15},... | collective-permute-start | bytes 245768
  823.8 8.3 collective-permute-start.6
Sparse Core Ops, SparseCore 0:
  10.1 69.8 all-gather.11
  83.8 108.1 all-gather.13
  195.2 106.9 all-gather.9
  304.2 61.4 all-gather.7
  371.2 231.0 reduce-scatter.5
  605.8 109.9 all-gather.5
where the time goes:
time: 843 us; the launch traced here: 842 us
  waiting for transfers between devices  688 us (82%)
  blocking collectives  83 us (10%)
  starting transfers between devices  24.4 us (3%)
  between operations  15 us (2%)
  matrix products  14.6 us (2%)
  other arithmetic  9.26 us (1%)
    reduce_scatter x1, waiting for transfers between devices, on_device(): lax.psum_scatter(lax.dot_general(cotangent, hidden, (((0,), (0,)), ((), (...  231 us
    all_gather x1, waiting for transfers between devices, on_device(): lax.all_gather(gate_local, 'dp', axis=0, tiled=True)  112 us
    all_gather x1, waiting for transfers between devices, on_device(): lax.all_gather(down_local, 'dp', axis=0, tiled=True)  110 us
    all_gather x1, waiting for transfers between devices, on_device(): lax.all_gather(up_local, 'dp', axis=0, tiled=True)  107 us
    unnamed x1, blocking collectives  83 us
    all_gather x1, waiting for transfers between devices, on_device(): lax.all_gather(inputs, 'tensor', axis=1, tiled=True)  65.3 us
    all_gather x1, waiting for transfers between devices, on_device(): lax.all_gather(grad_out, 'tensor', axis=1, tiled=True)  60.7 us
    unnamed x8, starting transfers between devices  24.2 us
  transfers between devices with their start and end apart: 14, of which 7 were waited for; matrix products, arithmetic and copies ran while one was open for 2% of the time, Pallas kernels for 0%

commit v1 on v0

v1 whole, which is shorter than its diff:
```python
import math

import jax
import jax.numpy as jnp
from jax import lax
from jax.experimental import pallas as pl
from jax.experimental.pallas import tpu as pltpu
from jax.sharding import PartitionSpec as P

D = 5120
FF_W = 8192
N_Z, N_Y, N_X, N_ZL = 2, 8, 4, 4
N_T = N_X * N_ZL * 2
TOK = 192
FEAT = 160
ROWS = 320
COLS = 256
HALF = D // 2

coef_one = 0.6931472
coef_two = 0.2402265
coef_three = 0.0555041

NN = (((1,), (0,)), ((), ()))
NT = (((1,), (1,)), ((), ()))


def _swap_pairs():
    pairs = []
    for z in range(N_Z):
        for y in range(N_Y):
            for t in range(N_T):
                x1, rest = t // 16, t % 16
                pairs.append(((z * N_Y + y) * N_T + t, (x1 * N_Y + y) * N_T + z * 16 + rest))
    return pairs


SWAP = _swap_pairs()
Z_SWAP = [(d, (d + N_Y) % (N_Z * N_Y)) for d in range(N_Z * N_Y)]
CORE_SWAP = [(t, t ^ 1) for t in range(N_T)]
ZC_GROUPS = [[x * 8 + i for i in range(8)] for x in range(N_X)]
X_GROUPS = [[x * 8 + i for x in range(N_X)] for i in range(8)]
Y_GROUPS = [[z * N_Y + y for y in range(N_Y)] for z in range(N_Z)]
ZXZ_GROUPS = [
    [(z * N_Y + y) * N_T + x * 8 + zl * 2 + c for z in range(N_Z) for x in range(N_X) for zl in range(N_ZL)]
    for y in range(N_Y)
    for c in range(2)
]


def decode(packed, fan):
    frac = ((packed >> 1) & 7).astype(jnp.float32) * 0.125
    power = jnp.where((packed & 16) != 0, 0.5, 1.0)
    power = power * jnp.where((packed & 32) != 0, 0.25, 1.0)
    power = power * jnp.where((packed & 64) != 0, 0.0625, 1.0)
    poly = 1.0 - frac * (coef_one - frac * (coef_two - coef_three * frac))
    value = power * poly * (3.0 / math.sqrt(fan))
    return jnp.where((packed & 1) != 0, -value, value)


def decode_kernel(gate_ref, up_ref, down_ref, out_ref):
    out_ref[:, 0:COLS] = decode(gate_ref[...], D).astype(jnp.bfloat16)
    out_ref[:, COLS : 2 * COLS] = decode(up_ref[...], D).astype(jnp.bfloat16)
    out_ref[:, 2 * COLS :] = decode(down_ref[...], FF_W).astype(jnp.bfloat16)


def forward_kernel(pos_ref, near_ref, far_ref, w_ref, own_ref, send_ref):
    z, core = pos_ref[0], pos_ref[1]
    for rel in range(2):
        h = z if rel == 0 else 1 - z
        gate_up = jnp.zeros((TOK, 2 * COLS), jnp.float32)
        hidden_grad = jnp.zeros((TOK, COLS), jnp.float32)
        for x0 in range(2):
            for far in range(2):
                pair = core if far == 0 else 1 - core
                acts_ref = far_ref if far else near_ref
                acts = acts_ref[2 * h + x0].T
                w = w_ref[pl.ds(x0 * 4 + 2 * pair, 2)].reshape(2 * ROWS, 3 * COLS)
                gate_up += lax.dot_general(acts[:TOK], w[:, : 2 * COLS], NN, preferred_element_type=jnp.float32)
                hidden_grad += lax.dot_general(acts[TOK:], w[:, 2 * COLS :], NN, preferred_element_type=jnp.float32)
        target = own_ref if rel == 0 else send_ref
        target[:, : 2 * COLS] = gate_up.astype(target.dtype)
        target[:, 2 * COLS :] = hidden_grad.astype(target.dtype)


def middle_kernel(own_ref, got_ref, out_ref):
    total = own_ref[...] + got_ref[...].astype(jnp.float32)
    gate, up, hidden_grad = total[:, :COLS], total[:, COLS : 2 * COLS], total[:, 2 * COLS :]
    sig = jax.nn.sigmoid(gate)
    out_ref[:, :COLS] = (hidden_grad * up * sig * (1.0 + gate * (1.0 - sig))).astype(jnp.bfloat16)
    out_ref[:, COLS : 2 * COLS] = (hidden_grad * gate * sig).astype(jnp.bfloat16)
    out_ref[:, 2 * COLS :] = (gate * sig * up).astype(jnp.bfloat16)


def down_kernel(pos_ref, near_ref, far_ref, own_ref, got_ref, out_ref):
    z, core = pos_ref[0], pos_ref[1]
    blank = jnp.zeros((TOK, COLS), jnp.bfloat16)
    hidden = jnp.concatenate([blank, own_ref[:, 2 * COLS :], blank, got_ref[:, 2 * COLS :]], axis=0)
    for x0 in range(2):
        for far in range(2):
            pair = core if far == 0 else 1 - core
            acts_ref = far_ref if far else near_ref
            acts = jnp.concatenate([acts_ref[2 * z + x0], acts_ref[2 * (1 - z) + x0]], axis=1)
            part = lax.dot_general(acts, hidden, NN, preferred_element_type=jnp.float32)
            out_ref[pl.ds(x0 * 4 + 2 * pair, 2)] = part.astype(jnp.bfloat16).reshape(2, ROWS, COLS)


def input_kernel(pos_ref, own_ref, got_ref, w_ref, keep_ref, send_ref):
    z, core = pos_ref[0], pos_ref[1]
    shape = (2 * 128, TOK)
    row = lax.broadcasted_iota(jnp.int32, shape, 0)
    col = lax.broadcasted_iota(jnp.int32, shape, 1)
    inner = row & 7
    group = (row >> 3) & 15
    side = (row >> 7) ^ core
    wanted = group * 12 + side * 6 + inner
    pick = jnp.where((wanted == col) & (inner < 6), 1.0, 0.0).astype(jnp.bfloat16)
    grads = []
    for ref in (own_ref, got_ref):
        picked = lax.dot_general(pick, ref[:, : 2 * COLS], NN, preferred_element_type=jnp.float32)
        grads.append(picked.astype(jnp.bfloat16))
    grads = jnp.concatenate(grads, axis=0)
    for q in range(4):
        w = w_ref[2 * q : 2 * q + 2].reshape(2 * ROWS, 3 * COLS)[:, : 2 * COLS]
        part = lax.dot_general(grads, w, NT, preferred_element_type=jnp.float32).astype(jnp.bfloat16)
        at = slice(q * 2 * ROWS, (q + 1) * 2 * ROWS)
        keep_ref[z, :, at] = part[0:128]
        send_ref[z, :, at] = part[128:256]
        keep_ref[1 - z, :, at] = part[256:384]
        send_ref[1 - z, :, at] = part[384:512]


VMEM = pl.BlockSpec(memory_space=pltpu.VMEM)
SMEM = pl.BlockSpec(memory_space=pltpu.SMEM)


def call(kernel, out_shapes, *args, name, flops=0):
    specs = [SMEM if a.dtype == jnp.int32 and a.ndim == 1 else VMEM for a in args]
    moved = sum(a.size * a.dtype.itemsize for a in args)
    moved += sum(o.size * o.dtype.itemsize for o in jax.tree.leaves(out_shapes))
    return pl.pallas_call(
        kernel,
        out_shape=out_shapes,
        in_specs=specs,
        out_specs=jax.tree.map(lambda _: VMEM, out_shapes),
        compiler_params=pltpu.CompilerParams(vmem_limit_bytes=48 * 2**20),
        cost_estimate=pl.CostEstimate(flops=flops, bytes_accessed=moved, transcendentals=0),
        name=name,
    )(*args)


def shaped(shape, dtype=jnp.bfloat16):
    return jax.ShapeDtypeStruct(shape, dtype)


def on_device(inputs, grad_out, gate_codes, up_codes, down_codes):
    dp, tensor = lax.axis_index("dp"), lax.axis_index("tensor")
    z, core = dp // N_Y, tensor % 2
    pos = jnp.stack([z, core]).astype(jnp.int32)

    w_own = call(decode_kernel, shaped((ROWS, 3 * COLS)), gate_codes, up_codes, down_codes, name="decode")
    w = lax.all_gather(w_own, "dp", axis=0, axis_index_groups=Y_GROUPS)

    acts = jnp.concatenate([inputs.T, grad_out.T], axis=1)
    acts = lax.ppermute(acts, ("dp", "tensor"), SWAP)
    acts = lax.all_gather(acts, "tensor", axis=0, axis_index_groups=ZC_GROUPS, tiled=True)
    mine = lax.dynamic_slice_in_dim(acts, core * 4 * FEAT, 4 * FEAT, 0)
    mine = jnp.broadcast_to(mine[None], (N_X, 4 * FEAT, 2 * TOK))
    near = lax.all_to_all(mine, "tensor", 0, 0, axis_index_groups=X_GROUPS, tiled=True)
    far = lax.ppermute(near, "tensor", CORE_SWAP)

    flops = 2 * HALF * 3 * COLS * 2 * TOK
    own, send = call(
        forward_kernel,
        (shaped((TOK, 3 * COLS), jnp.float32), shaped((TOK, 3 * COLS))),
        pos, near, far, w, name="forward", flops=flops,
    )
    got = lax.ppermute(send, "dp", Z_SWAP)
    own = call(middle_kernel, shaped((TOK, 3 * COLS)), own, got, name="middle")
    got = lax.ppermute(own, "dp", Z_SWAP)

    down = call(down_kernel, shaped((N_Y, ROWS, COLS)), pos, near, far, own, got, name="down", flops=flops // 3)
    down_grad = lax.psum_scatter(
        down.reshape(N_Y * ROWS, COLS), "dp", scatter_dimension=0, axis_index_groups=Y_GROUPS, tiled=True
    )

    keep, send = call(
        input_kernel,
        (shaped((2, 128, HALF)), shaped((2, 128, HALF))),
        pos, own, got, w, name="input", flops=2 * flops // 3,
    )
    other = lax.ppermute(send, "tensor", CORE_SWAP)
    summed = (keep.astype(jnp.float32) + other.astype(jnp.float32)).astype(jnp.bfloat16)
    parts = lax.all_to_all(
        summed.reshape(32, 8, HALF), ("dp", "tensor"), 0, 0, axis_index_groups=ZXZ_GROUPS, tiled=True
    )
    total = jnp.sum(parts.reshape(2, 16, 8, HALF).astype(jnp.float32), axis=1).astype(jnp.bfloat16)
    input_grad = jnp.concatenate([total[0, :6], total[1, :6]], axis=1)
    return input_grad, down_grad.astype(jnp.float32) * decode(down_codes, FF_W)


def solution(mesh):
    in_specs = (P("dp", "tensor"),) * 5
    out_specs = (P(("dp", "tensor"), None), P("dp", "tensor"))
    return jax.shard_map(on_device, mesh=mesh, in_specs=in_specs, out_specs=out_specs, check_vma=False)
```

time: 843 us -> 190 us (0.23)
  waiting for transfers between devices: 688 us -> 48.5 us
  blocking collectives: 83 us -> 63.4 us
  Pallas kernels: 0 us -> 15.6 us
  matrix products: 14.6 us -> 0 us
  starting transfers between devices: 24.4 us -> 38.5 us
    all_gather x5 -> x1, waiting for transfers between devices: 455 us -> 0.01 us  [on_device(): w = lax.all_gather(w_own, 'dp', axis=0, axis_index_groups=Y_GROUPS)]
    reduce_scatter x1, waiting for transfers between devices: 231 us -> 26.2 us  [on_device(): lax.psum_scatter(down.reshape(N_Y * ROWS, COLS), 'dp', scatter_dimension=...]
    unnamed x1 -> x0, blocking collectives: 83 us -> none
    all_to_all x0 -> x1, blocking collectives: none -> 37.7 us  [on_device(): lax.all_to_all(mine, 'tensor', 0, 0, axis_index_groups=X_GROUPS, tiled=True)]
    ppermute x0 -> x5, starting transfers between devices: none -> 29.9 us  [the longest x1 11.5 us: on_device(): other = lax.ppermute(send, 'tensor', CORE_SWAP)]
    all_gather x0 -> x1, blocking collectives: none -> 25.6 us  [on_device(): lax.all_gather(acts, 'tensor', axis=0, axis_index_groups=ZC_GROUPS, tiled...]
    unnamed x8 -> x0, starting transfers between devices: 24.2 us -> none
    ppermute x0 -> x5, waiting for transfers between devices: none -> 16.8 us  [the longest x1 8.8 us: on_device(): got = lax.ppermute(send, 'dp', Z_SWAP)]
  transfers between devices with their start and end apart: 14 -> 8, of which waited for: 7 -> 5; matrix products, arithmetic and copies ran while one was open for 2% -> 3% of each run, Pallas kernels for 0% -> 2%
where the time goes in v1:
time: 190 us; the launch traced here: 189 us
  blocking collectives  63.4 us (33%)
  waiting for transfers between devices  48.5 us (26%)
  starting transfers between devices  38.5 us (20%)
  Pallas kernels  15.6 us (8%)
  between operations  14.2 us (7%)
  other arithmetic  5.64 us (3%)
  local copies, waits for them, and re-layouts  3.15 us (2%)
    all_to_all x1, blocking collectives, on_device(): lax.all_to_all(mine, 'tensor', 0, 0, axis_index_groups=X_GROUPS, tiled=True)  37.7 us
    reduce_scatter x1, waiting for transfers between devices, on_device(): lax.psum_scatter(down.reshape(N_Y * ROWS, COLS), 'dp', scatter_dimension=...  26.2 us
    all_gather x1, blocking collectives, on_device(): lax.all_gather(acts, 'tensor', axis=0, axis_index_groups=ZC_GROUPS, tiled...  25.6 us
    pallas_call x5, Pallas kernels, call(): pl.pallas_call(kernel, out_shape=out_shapes, in_specs=specs, out_specs=ja...  15.6 us
    ppermute x1, starting transfers between devices, on_device(): other = lax.ppermute(send, 'tensor', CORE_SWAP)  11.5 us
    ppermute x1, waiting for transfers between devices, on_device(): got = lax.ppermute(send, 'dp', Z_SWAP)  8.8 us
    all_to_all x1, starting transfers between devices, on_device(): lax.all_to_all(summed.reshape(32, 8, HALF), ('dp', 'tensor'), 0, 0, axis_...  8.56 us
    ppermute x1, starting transfers between devices, on_device(): got = lax.ppermute(send, 'dp', Z_SWAP)  7.54 us
  transfers between devices with their start and end apart: 8, of which 5 were waited for; matrix products, arithmetic and copies ran while one was open for 3% of the time, Pallas kernels for 2%

profile of v1, /device:TPU:1, one launch (start us, length us, event | category | flops | bytes accessed | tf_op | source)
XLA Modules:
  0.0 189.0 jit_solution(7346297916165170573)
XLA Ops:
  7.2 0.0 all-gather.3.cloned.1.call-start
  7.2 0.0 copy-start
  7.2 1.0 copy-done
  8.2 0.0 copy-start.2
  8.2 1.0 copy-done.2
  9.2 0.0 copy-start.3
  9.2 1.0 copy-done.3
  10.1 0.0 copy-start.4
  10.1 0.0 copy-start.5
  10.1 1.7 decode.1
  11.8 0.0 all-gather.3.cloned.1.call-update
  11.8 0.0 reduce-scatter.2.cloned.1.call-start
  11.9 0.0 copy-done.4
  11.9 0.0 copy-done.5
  11.9 0.1 pad_maximum_fusion
  12.0 0.7 collective-permute-start
  12.7 0.0 collective-permute-done
  12.7 25.6 %all_gather.9 = bf16[1280,384]{1,0:T(8,128)(2,1)S(1)} all-gather(bf16[160,384]{1,0:T(8,128)(2,1)S(1)} %collective-permute-done), channel_id=1, replica_groups={{0,1,2,3,4,5,6,7},{8,9,10,11,12,13,14,15},{16,17,18,19,20,21,22,23},{24..., dimensions={0}, use_global_device_ids=true | all-gather | bytes 1105920 | tf_op jit(solution)/shard_map/all_gather | solution.py:166
  38.4 0.1 constant_dynamic-slice_fusion
  38.4 0.2 broadcast_in_dim.22
  38.6 37.7 %all_to_all.10.near_ref = bf16[4,640,384]{2,1,0:T(8,128)(2,1)S(1)} all-to-all(bf16[4,640,384]{2,1,0:T(8,128)(2,1)S(1)} %broadcast_in_dim.22), channel_id=1, replica_groups={{0,8,16,24},{1,9,17,25},{2,10,18,26},{3,11,19,27},{4,12,20,28},{5,13,21..., dimensions={0} | all-to-all | bytes 3932160 | tf_op jit(solution)/shard_map/all_to_all | solution.py:169
  76.3 3.2 %collective-permute-start.1 = (bf16[4,640,384]{2,1,0:T(8,128)(2,1)S(1)}, bf16[4,640,384]{2,1,0:T(8,128)(2,1)}, u32[]{:S(2)}, u32[]{:S(2)}) collective-permute-start(bf16[4,640,384]{2,1,0:T(8,128)(2,1)S(1)} %all_to_all.10.near_ref), channel_id=1, source_target_pairs={{0,1},{1,0},{2,3},{3,2},{4,5},{5,4},{6,7},{7,6},{8,9},{9,8},{10,11... | collective-permute-start | bytes 5898248 | tf_op jit(solution)/shard_map/ppermute | solution.py:170
  79.5 0.1 pad_add_fusion.pos_ref
  79.6 3.6 %collective-permute-done.1.far_ref = bf16[4,640,384]{2,1,0:T(8,128)(2,1)} collective-permute-done((bf16[4,640,384]{2,1,0:T(8,128)(2,1)S(1)}, bf16[4,640,384]{2,1,0:T(8,128)(2,1)}, u32[]{:S(2)}, u32[]{:S(2)}) %collective-permute-start.1) | collective-permute-done | bytes 1966112 | tf_op jit(solution)/shard_map/ppermute | solution.py:170
  83.2 0.0 all-gather.3.cloned.1.call-done
  83.2 4.7 %forward.1 = (f32[192,768]{1,0:T(8,128)S(1)}, bf16[192,768]{1,0:T(8,128)(2,1)S(1)}) custom-call(s32[2]{0:T(128)S(1)} %pad_add_fusion.pos_ref, bf16[4,640,384]{2,1,0:T(8,128)(2,1)S(1)} %all_to_all.10.near_ref, bf16[4,640,384]{2,1,0:T(8,128)(2,1)} %collective-permute-done.1.far_ref, bf16[8,320,768]{2,1,0:T(8,128)(2,1)} %bitcast.13), custom_call_target="tpu_custom_call" | custom-call | flops 1509949440 | bytes 8749064 | tf_op jit(solution)/shard_map/forward/pallas_call | solution.py:141
  88.0 7.5 %collective-permute-start.2 = (bf16[192,768]{1,0:T(8,128)(2,1)S(1)}, bf16[192,768]{1,0:T(8,128)(2,1)S(1)}, u32[]{:S(2)}, u32[]{:S(2)}) collective-permute-start(bf16[192,768]{1,0:T(8,128)(2,1)S(1)} %get-tuple-element.7), channel_id=1, source_target_pairs={{0,256},{32,288},{64,320},{96,352},{128,384},{160,416},{192,448},{... | collective-permute-start | bytes 884744 | tf_op jit(solution)/shard_map/ppermute | solution.py:178
  95.5 8.8 %collective-permute-done.2.got_ref = bf16[192,768]{1,0:T(8,128)(2,1)S(1)} collective-permute-done((bf16[192,768]{1,0:T(8,128)(2,1)S(1)}, bf16[192,768]{1,0:T(8,128)(2,1)S(1)}, u32[]{:S(2)}, u32[]{:S(2)}) %collective-permute-start.2) | collective-permute-done | bytes 294944 | tf_op jit(solution)/shard_map/ppermute | solution.py:178
  104.3 0.1 middle.1.own_ref
  104.5 7.0 %collective-permute-start.3 = (bf16[192,768]{1,0:T(8,128)(2,1)S(1)}, bf16[192,768]{1,0:T(8,128)(2,1)S(1)}, u32[]{:S(2)}, u32[]{:S(2)}) collective-permute-start(bf16[192,768]{1,0:T(8,128)(2,1)S(1)} %middle.1.own_ref), channel_id=1, source_target_pairs={{0,256},{32,288},{64,320},{96,352},{128,384},{160,416},{192,448},{... | collective-permute-start | bytes 884744 | tf_op jit(solution)/shard_map/ppermute | solution.py:180
  111.5 4.4 %collective-permute-done.3.got_ref = bf16[192,768]{1,0:T(8,128)(2,1)S(1)} collective-permute-done((bf16[192,768]{1,0:T(8,128)(2,1)S(1)}, bf16[192,768]{1,0:T(8,128)(2,1)S(1)}, u32[]{:S(2)}, u32[]{:S(2)}) %collective-permute-start.3) | collective-permute-done | bytes 294944 | tf_op jit(solution)/shard_map/ppermute | solution.py:180
  115.9 5.1 %input.1 = (bf16[2,128,2560]{2,1,0:T(8,128)(2,1)S(1)}, bf16[2,128,2560]{2,1,0:T(8,128)(2,1)}) custom-call(s32[2]{0:T(128)S(1)} %pad_add_fusion.pos_ref, bf16[192,768]{1,0:T(8,128)(2,1)S(1)} %middle.1.own_ref, bf16[192,768]{1,0:T(8,128)(2,1)S(1)} %collective-permute-done.3.got_ref, bf16[8,320,768]{2,1,0:T(8,128)(2,1)} %bitcast.14), custom_call_target="tpu_custom_call" | custom-call | flops 1006632960 | bytes 7143432 | tf_op jit(solution)/shard_map/input/pallas_call | solution.py:141
  121.0 11.5 %collective-permute-start.4 = (bf16[2,128,2560]{2,1,0:T(8,128)(2,1)}, bf16[2,128,2560]{2,1,0:T(8,128)(2,1)}, u32[]{:S(2)}, u32[]{:S(2)}) collective-permute-start(bf16[2,128,2560]{2,1,0:T(8,128)(2,1)} %get-tuple-element.9), channel_id=1, source_target_pairs={{0,1},{1,0},{2,3},{3,2},{4,5},{5,4},{6,7},{7,6},{8,9},{9,8},{10,11... | collective-permute-start | bytes 3932168 | tf_op jit(solution)/shard_map/ppermute | solution.py:192
  132.5 3.9 %down.1 = bf16[8,320,256]{2,1,0:T(8,128)(2,1)} custom-call(s32[2]{0:T(128)S(1)} %pad_add_fusion.pos_ref, bf16[4,640,384]{2,1,0:T(8,128)(2,1)S(1)} %all_to_all.10.near_ref, bf16[4,640,384]{2,1,0:T(8,128)(2,1)} %collective-permute-done.1.far_ref, bf16[192,768]{1,0:T(8,128)(2,1)S(1)} %middle.1.own_ref, bf16[192,768]{1,0:T(8,128)(2,1)S(1)} %collective-permute-done.3.got_ref), custom_call_target="tpu_custom_call" | custom-call | flops 503316480 | bytes 5832712 | tf_op jit(solution)/shard_map/down/pallas_call | solution.py:141
  136.4 0.0 reduce-scatter.2.cloned.1.call-update
  136.4 0.0 collective-permute-done.4
  136.5 2.7 %add_convert_fusion = bf16[2,128,2560]{2,1,0:T(8,128)(2,1)} fusion(bf16[2,128,2560]{2,1,0:T(8,128)(2,1)} %collective-permute-done.4, bf16[2,128,2560]{2,1,0:T(8,128)(2,1)S(1)} %get-tuple-element.8), kind=kLoop, calls=%fused_computation | loop fusion | flops 2621440 | bytes 3932160 | tf_op jit(solution)/shard_map/convert_element_type | solution.py:193
  139.1 0.0 copy-start.1
  139.1 8.6 %all-to-all-start.1 = ((bf16[32,8,2560]{2,1,0:T(8,128)(2,1)}), bf16[32,8,2560]{2,1,0:T(8,128)(2,1)S(1)}, u32[]{:S(2)}, u32[]{:S(2)}) async-start(bf16[32,8,2560]{2,1,0:T(8,128)(2,1)} %bitcast.15), calls=%async_computation.1 | async-start | bytes 2621440 | tf_op jit(solution)/shard_map/all_to_all | solution.py:194
  147.7 26.2 %reduce-scatter.2.cloned.1.call-done = bf16[320,256]{1,0:T(8,128)(2,1)} async-done(((bf16[2560,256]{1,0:T(8,128)(2,1)}), bf16[320,256]{1,0:T(8,128)(2,1)}) %reduce-scatter.2.cloned.1.call-update) | async-done | bytes 163856 | tf_op jit(solution)/shard_map/reduce_scatter | solution.py:183
  173.9 0.0 copy-done.1
  173.9 2.0 %fusion = f32[320,256]{1,0:T(8,128)} fusion(s32[320,256]{1,0:T(8,128)S(1)} %copy-done.1, bf16[320,256]{1,0:T(8,128)(2,1)} %reduce-scatter.2.cloned.1.call-done), kind=kLoop, calls=%fused_computation.3 | loop fusion | flops 2375680 | bytes 819200 | tf_op jit(solution)/shard_map/mul | solution.py:199
  175.9 5.4 %all-to-all-done.1 = bf16[32,8,2560]{2,1,0:T(8,128)(2,1)S(1)} async-done(((bf16[32,8,2560]{2,1,0:T(8,128)(2,1)}), bf16[32,8,2560]{2,1,0:T(8,128)(2,1)S(1)}, u32[]{:S(2)}, u32[]{:S(2)}) %all-to-all-start.1) | async-done | bytes 1310752 | tf_op jit(solution)/shard_map/all_to_all | solution.py:194
  181.3 0.2 bitcast_reduce_fusion
  181.5 0.7 pad_maximum_fusion.1
  (1 shorter events, 0.0 us)
Async XLA Ops:
  7.2 76.1 %all-gather.3.cloned.1.call-start = ((), (), s32[]{:S(2)}) async-start(), calls=%async_computation.4 | async-start | bytes 4423680 | tf_op jit(solution)/shard_map/all_gather | solution.py:162
  7.2 1.0 copy-start
  8.2 1.0 copy-start.2
  9.2 1.0 copy-start.3
  10.1 1.8 copy-start.4
  10.1 1.8 copy-start.5
  11.8 162.1 %reduce-scatter.2.cloned.1.call-start = ((), (), s32[]{:S(2)}) async-start(), calls=%async_computation.3 | async-start | bytes 1474560 | tf_op jit(solution)/shard_map/reduce_scatter | solution.py:183
  12.0 0.7 collective-permute-start
  76.3 6.9 %collective-permute-start.1 = (bf16[4,640,384]{2,1,0:T(8,128)(2,1)S(1)}, bf16[4,640,384]{2,1,0:T(8,128)(2,1)}, u32[]{:S(2)}, u32[]{:S(2)}) collective-permute-start(bf16[4,640,384]{2,1,0:T(8,128)(2,1)S(1)} %all_to_all.10.near_ref), channel_id=1, source_target_pairs={{0,1},{1,0},{2,3},{3,2},{4,5},{5,4},{6,7},{7,6},{8,9},{9,8},{10,11... | collective-permute-start | bytes 5898248 | tf_op jit(solution)/shard_map/ppermute | solution.py:170
  88.0 16.3 %collective-permute-start.2 = (bf16[192,768]{1,0:T(8,128)(2,1)S(1)}, bf16[192,768]{1,0:T(8,128)(2,1)S(1)}, u32[]{:S(2)}, u32[]{:S(2)}) collective-permute-start(bf16[192,768]{1,0:T(8,128)(2,1)S(1)} %get-tuple-element.7), channel_id=1, source_target_pairs={{0,256},{32,288},{64,320},{96,352},{128,384},{160,416},{192,448},{... | collective-permute-start | bytes 884744 | tf_op jit(solution)/shard_map/ppermute | solution.py:178
  104.5 11.4 %collective-permute-start.3 = (bf16[192,768]{1,0:T(8,128)(2,1)S(1)}, bf16[192,768]{1,0:T(8,128)(2,1)S(1)}, u32[]{:S(2)}, u32[]{:S(2)}) collective-permute-start(bf16[192,768]{1,0:T(8,128)(2,1)S(1)} %middle.1.own_ref), channel_id=1, source_target_pairs={{0,256},{32,288},{64,320},{96,352},{128,384},{160,416},{192,448},{... | collective-permute-start | bytes 884744 | tf_op jit(solution)/shard_map/ppermute | solution.py:180
  121.0 15.4 %collective-permute-start.4 = (bf16[2,128,2560]{2,1,0:T(8,128)(2,1)}, bf16[2,128,2560]{2,1,0:T(8,128)(2,1)}, u32[]{:S(2)}, u32[]{:S(2)}) collective-permute-start(bf16[2,128,2560]{2,1,0:T(8,128)(2,1)} %get-tuple-element.9), channel_id=1, source_target_pairs={{0,1},{1,0},{2,3},{3,2},{4,5},{5,4},{6,7},{7,6},{8,9},{9,8},{10,11... | collective-permute-start | bytes 3932168 | tf_op jit(solution)/shard_map/ppermute | solution.py:192
  139.1 34.8 %copy-start.1 = (s32[320,256]{1,0:T(8,128)S(1)}, s32[320,256]{1,0:T(8,128)}, u32[]{:S(2)}) copy-start(s32[320,256]{1,0:T(8,128)} %down_ref.1) | copy-start | bytes 983044
  139.1 42.2 %all-to-all-start.1 = ((bf16[32,8,2560]{2,1,0:T(8,128)(2,1)}), bf16[32,8,2560]{2,1,0:T(8,128)(2,1)S(1)}, u32[]{:S(2)}, u32[]{:S(2)}) async-start(bf16[32,8,2560]{2,1,0:T(8,128)(2,1)} %bitcast.15), calls=%async_computation.1 | async-start | bytes 2621440 | tf_op jit(solution)/shard_map/all_to_all | solution.py:194
Sparse Core Ops, SparseCore 0:
  12.0 60.1 all-gather.2
  136.6 37.3 reduce-scatter.1

commit v2 on v1

v2 whole, which is shorter than its diff:
```python
import math

import jax
import jax.numpy as jnp
from jax import lax
from jax.experimental import pallas as pl
from jax.experimental.pallas import tpu as pltpu
from jax.sharding import PartitionSpec as P

D = 5120
FF_W = 8192
N_Z, N_Y, N_X, N_ZL = 2, 8, 4, 4
N_T = N_X * N_ZL * 2
TOK = 192
FEAT = 160
HALF_FEAT = 80
ROWS = 320
COLS = 256
HALF = D // 2

coef_one = 0.6931472
coef_two = 0.2402265
coef_three = 0.0555041

NN = (((1,), (0,)), ((), ()))
NT = (((1,), (1,)), ((), ()))


def _swap_pairs():
    pairs = []
    for z in range(N_Z):
        for y in range(N_Y):
            for t in range(N_T):
                x1, rest = t // 16, t % 16
                pairs.append(((z * N_Y + y) * N_T + t, (x1 * N_Y + y) * N_T + z * 16 + rest))
    return pairs


SWAP = _swap_pairs()
Z_SWAP = [(d, (d + N_Y) % (N_Z * N_Y)) for d in range(N_Z * N_Y)]
CORE_SWAP = [(t, t ^ 1) for t in range(N_T)]
ZL_GROUPS = [[x * 8 + zl * 2 + c for zl in range(N_ZL)] for x in range(N_X) for c in range(2)]
X_GROUPS = [[x * 8 + i for x in range(N_X)] for i in range(8)]
Y_GROUPS = [[z * N_Y + y for y in range(N_Y)] for z in range(N_Z)]
Z_GROUPS = [
    [(z * N_Y + y) * N_T + x * 8 + zl * 2 + c for z in range(N_Z) for zl in range(N_ZL)]
    for y in range(N_Y)
    for x in range(N_X)
    for c in range(2)
]


def decode(packed, fan):
    frac = ((packed >> 1) & 7).astype(jnp.float32) * 0.125
    power = jnp.where((packed & 16) != 0, 0.5, 1.0)
    power = power * jnp.where((packed & 32) != 0, 0.25, 1.0)
    power = power * jnp.where((packed & 64) != 0, 0.0625, 1.0)
    poly = 1.0 - frac * (coef_one - frac * (coef_two - coef_three * frac))
    value = power * poly * (3.0 / math.sqrt(fan))
    return jnp.where((packed & 1) != 0, -value, value)


def decode_kernel(gate_ref, up_ref, down_ref, out_ref, down_w_ref, codes, sems):
    copies = [
        pltpu.make_async_copy(ref, codes.at[i], sems.at[i]) for i, ref in enumerate((gate_ref, up_ref, down_ref))
    ]
    for copy in copies:
        copy.start()
    for i, fan in enumerate((D, D, FF_W)):
        copies[i].wait()
        value = decode(codes[i], fan)
        out_ref[:, :, i * COLS : (i + 1) * COLS] = value.astype(jnp.bfloat16).reshape(2, FEAT, COLS)
    down_w_ref[...] = value


def forward(acts_ref, which, w_ref):
    sums = [[None, None], [None, None]]
    for x0 in range(2):
        for kind, cols in ((0, slice(0, 2 * COLS)), (1, slice(2 * COLS, 3 * COLS))):
            rows = slice(kind * HALF_FEAT, (kind + 1) * HALF_FEAT)
            acts = []
            for h in range(2):
                part = jnp.concatenate([acts_ref[2 * h + x0, zl, rows] for zl in range(N_ZL)], axis=0)
                acts.append(part.T)
            for half in range(2):
                rows = slice(half * HALF_FEAT, (half + 1) * HALF_FEAT)
                w = [w_ref[x0 * N_ZL + zl, which, rows, cols] for zl in range(N_ZL)]
                w = jnp.concatenate(w, axis=0)
                for h in range(2):
                    part = acts[h][half * TOK : (half + 1) * TOK]
                    part = lax.dot_general(part, w, NN, preferred_element_type=jnp.float32)
                    sums[h][kind] = part if sums[h][kind] is None else sums[h][kind] + part
    return sums


def near_kernel(pos_ref, acts_ref, w_ref, out_ref):
    sums = forward(acts_ref, pos_ref[1], w_ref)
    for h in range(2):
        out_ref[h, :, : 2 * COLS] = sums[h][0]
        out_ref[h, :, 2 * COLS :] = sums[h][1]


def far_kernel(pos_ref, acts_ref, w_ref, near_ref, own_ref, gate_up_ref, hidden_grad_ref):
    sums = forward(acts_ref, 1 - pos_ref[1], w_ref)
    for h in range(2):
        gate_up = sums[h][0] + near_ref[h, :, : 2 * COLS]
        hidden_grad = sums[h][1] + near_ref[h, :, 2 * COLS :]
        own_ref[h, :, : 2 * COLS] = gate_up
        own_ref[h, :, 2 * COLS :] = hidden_grad
        gate_up_ref[h] = gate_up.astype(jnp.bfloat16)
        hidden_grad_ref[h] = hidden_grad.astype(jnp.bfloat16)


def copy_kernel(w_ref, out_ref):
    out_ref[...] = w_ref[:, :, :, : 2 * COLS]


def down_kernel(pos_ref, near_ref, far_ref, own_ref, got_ref, out_ref):
    core = pos_ref[1]
    blank = jnp.zeros((TOK, COLS), jnp.bfloat16)
    rows = []
    for h in range(2):
        total = own_ref[h, :, : 2 * COLS] + got_ref[h].astype(jnp.float32)
        gate, up = total[:, :COLS], total[:, COLS:]
        hidden = (gate * jax.nn.sigmoid(gate) * up).astype(jnp.bfloat16)
        rows += [jnp.concatenate([hidden, blank], axis=1), jnp.concatenate([blank, hidden], axis=1)]
    hidden = jnp.concatenate(rows, axis=0)
    for x0 in range(2):
        for ref, which in ((near_ref, core), (far_ref, 1 - core)):
            grads = [
                jnp.concatenate([ref[2 * h + x0, zl, HALF_FEAT:] for zl in range(N_ZL)], axis=0) for h in range(2)
            ]
            acts = jnp.concatenate(grads, axis=1)
            part = lax.dot_general(acts, hidden, NN, preferred_element_type=jnp.float32).astype(jnp.bfloat16)
            for zl in range(N_ZL):
                rows = part[zl * HALF_FEAT : (zl + 1) * HALF_FEAT]
                out_ref[x0 * N_ZL + zl, which, :HALF_FEAT] = rows[:, :COLS]
                out_ref[x0 * N_ZL + zl, which, HALF_FEAT:] = rows[:, COLS:]


def input_part(pos_ref, own_ref, gate_up_ref, hidden_grad_ref, w_ref, out_ref, side):
    rows = N_X * 48
    row = lax.broadcasted_iota(jnp.int32, (rows, 2 * TOK), 0)
    col = lax.broadcasted_iota(jnp.int32, (rows, 2 * TOK), 1)
    x = (row * 1366) >> 16
    left = row - 48 * x
    h = jnp.where(left >= 24, 1, 0)
    left = left - 24 * h
    zl = (left * 10923) >> 16
    wanted = h * TOK + x * 48 + zl * 12 + side * 6 + left - 6 * zl
    pick = jnp.where(wanted == col, 1.0, 0.0).astype(jnp.bfloat16)
    grads = []
    for h in range(2):
        total = own_ref[h, :, : 2 * COLS] + gate_up_ref[h].astype(jnp.float32)
        gate, up = total[:, :COLS], total[:, COLS:]
        hidden_grad = own_ref[h, :, 2 * COLS :] + hidden_grad_ref[h].astype(jnp.float32)
        sig = jax.nn.sigmoid(gate)
        gate_grad = (hidden_grad * up * sig * (1.0 + gate * (1.0 - sig))).astype(jnp.bfloat16)
        up_grad = (hidden_grad * gate * sig).astype(jnp.bfloat16)
        grads.append(jnp.concatenate([gate_grad, up_grad], axis=1))
    grads = jnp.concatenate(grads, axis=0)
    grads = lax.dot_general(pick, grads, NN, preferred_element_type=jnp.float32).astype(jnp.bfloat16)
    for q in range(4):
        pair = w_ref[2 * q : 2 * q + 2].reshape(2 * ROWS, 2 * COLS)
        part = lax.dot_general(grads, pair, NT, preferred_element_type=jnp.float32)
        at = slice(q * 2 * ROWS, (q + 1) * 2 * ROWS)
        out_ref[:, :, at] = part.astype(jnp.bfloat16).reshape(N_X, 48, 2 * ROWS)


def input_send_kernel(pos_ref, *refs):
    input_part(pos_ref, *refs, 1 - pos_ref[1])


def input_keep_kernel(pos_ref, *refs):
    input_part(pos_ref, *refs, pos_ref[1])


def add_kernel(a_ref, b_ref, out_ref):
    out_ref[...] = (a_ref[...].astype(jnp.float32) + b_ref[...].astype(jnp.float32)).astype(jnp.bfloat16)


def x_sum_kernel(parts_ref, out_ref):
    total = parts_ref[0].astype(jnp.float32)
    for i in range(1, N_X):
        total += parts_ref[i].astype(jnp.float32)
    row = lax.broadcasted_iota(jnp.int32, (64, 48), 0)
    col = lax.broadcasted_iota(jnp.int32, (64, 48), 1)
    pick = jnp.where(((row >> 3) * 6 + (row & 7) == col) & ((row & 7) < 6), 1.0, 0.0).astype(jnp.bfloat16)
    total = lax.dot_general(pick, total.astype(jnp.bfloat16), NN, preferred_element_type=jnp.float32)
    out_ref[...] = total.astype(jnp.bfloat16)


def input_sum_kernel(parts_ref, out_ref):
    for z in range(2):
        total = parts_ref[4 * z].astype(jnp.float32)
        for i in range(1, 4):
            total += parts_ref[4 * z + i].astype(jnp.float32)
        out_ref[:, z * HALF : (z + 1) * HALF] = total[:6].astype(jnp.bfloat16)


def down_log_kernel(grad_ref, down_w_ref, out_ref):
    out_ref[...] = grad_ref[...].astype(jnp.float32) * down_w_ref[...]


VMEM = pl.BlockSpec(memory_space=pltpu.VMEM)
SMEM = pl.BlockSpec(memory_space=pltpu.SMEM)
HBM = pl.BlockSpec(memory_space=pltpu.HBM)


def call(kernel, out_shapes, *args, name, flops=0, scratch=(), hbm=(), limit=16):
    specs = [SMEM if a.dtype == jnp.int32 and a.ndim == 1 else HBM if i in hbm else VMEM for i, a in enumerate(args)]
    moved = 0
    if flops:
        moved = sum(a.size * a.dtype.itemsize for a in args)
        moved += sum(o.size * o.dtype.itemsize for o in jax.tree.leaves(out_shapes))
    return pl.pallas_call(
        kernel,
        out_shape=out_shapes,
        in_specs=specs,
        out_specs=jax.tree.map(lambda _: VMEM, out_shapes),
        scratch_shapes=scratch,
        compiler_params=pltpu.CompilerParams(vmem_limit_bytes=limit * 2**20),
        cost_estimate=pl.CostEstimate(flops=flops, bytes_accessed=moved, transcendentals=0),
        name=name,
    )(*args)


def shaped(shape, dtype=jnp.bfloat16):
    return jax.ShapeDtypeStruct(shape, dtype)


def on_device(inputs, grad_out, gate_codes, up_codes, down_codes):
    dp, tensor = lax.axis_index("dp"), lax.axis_index("tensor")
    pos = jnp.stack([dp // N_Y, tensor % 2, dp % N_Y, tensor // 2 % N_ZL]).astype(jnp.int32)
    wide, bf16, f32 = 3 * COLS, jnp.bfloat16, jnp.float32

    w, down_w = call(
        decode_kernel, (shaped((2, FEAT, wide)), shaped((ROWS, COLS), f32)), gate_codes, up_codes, down_codes,
        name="decode", flops=ROWS * COLS * 32,
        scratch=[pltpu.VMEM((3, ROWS, COLS), jnp.int32), pltpu.SemaphoreType.DMA((3,))], hbm=(0, 1, 2), limit=60,
    )
    w = lax.all_gather(w, "dp", axis=0, axis_index_groups=Y_GROUPS)

    def folded(acts):
        acts = acts.T
        return jnp.concatenate([acts[:HALF_FEAT], acts[HALF_FEAT:]], axis=1)

    acts = jnp.concatenate([folded(inputs), folded(grad_out)], axis=0)
    acts = lax.ppermute(acts, ("dp", "tensor"), SWAP)
    acts = jnp.broadcast_to(acts[None], (N_ZL, FEAT, 2 * TOK))
    acts = lax.all_to_all(acts, "tensor", 0, 0, axis_index_groups=ZL_GROUPS, tiled=True)

    acts = jnp.broadcast_to(acts[None], (N_X, N_ZL, FEAT, 2 * TOK))
    near = lax.all_to_all(acts, "tensor", 0, 0, axis_index_groups=X_GROUPS, tiled=True)
    near, w = lax.optimization_barrier((near, w))
    far = lax.ppermute(near, "tensor", CORE_SWAP)

    flops = HALF * 3 * COLS * 2 * TOK
    sums = call(near_kernel, shaped((2, TOK, wide), f32), pos, near, w, name="forward_near", flops=flops)
    own, gate_up, hidden_grad = call(
        far_kernel,
        (shaped((2, TOK, wide), f32), shaped((2, TOK, 2 * COLS)), shaped((2, TOK, COLS))),
        pos, far, w, sums, name="forward_far",
    )
    w_own, _ = lax.optimization_barrier((w, own))
    gate_up = lax.ppermute(gate_up, "dp", Z_SWAP)
    hidden_grad = lax.ppermute(hidden_grad, "dp", Z_SWAP)
    w_gate_up = call(copy_kernel, shaped((N_Y, 2, FEAT, 2 * COLS)), w_own, name="copy", flops=flops)

    down = call(down_kernel, shaped((N_Y, 2, FEAT, COLS)), pos, near, far, own, gate_up, name="down")
    down, hidden_grad, w_gate_up = lax.optimization_barrier((down, hidden_grad, w_gate_up))
    down_grad = lax.psum_scatter(
        down.reshape(N_Y * ROWS, COLS), "dp", scatter_dimension=0, axis_index_groups=Y_GROUPS, tiled=True
    )

    out = shaped((N_X, 48, HALF))
    grads = (own, gate_up, hidden_grad)
    send = call(input_send_kernel, out, pos, *grads, w_gate_up, name="input_send", flops=flops)
    other = lax.ppermute(send, "tensor", CORE_SWAP)
    keep = call(input_keep_kernel, out, pos, *grads, w_gate_up, name="input_keep", flops=flops)
    parts = call(add_kernel, out, keep, other, name="add")
    parts = lax.all_to_all(parts, "tensor", 0, 0, axis_index_groups=X_GROUPS, tiled=True)
    parts = call(x_sum_kernel, shaped((64, HALF)), parts, name="x_sum").reshape(N_Y, 8, HALF)
    parts = lax.all_to_all(parts, ("dp", "tensor"), 0, 0, axis_index_groups=Z_GROUPS, tiled=True)
    input_grad = call(input_sum_kernel, shaped((6, D)), parts, name="input_sum")
    down_log_grad = call(
        down_log_kernel, shaped((ROWS, COLS), f32), down_grad, down_w, name="down_log", flops=flops
    )
    return input_grad, down_log_grad


def solution(mesh):
    in_specs = (P("dp", "tensor"),) * 5
    out_specs = (P(("dp", "tensor"), None), P("dp", "tensor"))
    return jax.shard_map(on_device, mesh=mesh, in_specs=in_specs, out_specs=out_specs, check_vma=False)
```

time: 190 us -> 171 us (0.900)
  waiting for transfers between devices: 48.5 us -> 14.3 us
  blocking collectives: 63.4 us -> 96 us
  starting transfers between devices: 38.5 us -> 21 us
  other arithmetic: 5.64 us -> 0.17 us
  local copies, waits for them, and re-layouts: 3.15 us -> 6.61 us
    all_to_all x1 -> x4, blocking collectives: 37.7 us -> 96 us  [the longest x1 38.1 us: on_device(): lax.all_to_all(acts, 'tensor', 0, 0, axis_index_groups=X_GROUPS, tiled=True)]
    reduce_scatter x1, waiting for transfers between devices: 26.2 us -> 0.01 us  [on_device(): lax.psum_scatter(down.reshape(N_Y * ROWS, COLS), 'dp', scatter_dimension=...]
    all_gather x1 -> x0, blocking collectives: 25.6 us -> none  [on_device(): lax.all_gather(acts, 'tensor', axis=0, axis_index_groups=ZC_GROUPS, tiled...]
    all_to_all x1 -> x0, starting transfers between devices: 8.56 us -> none  [on_device(): lax.all_to_all(summed.reshape(32, 8, HALF), ('dp', 'tensor'), 0, 0, axis_...]
    all_to_all x1 -> x0, waiting for transfers between devices: 5.42 us -> none  [on_device(): lax.all_to_all(summed.reshape(32, 8, HALF), ('dp', 'tensor'), 0, 0, axis_...]
    ppermute x1, starting transfers between devices: 11.5 us -> 6.34 us  [on_device(): other = lax.ppermute(send, 'tensor', CORE_SWAP)]
    ppermute x2, starting transfers between devices: 14.5 us -> 9.49 us  [the longest x1 7.57 us: on_device(): gate_up = lax.ppermute(gate_up, 'dp', Z_SWAP)]
    ppermute x1, waiting for transfers between devices: 3.62 us -> 0.01 us  [on_device(): far = lax.ppermute(near, 'tensor', CORE_SWAP)]
  transfers between devices with their start and end apart: 8 -> 7, of which waited for: 5 -> 3; matrix products, arithmetic and copies ran while one was open for 3% -> 1% of each run, Pallas kernels for 2% -> 6%
where the time goes in v2:
time: 171 us; the launch traced here: 169 us
  blocking collectives  96 us (56%)
  starting transfers between devices  21 us (12%)
  Pallas kernels  16.4 us (10%)
  waiting for transfers between devices  14.3 us (8%)
  between operations  14.3 us (8%)
  local copies, waits for them, and re-layouts  6.61 us (4%)
    all_to_all x1, blocking collectives, on_device(): lax.all_to_all(acts, 'tensor', 0, 0, axis_index_groups=X_GROUPS, tiled=True)  38.1 us
    all_to_all x1, blocking collectives, on_device(): lax.all_to_all(acts, 'tensor', 0, 0, axis_index_groups=ZL_GROUPS, tiled=T...  23.4 us
    all_to_all x1, blocking collectives, on_device(): lax.all_to_all(parts, ('dp', 'tensor'), 0, 0, axis_index_groups=Z_GROUPS,...  18.1 us
    pallas_call x11, Pallas kernels, call(): pl.pallas_call(kernel, out_shape=out_shapes, in_specs=specs, out_specs=ja...  16.4 us
    all_to_all x1, blocking collectives, on_device(): lax.all_to_all(parts, 'tensor', 0, 0, axis_index_groups=X_GROUPS, tiled=T...  16.4 us
    ppermute x1, waiting for transfers between devices, on_device(): gate_up = lax.ppermute(gate_up, 'dp', Z_SWAP)  11.4 us
    ppermute x1, starting transfers between devices, on_device(): gate_up = lax.ppermute(gate_up, 'dp', Z_SWAP)  7.57 us
    ppermute x1, starting transfers between devices, on_device(): other = lax.ppermute(send, 'tensor', CORE_SWAP)  6.34 us
  transfers between devices with their start and end apart: 7, of which 3 were waited for; matrix products, arithmetic and copies ran while one was open for 1% of the time, Pallas kernels for 6%

profile of v2, /device:TPU:1, one launch (start us, length us, event | category | flops | bytes accessed | tf_op | source)
XLA Modules:
  0.0 168.8 jit_solution(7247208737053287823)
XLA Ops:
  7.2 0.0 all-gather.3.cloned.1.call-start
  7.2 2.8 %decode.1 = (bf16[2,160,768]{2,1,0:T(8,128)(2,1)}, f32[320,256]{1,0:T(8,128)}) custom-call(s32[320,256]{1,0:T(8,128)} %gate_ref.1, s32[320,256]{1,0:T(8,128)} %up_ref.1, s32[320,256]{1,0:T(8,128)} %down_ref.1), custom_call_target="tpu_custom_call" | custom-call | flops 2621440 | bytes 1802240 | tf_op jit(solution)/shard_map/decode/pallas_call | solution.py:216
  10.0 0.0 all-gather.3.cloned.1.call-update
  10.0 0.0 reduce-scatter.2.cloned.1.call-start
  10.1 0.9 fusion
  10.9 0.1 maximum_maximum_fusion
  11.0 0.7 collective-permute-start
  11.7 0.0 collective-permute-done
  11.8 23.4 %all_to_all.20 = bf16[4,160,384]{2,1,0:T(8,128)(2,1)S(1)} all-to-all(bf16[4,160,384]{2,1,0:T(8,128)(2,1)S(1)} %broadcast_in_dim.4), channel_id=1, replica_groups={{0,2,4,6},{1,3,5,7},{8,10,12,14},{9,11,13,15},{16,18,20,22},{17,19,21,2..., dimensions={0} | all-to-all | bytes 983040 | tf_op jit(solution)/shard_map/all_to_all | solution.py:251
  35.2 0.2 broadcast_in_dim.5
  35.4 38.1 %all_to_all.21.acts_ref.near_ref = bf16[4,4,160,384]{3,2,1,0:T(8,128)(2,1)S(1)} all-to-all(bf16[4,4,160,384]{3,2,1,0:T(8,128)(2,1)S(1)} %broadcast_in_dim.5), channel_id=1, replica_groups={{0,8,16,24},{1,9,17,25},{2,10,18,26},{3,11,19,27},{4,12,20,28},{5,13,21..., dimensions={0} | all-to-all | bytes 3932160 | tf_op jit(solution)/shard_map/all_to_all | solution.py:254
  73.5 0.0 copy-start.2
  73.5 4.4 %collective-permute-start.1 = (bf16[4,4,160,384]{3,2,1,0:T(8,128)(2,1)S(1)}, bf16[4,4,160,384]{3,2,1,0:T(8,128)(2,1)}, u32[]{:S(2)}, u32[]{:S(2)}) collective-permute-start(bf16[4,4,160,384]{3,2,1,0:T(8,128)(2,1)S(1)} %all_to_all.21.acts_ref.near_ref), channel_id=1, source_target_pairs={{0,1},{1,0},{2,3},{3,2},{4,5},{5,4},{6,7},{7,6},{8,9},{9,8},{10,11... | collective-permute-start | bytes 5898248 | tf_op jit(solution)/shard_map/ppermute | solution.py:256
  78.0 0.1 pad_add_fusion.pos_ref
  78.0 2.1 %copy-done = bf16[16,160,768]{2,1,0:T(8,128)(2,1)S(1)} copy-done((bf16[16,160,768]{2,1,0:T(8,128)(2,1)S(1)}, bf16[16,160,768]{2,1,0:T(8,128)(2,1)}, u32[]{:S(2)}) %copy-start) | copy-done | bytes 3932184
  80.2 2.0 %forward_near.1.near_ref = f32[2,192,768]{2,1,0:T(8,128)S(1)} custom-call(s32[4]{0:T(128)S(1)} %pad_add_fusion.pos_ref, bf16[4,4,160,384]{3,2,1,0:T(8,128)(2,1)S(1)} %all_to_all.21.acts_ref.near_ref, bf16[8,2,160,768]{3,2,1,0:T(8,128)(2,1)S(1)} %bitcast.9), custom_call_target="tpu_custom_call" | custom-call | flops 754974720 | bytes 7077904 | tf_op jit(solution)/shard_map/forward_near/pallas_call | solution.py:216
  82.1 0.0 copy-done.2
  82.1 0.0 collective-permute-done.1.acts_ref.far_ref
  82.2 0.1 copy-done.1
  82.3 3.0 %forward_far.1 = (f32[2,192,768]{2,1,0:T(8,128)S(1)}, bf16[2,192,512]{2,1,0:T(8,128)(2,1)S(1)}, bf16[2,192,256]{2,1,0:T(8,128)(2,1)S(1)}) custom-call(s32[4]{0:T(128)S(1)} %pad_add_fusion.pos_ref, bf16[4,4,160,384]{3,2,1,0:T(8,128)(2,1)} %collective-permute-done.1.acts_ref.far_ref, bf16[8,2,160,768]{3,2,1,0:T(8,128)(2,1)S(1)} %bitcast.10, ...), custom_call_target="tpu_custom_call" | custom-call | tf_op jit(solution)/shard_map/forward_far/pallas_call | solution.py:216
  85.3 0.0 copy-start.4
  85.3 7.6 %collective-permute-start.2 = (bf16[2,192,512]{2,1,0:T(8,128)(2,1)S(1)}, bf16[2,192,512]{2,1,0:T(8,128)(2,1)S(1)}, u32[]{:S(2)}, u32[]{:S(2)}) collective-permute-start(bf16[2,192,512]{2,1,0:T(8,128)(2,1)S(1)} %get-tuple-element.17), channel_id=1, source_target_pairs={{0,256},{32,288},{64,320},{96,352},{128,384},{160,416},{192,448},{... | collective-permute-start | bytes 1179656 | tf_op jit(solution)/shard_map/ppermute | solution.py:266
  92.9 1.9 %collective-permute-start.3 = (bf16[2,192,256]{2,1,0:T(8,128)(2,1)S(1)}, bf16[2,192,256]{2,1,0:T(8,128)(2,1)S(1)}, u32[]{:S(2)}, u32[]{:S(2)}) collective-permute-start(bf16[2,192,256]{2,1,0:T(8,128)(2,1)S(1)} %get-tuple-element.18), channel_id=1, source_target_pairs={{0,256},{32,288},{64,320},{96,352},{128,384},{160,416},{192,448},{... | collective-permute-start | bytes 589832 | tf_op jit(solution)/shard_map/ppermute | solution.py:267
  94.8 0.0 copy-start.3
  94.8 0.2 copy.8.refs_3_
  95.0 11.4 %collective-permute-done.2.got_ref.refs_1_ = bf16[2,192,512]{2,1,0:T(8,128)(2,1)S(1)} collective-permute-done((bf16[2,192,512]{2,1,0:T(8,128)(2,1)S(1)}, bf16[2,192,512]{2,1,0:T(8,128)(2,1)S(1)}, u32[]{:S(2)}, u32[]{:S(2)}) %collective-permute-start.2) | collective-permute-done | bytes 393248 | tf_op jit(solution)/shard_map/ppermute | solution.py:266
  106.4 0.0 copy-done.4
  106.4 0.0 copy-done.3
  106.4 2.8 %down.1 = bf16[8,2,160,256]{3,2,1,0:T(8,128)(2,1)S(1)} custom-call(s32[4]{0:T(128)S(1)} %pad_add_fusion.pos_ref, bf16[4,4,160,384]{3,2,1,0:T(8,128)(2,1)S(1)} %copy-done.3, bf16[4,4,160,384]{3,2,1,0:T(8,128)(2,1)} %collective-permute-done.1.acts_ref.far_ref, f32[2,192,768]{2,1,0:T(8,128)S(1)} %get-tuple-element.16.own_ref.refs_0_, ...), custom_call_target="tpu_custom_call" | custom-call | tf_op jit(solution)/shard_map/down/pallas_call | solution.py:216
  109.1 0.0 copy-start.6
  109.1 1.1 copy-done.6
  110.2 2.6 %collective-permute-done.3.refs_2_ = bf16[2,192,256]{2,1,0:T(8,128)(2,1)S(1)} collective-permute-done((bf16[2,192,256]{2,1,0:T(8,128)(2,1)S(1)}, bf16[2,192,256]{2,1,0:T(8,128)(2,1)S(1)}, u32[]{:S(2)}, u32[]{:S(2)}) %collective-permute-start.3) | collective-permute-done | bytes 196640 | tf_op jit(solution)/shard_map/ppermute | solution.py:267
  112.8 0.0 reduce-scatter.2.cloned.1.call-update
  112.8 0.0 copy-start.5
  112.8 1.3 copy-done.5
  114.1 1.9 %input_send.1 = bf16[4,48,2560]{2,1,0:T(8,128)(2,1)S(1)} custom-call(s32[4]{0:T(128)S(1)} %pad_add_fusion.pos_ref, f32[2,192,768]{2,1,0:T(8,128)S(1)} %copy-done.5, bf16[2,192,512]{2,1,0:T(8,128)(2,1)S(1)} %collective-permute-done.2.got_ref.refs_1_, bf16[2,192,256]{2,1,0:T(8,128)(2,1)S(1)} %collective-permute-done.3.refs_2_, ...), custom_call_target="tpu_custom_call" | custom-call | flops 754974720 | bytes 5373968 | tf_op jit(solution)/shard_map/input_send/pallas_call | solution.py:216
  116.0 6.3 %collective-permute-start.4 = (bf16[4,48,2560]{2,1,0:T(8,128)(2,1)S(1)}, bf16[4,48,2560]{2,1,0:T(8,128)(2,1)S(1)}, u32[]{:S(2)}, u32[]{:S(2)}) collective-permute-start(bf16[4,48,2560]{2,1,0:T(8,128)(2,1)S(1)} %input_send.1), channel_id=1, source_target_pairs={{0,1},{1,0},{2,3},{3,2},{4,5},{5,4},{6,7},{7,6},{8,9},{9,8},{10,11... | collective-permute-start | bytes 2949128 | tf_op jit(solution)/shard_map/ppermute | solution.py:279
  122.3 1.9 %input_keep.1.a_ref = bf16[4,48,2560]{2,1,0:T(8,128)(2,1)S(1)} custom-call(s32[4]{0:T(128)S(1)} %pad_add_fusion.pos_ref, f32[2,192,768]{2,1,0:T(8,128)S(1)} %copy-done.5, bf16[2,192,512]{2,1,0:T(8,128)(2,1)S(1)} %collective-permute-done.2.got_ref.refs_1_, bf16[2,192,256]{2,1,0:T(8,128)(2,1)S(1)} %collective-permute-done.3.refs_2_, ...), custom_call_target="tpu_custom_call" | custom-call | flops 754974720 | bytes 5373968 | tf_op jit(solution)/shard_map/input_keep/pallas_call | solution.py:216
  124.2 0.3 collective-permute-done.4.b_ref
  124.5 0.2 add.25
  124.7 0.0 copy-start.7
  124.8 16.4 %all_to_all.22.parts_ref = bf16[4,48,2560]{2,1,0:T(8,128)(2,1)S(1)} all-to-all(bf16[4,48,2560]{2,1,0:T(8,128)(2,1)S(1)} %add.25), channel_id=1, replica_groups={{0,8,16,24},{1,9,17,25},{2,10,18,26},{3,11,19,27},{4,12,20,28},{5,13,21..., dimensions={0} | all-to-all | bytes 1966080 | tf_op jit(solution)/shard_map/all_to_all | solution.py:282
  141.1 0.3 x_sum.1
  141.4 18.1 %all_to_all.23.parts_ref = bf16[8,8,2560]{2,1,0:T(8,128)(2,1)S(1)} all-to-all(bf16[8,8,2560]{2,1,0:T(8,128)(2,1)S(1)} %bitcast.13), channel_id=1, replica_groups={{0,2,4,6,256,258,260,262},{1,3,5,7,257,259,261,263},{8,10,12,14,264,266..., dimensions={0} | all-to-all | bytes 655360 | tf_op jit(solution)/shard_map/all_to_all | solution.py:284
  159.6 0.7 input_sum.1
  160.2 0.0 copy-done.7
  160.3 0.9 copy-done.8
  161.2 0.8 down_log.1
  (6 shorter events, 0.1 us)
Async XLA Ops:
  7.2 66.3 %all-gather.3.cloned.1.call-start = ((), (), s32[]{:S(2)}) async-start(), calls=%async_computation.6 | async-start | bytes 4423680 | tf_op jit(solution)/shard_map/all_gather | solution.py:242
  10.0 150.2 %reduce-scatter.2.cloned.1.call-start = ((), (), s32[]{:S(2)}) async-start(), calls=%async_computation.5 | async-start | bytes 1474560 | tf_op jit(solution)/shard_map/reduce_scatter | solution.py:272
  11.0 0.7 collective-permute-start
  73.5 8.7 %copy-start.2 = (bf16[4,4,160,384]{3,2,1,0:T(8,128)(2,1)}, bf16[4,4,160,384]{3,2,1,0:T(8,128)(2,1)S(1)}, u32[]{:S(2)}) copy-start(bf16[4,4,160,384]{3,2,1,0:T(8,128)(2,1)S(1)} %all_to_all.21.acts_ref.near_ref) | copy-start | bytes 5898244
  73.5 8.7 %collective-permute-start.1 = (bf16[4,4,160,384]{3,2,1,0:T(8,128)(2,1)S(1)}, bf16[4,4,160,384]{3,2,1,0:T(8,128)(2,1)}, u32[]{:S(2)}, u32[]{:S(2)}) collective-permute-start(bf16[4,4,160,384]{3,2,1,0:T(8,128)(2,1)S(1)} %all_to_all.21.acts_ref.near_ref), channel_id=1, source_target_pairs={{0,1},{1,0},{2,3},{3,2},{4,5},{5,4},{6,7},{7,6},{8,9},{9,8},{10,11... | collective-permute-start | bytes 5898248 | tf_op jit(solution)/shard_map/ppermute | solution.py:256
  78.0 2.1 %copy-start = (bf16[16,160,768]{2,1,0:T(8,128)(2,1)S(1)}, bf16[16,160,768]{2,1,0:T(8,128)(2,1)}, u32[]{:S(2)}) copy-start(bf16[16,160,768]{2,1,0:T(8,128)(2,1)} %all-gather.3.cloned.1.call-done) | copy-start | bytes 11796484
  80.2 2.1 %copy-start.1 = (bf16[16,160,768]{2,1,0:T(8,128)(2,1)S(1)}, bf16[16,160,768]{2,1,0:T(8,128)(2,1)}, u32[]{:S(2)}) copy-start(bf16[16,160,768]{2,1,0:T(8,128)(2,1)} %all-gather.3.cloned.1.call-done) | copy-start | bytes 11796484
  85.3 21.1 %copy-start.4 = (f32[2,192,768]{2,1,0:T(8,128)}, f32[2,192,768]{2,1,0:T(8,128)S(1)}, u32[]{:S(2)}) copy-start(f32[2,192,768]{2,1,0:T(8,128)S(1)} %get-tuple-element.16.own_ref.refs_0_) | copy-start | bytes 3538948
  85.3 21.1 %collective-permute-start.2 = (bf16[2,192,512]{2,1,0:T(8,128)(2,1)S(1)}, bf16[2,192,512]{2,1,0:T(8,128)(2,1)S(1)}, u32[]{:S(2)}, u32[]{:S(2)}) collective-permute-start(bf16[2,192,512]{2,1,0:T(8,128)(2,1)S(1)} %get-tuple-element.17), channel_id=1, source_target_pairs={{0,256},{32,288},{64,320},{96,352},{128,384},{160,416},{192,448},{... | collective-permute-start | bytes 1179656 | tf_op jit(solution)/shard_map/ppermute | solution.py:266
  92.9 19.9 %collective-permute-start.3 = (bf16[2,192,256]{2,1,0:T(8,128)(2,1)S(1)}, bf16[2,192,256]{2,1,0:T(8,128)(2,1)S(1)}, u32[]{:S(2)}, u32[]{:S(2)}) collective-permute-start(bf16[2,192,256]{2,1,0:T(8,128)(2,1)S(1)} %get-tuple-element.18), channel_id=1, source_target_pairs={{0,256},{32,288},{64,320},{96,352},{128,384},{160,416},{192,448},{... | collective-permute-start | bytes 589832 | tf_op jit(solution)/shard_map/ppermute | solution.py:267
  94.8 11.6 %copy-start.3 = (bf16[4,4,160,384]{3,2,1,0:T(8,128)(2,1)S(1)}, bf16[4,4,160,384]{3,2,1,0:T(8,128)(2,1)}, u32[]{:S(2)}) copy-start(bf16[4,4,160,384]{3,2,1,0:T(8,128)(2,1)} %copy-done.2) | copy-start | bytes 5898244
  109.1 1.1 copy-start.6
  112.8 1.3 copy-start.5
  116.0 8.5 %collective-permute-start.4 = (bf16[4,48,2560]{2,1,0:T(8,128)(2,1)S(1)}, bf16[4,48,2560]{2,1,0:T(8,128)(2,1)S(1)}, u32[]{:S(2)}, u32[]{:S(2)}) collective-permute-start(bf16[4,48,2560]{2,1,0:T(8,128)(2,1)S(1)} %input_send.1), channel_id=1, source_target_pairs={{0,1},{1,0},{2,3},{3,2},{4,5},{5,4},{6,7},{7,6},{8,9},{9,8},{10,11... | collective-permute-start | bytes 2949128 | tf_op jit(solution)/shard_map/ppermute | solution.py:279
  124.7 35.5 %copy-start.7 = (f32[320,256]{1,0:T(8,128)S(1)}, f32[320,256]{1,0:T(8,128)}, u32[]{:S(2)}) copy-start(f32[320,256]{1,0:T(8,128)} %get-tuple-element.23.down_w_ref) | copy-start | bytes 983044
  160.2 0.9 copy-start.8
Sparse Core Ops, SparseCore 0:
  10.2 60.1 all-gather.2
  112.9 41.8 reduce-scatter.1

commit v3 on v2

--- a/solution.py
+++ b/solution.py
@@ -17,6 +17,7 @@
 ROWS = 320
 COLS = 256
 HALF = D // 2
+QUARTER = HALF // 4
 
 coef_one = 0.6931472
 coef_two = 0.2402265
@@ -26,17 +27,17 @@
 NT = (((1,), (1,)), ((), ()))
 
 
-def _swap_pairs():
+def _turn_pairs():
     pairs = []
     for z in range(N_Z):
         for y in range(N_Y):
             for t in range(N_T):
                 x1, rest = t // 16, t % 16
-                pairs.append(((z * N_Y + y) * N_T + t, (x1 * N_Y + y) * N_T + z * 16 + rest))
+                pairs.append(((z * N_Y + y) * N_T + t, (x1 * N_Y + y) * N_T + (1 - z) * 16 + rest))
     return pairs
 
 
-SWAP = _swap_pairs()
+TURN = _turn_pairs()
 Z_SWAP = [(d, (d + N_Y) % (N_Z * N_Y)) for d in range(N_Z * N_Y)]
 CORE_SWAP = [(t, t ^ 1) for t in range(N_T)]
 ZL_GROUPS = [[x * 8 + zl * 2 + c for zl in range(N_ZL)] for x in range(N_X) for c in range(2)]
@@ -80,7 +81,7 @@
             rows = slice(kind * HALF_FEAT, (kind + 1) * HALF_FEAT)
             acts = []
             for h in range(2):
-                part = jnp.concatenate([acts_ref[2 * h + x0, zl, rows] for zl in range(N_ZL)], axis=0)
+                part = jnp.concatenate([acts_ref[2 - 2 * h + x0, zl, rows] for zl in range(N_ZL)], axis=0)
                 acts.append(part.T)
             for half in range(2):
                 rows = slice(half * HALF_FEAT, (half + 1) * HALF_FEAT)
@@ -128,7 +129,7 @@
     for x0 in range(2):
         for ref, which in ((near_ref, core), (far_ref, 1 - core)):
             grads = [
-                jnp.concatenate([ref[2 * h + x0, zl, HALF_FEAT:] for zl in range(N_ZL)], axis=0) for h in range(2)
+                jnp.concatenate([ref[2 - 2 * h + x0, zl, HALF_FEAT:] for zl in range(N_ZL)], axis=0) for h in range(2)
             ]
             acts = jnp.concatenate(grads, axis=1)
             part = lax.dot_general(acts, hidden, NN, preferred_element_type=jnp.float32).astype(jnp.bfloat16)
@@ -183,23 +184,34 @@
     total = parts_ref[0].astype(jnp.float32)
     for i in range(1, N_X):
         total += parts_ref[i].astype(jnp.float32)
-    row = lax.broadcasted_iota(jnp.int32, (64, 48), 0)
-    col = lax.broadcasted_iota(jnp.int32, (64, 48), 1)
-    pick = jnp.where(((row >> 3) * 6 + (row & 7) == col) & ((row & 7) < 6), 1.0, 0.0).astype(jnp.bfloat16)
-    total = lax.dot_general(pick, total.astype(jnp.bfloat16), NN, preferred_element_type=jnp.float32)
-    out_ref[...] = total.astype(jnp.bfloat16)
+    total = total.astype(jnp.bfloat16)
+    row = lax.broadcasted_iota(jnp.int32, (N_Y * 24, 48), 0)
+    col = lax.broadcasted_iota(jnp.int32, (N_Y * 24, 48), 1)
+    k = (row * 2731) >> 16
+    left = row - 24 * k
+    packed = None
+    for q in range(4):
+        inside = (left >= 6 * q) & (left < 6 * q + 6)
+        pick = jnp.where(inside & (k * 6 + left - 6 * q == col), 1.0, 0.0).astype(jnp.bfloat16)
+        part = total[:, q * QUARTER : (q + 1) * QUARTER]
+        part = lax.dot_general(pick, part, NN, preferred_element_type=jnp.float32)
+        packed = part if packed is None else packed + part
+    out_ref[...] = packed.astype(jnp.bfloat16)
 
 
 def input_sum_kernel(parts_ref, out_ref):
+    row = lax.broadcasted_iota(jnp.int32, (8, 24), 0)
+    col = lax.broadcasted_iota(jnp.int32, (8, 24), 1)
     for z in range(2):
         total = parts_ref[4 * z].astype(jnp.float32)
         for i in range(1, 4):
             total += parts_ref[4 * z + i].astype(jnp.float32)
-        out_ref[:, z * HALF : (z + 1) * HALF] = total[:6].astype(jnp.bfloat16)
-
-
-def down_log_kernel(grad_ref, down_w_ref, out_ref):
-    out_ref[...] = grad_ref[...].astype(jnp.float32) * down_w_ref[...]
+        total = total.astype(jnp.bfloat16)
+        for q in range(4):
+            pick = jnp.where((row + 6 * q == col) & (row < 6), 1.0, 0.0).astype(jnp.bfloat16)
+            part = lax.dot_general(pick, total, NN, preferred_element_type=jnp.float32)
+            at = z * HALF + q * QUARTER
+            out_ref[:, at : at + QUARTER] = part[:6].astype(jnp.bfloat16)
 
 
 VMEM = pl.BlockSpec(memory_space=pltpu.VMEM)
@@ -246,7 +258,7 @@
         return jnp.concatenate([acts[:HALF_FEAT], acts[HALF_FEAT:]], axis=1)
 
     acts = jnp.concatenate([folded(inputs), folded(grad_out)], axis=0)
-    acts = lax.ppermute(acts, ("dp", "tensor"), SWAP)
+    acts = lax.ppermute(acts, ("dp", "tensor"), TURN)
     acts = jnp.broadcast_to(acts[None], (N_ZL, FEAT, 2 * TOK))
     acts = lax.all_to_all(acts, "tensor", 0, 0, axis_index_groups=ZL_GROUPS, tiled=True)
 
@@ -280,12 +292,10 @@
     keep = call(input_keep_kernel, out, pos, *grads, w_gate_up, name="input_keep", flops=flops)
     parts = call(add_kernel, out, keep, other, name="add")
     parts = lax.all_to_all(parts, "tensor", 0, 0, axis_index_groups=X_GROUPS, tiled=True)
-    parts = call(x_sum_kernel, shaped((64, HALF)), parts, name="x_sum").reshape(N_Y, 8, HALF)
+    parts = call(x_sum_kernel, shaped((N_Y * 24, QUARTER)), parts, name="x_sum").reshape(N_Y, 24, QUARTER)
     parts = lax.all_to_all(parts, ("dp", "tensor"), 0, 0, axis_index_groups=Z_GROUPS, tiled=True)
     input_grad = call(input_sum_kernel, shaped((6, D)), parts, name="input_sum")
-    down_log_grad = call(
-        down_log_kernel, shaped((ROWS, COLS), f32), down_grad, down_w, name="down_log", flops=flops
-    )
+    down_log_grad = down_grad.astype(f32) * down_w
     return input_grad, down_log_grad
 
 

time: 171 us -> 169 us (0.988)
  blocking collectives: 96 us -> 79.9 us
  waiting for transfers between devices: 14.3 us -> 22.6 us
  starting transfers between devices: 21 us -> 26.2 us
    all_to_all x1, blocking collectives: 38.1 us -> 26.4 us  [on_device(): lax.all_to_all(acts, 'tensor', 0, 0, axis_index_groups=X_GROUPS, tiled=True)]
    ppermute x1, waiting for transfers between devices: 0.01 us -> 8.34 us  [on_device(): acts = lax.ppermute(acts, ('dp', 'tensor'), TURN)]
    ppermute x1, starting transfers between devices: 0.67 us -> 5.48 us  [on_device(): acts = lax.ppermute(acts, ('dp', 'tensor'), TURN)]
    all_to_all x1, blocking collectives: 23.4 us -> 20.6 us  [on_device(): lax.all_to_all(acts, 'tensor', 0, 0, axis_index_groups=ZL_GROUPS, tiled=T...]
    unnamed x18 -> x16, local copies, waits for them, and re-layouts: 5.51 us -> 4.6 us
    pallas_call x11 -> x10, Pallas kernels: 16.4 us -> 16 us  [call(): pl.pallas_call(kernel, out_shape=out_shapes, in_specs=specs, out_specs=ja...]
  transfers between devices with their start and end apart: 7 -> 7, of which waited for: 3 -> 4; matrix products, arithmetic and copies ran while one was open for 1% -> 1% of each run, Pallas kernels for 6% -> 6%
where the time goes in v3:
time: 169 us; the launch traced here: 167 us
  blocking collectives  79.9 us (47%)
  starting transfers between devices  26.2 us (16%)
  waiting for transfers between devices  22.6 us (13%)
  Pallas kernels  16 us (9%)
  between operations  14.3 us (8%)
  local copies, waits for them, and re-layouts  5.7 us (3%)
  other arithmetic  1.84 us (1%)
    all_to_all x1, blocking collectives, on_device(): lax.all_to_all(acts, 'tensor', 0, 0, axis_index_groups=X_GROUPS, tiled=True)  26.4 us
    all_to_all x1, blocking collectives, on_device(): lax.all_to_all(acts, 'tensor', 0, 0, axis_index_groups=ZL_GROUPS, tiled=T...  20.6 us
    all_to_all x1, blocking collectives, on_device(): lax.all_to_all(parts, ('dp', 'tensor'), 0, 0, axis_index_groups=Z_GROUPS,...  16.5 us
    all_to_all x1, blocking collectives, on_device(): lax.all_to_all(parts, 'tensor', 0, 0, axis_index_groups=X_GROUPS, tiled=T...  16.4 us
    pallas_call x10, Pallas kernels, call(): pl.pallas_call(kernel, out_shape=out_shapes, in_specs=specs, out_specs=ja...  16 us
    ppermute x1, waiting for transfers between devices, on_device(): gate_up = lax.ppermute(gate_up, 'dp', Z_SWAP)  11.4 us
    ppermute x1, waiting for transfers between devices, on_device(): acts = lax.ppermute(acts, ('dp', 'tensor'), TURN)  8.34 us
    ppermute x1, starting transfers between devices, on_device(): gate_up = lax.ppermute(gate_up, 'dp', Z_SWAP)  8.01 us
  transfers between devices with their start and end apart: 7, of which 4 were waited for; matrix products, arithmetic and copies ran while one was open for 1% of the time, Pallas kernels for 6%

profile of v3, /device:TPU:1, one launch (start us, length us, event | category | flops | bytes accessed | tf_op | source)
XLA Modules:
  0.0 166.5 jit_solution(13112003407432572837)
XLA Ops:
  7.2 0.0 all-gather.3.cloned.1.call-start
  7.2 2.8 %decode.1 = (bf16[2,160,768]{2,1,0:T(8,128)(2,1)}, f32[320,256]{1,0:T(8,128)}) custom-call(s32[320,256]{1,0:T(8,128)} %gate_ref.1, s32[320,256]{1,0:T(8,128)} %up_ref.1, s32[320,256]{1,0:T(8,128)} %down_ref.1), custom_call_target="tpu_custom_call" | custom-call | flops 2621440 | bytes 1802240 | tf_op jit(solution)/shard_map/decode/pallas_call | solution.py:228
  10.0 0.0 all-gather.3.cloned.1.call-update
  10.0 0.0 reduce-scatter.2.cloned.1.call-start
  10.1 0.9 fusion
  10.9 0.1 maximum_maximum_fusion
  11.0 5.5 %collective-permute-start = (bf16[160,384]{1,0:T(8,128)(2,1)S(1)}, bf16[160,384]{1,0:T(8,128)(2,1)S(1)}, u32[]{:S(2)}, u32[]{:S(2)}) collective-permute-start(bf16[160,384]{1,0:T(8,128)(2,1)S(1)} %maximum_maximum_fusion), channel_id=1, source_target_pairs={{0,16},{1,17},{2,18},{3,19},{4,20},{5,21},{6,22},{7,23},{8,24},{9,... | collective-permute-start | bytes 368648 | tf_op jit(solution)/shard_map/ppermute | solution.py:261
  16.5 8.3 %collective-permute-done = bf16[160,384]{1,0:T(8,128)(2,1)S(1)} collective-permute-done((bf16[160,384]{1,0:T(8,128)(2,1)S(1)}, bf16[160,384]{1,0:T(8,128)(2,1)S(1)}, u32[]{:S(2)}, u32[]{:S(2)}) %collective-permute-start) | collective-permute-done | bytes 122912 | tf_op jit(solution)/shard_map/ppermute | solution.py:261
  24.9 20.6 %all_to_all.20 = bf16[4,160,384]{2,1,0:T(8,128)(2,1)S(1)} all-to-all(bf16[4,160,384]{2,1,0:T(8,128)(2,1)S(1)} %broadcast_in_dim.4), channel_id=1, replica_groups={{0,2,4,6},{1,3,5,7},{8,10,12,14},{9,11,13,15},{16,18,20,22},{17,19,21,2..., dimensions={0} | all-to-all | bytes 983040 | tf_op jit(solution)/shard_map/all_to_all | solution.py:263
  45.6 0.2 broadcast_in_dim.5
  45.8 26.4 %all_to_all.21.acts_ref.near_ref = bf16[4,4,160,384]{3,2,1,0:T(8,128)(2,1)S(1)} all-to-all(bf16[4,4,160,384]{3,2,1,0:T(8,128)(2,1)S(1)} %broadcast_in_dim.5), channel_id=1, replica_groups={{0,8,16,24},{1,9,17,25},{2,10,18,26},{3,11,19,27},{4,12,20,28},{5,13,21..., dimensions={0} | all-to-all | bytes 3932160 | tf_op jit(solution)/shard_map/all_to_all | solution.py:266
  72.2 0.0 copy-start.2
  72.2 0.0 all-gather.3.cloned.1.call-done
  72.2 4.4 %collective-permute-start.1 = (bf16[4,4,160,384]{3,2,1,0:T(8,128)(2,1)S(1)}, bf16[4,4,160,384]{3,2,1,0:T(8,128)(2,1)}, u32[]{:S(2)}, u32[]{:S(2)}) collective-permute-start(bf16[4,4,160,384]{3,2,1,0:T(8,128)(2,1)S(1)} %all_to_all.21.acts_ref.near_ref), channel_id=1, source_target_pairs={{0,1},{1,0},{2,3},{3,2},{4,5},{5,4},{6,7},{7,6},{8,9},{9,8},{10,11... | collective-permute-start | bytes 5898248 | tf_op jit(solution)/shard_map/ppermute | solution.py:268
  76.7 0.1 pad_add_fusion.pos_ref
  76.7 2.1 %copy-done = bf16[16,160,768]{2,1,0:T(8,128)(2,1)S(1)} copy-done((bf16[16,160,768]{2,1,0:T(8,128)(2,1)S(1)}, bf16[16,160,768]{2,1,0:T(8,128)(2,1)}, u32[]{:S(2)}) %copy-start) | copy-done | bytes 3932184
  78.9 2.0 %forward_near.1.near_ref = f32[2,192,768]{2,1,0:T(8,128)S(1)} custom-call(s32[4]{0:T(128)S(1)} %pad_add_fusion.pos_ref, bf16[4,4,160,384]{3,2,1,0:T(8,128)(2,1)S(1)} %all_to_all.21.acts_ref.near_ref, bf16[8,2,160,768]{3,2,1,0:T(8,128)(2,1)S(1)} %bitcast.9), custom_call_target="tpu_custom_call" | custom-call | flops 754974720 | bytes 7077904 | tf_op jit(solution)/shard_map/forward_near/pallas_call | solution.py:228
  80.8 0.0 copy-done.2
  80.8 0.0 collective-permute-done.1.acts_ref.far_ref
  80.8 0.1 copy-done.1
  81.0 3.0 %forward_far.1 = (f32[2,192,768]{2,1,0:T(8,128)S(1)}, bf16[2,192,512]{2,1,0:T(8,128)(2,1)S(1)}, bf16[2,192,256]{2,1,0:T(8,128)(2,1)S(1)}) custom-call(s32[4]{0:T(128)S(1)} %pad_add_fusion.pos_ref, bf16[4,4,160,384]{3,2,1,0:T(8,128)(2,1)} %collective-permute-done.1.acts_ref.far_ref, bf16[8,2,160,768]{3,2,1,0:T(8,128)(2,1)S(1)} %bitcast.10, ...), custom_call_target="tpu_custom_call" | custom-call | tf_op jit(solution)/shard_map/forward_far/pallas_call | solution.py:228
  84.0 0.0 copy-start.4
  84.0 8.0 %collective-permute-start.2 = (bf16[2,192,512]{2,1,0:T(8,128)(2,1)S(1)}, bf16[2,192,512]{2,1,0:T(8,128)(2,1)S(1)}, u32[]{:S(2)}, u32[]{:S(2)}) collective-permute-start(bf16[2,192,512]{2,1,0:T(8,128)(2,1)S(1)} %get-tuple-element.17), channel_id=1, source_target_pairs={{0,256},{32,288},{64,320},{96,352},{128,384},{160,416},{192,448},{... | collective-permute-start | bytes 1179656 | tf_op jit(solution)/shard_map/ppermute | solution.py:278
  92.0 1.9 %collective-permute-start.3 = (bf16[2,192,256]{2,1,0:T(8,128)(2,1)S(1)}, bf16[2,192,256]{2,1,0:T(8,128)(2,1)S(1)}, u32[]{:S(2)}, u32[]{:S(2)}) collective-permute-start(bf16[2,192,256]{2,1,0:T(8,128)(2,1)S(1)} %get-tuple-element.18), channel_id=1, source_target_pairs={{0,256},{32,288},{64,320},{96,352},{128,384},{160,416},{192,448},{... | collective-permute-start | bytes 589832 | tf_op jit(solution)/shard_map/ppermute | solution.py:279
  93.9 0.0 copy-start.3
  93.9 0.2 copy.8.refs_3_
  94.1 11.4 %collective-permute-done.2.got_ref.refs_1_ = bf16[2,192,512]{2,1,0:T(8,128)(2,1)S(1)} collective-permute-done((bf16[2,192,512]{2,1,0:T(8,128)(2,1)S(1)}, bf16[2,192,512]{2,1,0:T(8,128)(2,1)S(1)}, u32[]{:S(2)}, u32[]{:S(2)}) %collective-permute-start.2) | collective-permute-done | bytes 393248 | tf_op jit(solution)/shard_map/ppermute | solution.py:278
  105.5 0.0 copy-done.4
  105.5 0.0 copy-done.3
  105.5 2.8 %down.1 = bf16[8,2,160,256]{3,2,1,0:T(8,128)(2,1)S(1)} custom-call(s32[4]{0:T(128)S(1)} %pad_add_fusion.pos_ref, bf16[4,4,160,384]{3,2,1,0:T(8,128)(2,1)S(1)} %copy-done.3, bf16[4,4,160,384]{3,2,1,0:T(8,128)(2,1)} %collective-permute-done.1.acts_ref.far_ref, f32[2,192,768]{2,1,0:T(8,128)S(1)} %get-tuple-element.16.own_ref.refs_0_, ...), custom_call_target="tpu_custom_call" | custom-call | tf_op jit(solution)/shard_map/down/pallas_call | solution.py:228
  108.3 0.0 copy-start.6
  108.3 1.1 copy-done.6
  109.4 2.6 %collective-permute-done.3.refs_2_ = bf16[2,192,256]{2,1,0:T(8,128)(2,1)S(1)} collective-permute-done((bf16[2,192,256]{2,1,0:T(8,128)(2,1)S(1)}, bf16[2,192,256]{2,1,0:T(8,128)(2,1)S(1)}, u32[]{:S(2)}, u32[]{:S(2)}) %collective-permute-start.3) | collective-permute-done | bytes 196640 | tf_op jit(solution)/shard_map/ppermute | solution.py:279
  111.9 0.0 reduce-scatter.2.cloned.1.call-update
  112.0 0.0 copy-start.5
  112.0 1.3 copy-done.5
  113.2 1.9 %input_send.1 = bf16[4,48,2560]{2,1,0:T(8,128)(2,1)S(1)} custom-call(s32[4]{0:T(128)S(1)} %pad_add_fusion.pos_ref, f32[2,192,768]{2,1,0:T(8,128)S(1)} %copy-done.5, bf16[2,192,512]{2,1,0:T(8,128)(2,1)S(1)} %collective-permute-done.2.got_ref.refs_1_, bf16[2,192,256]{2,1,0:T(8,128)(2,1)S(1)} %collective-permute-done.3.refs_2_, ...), custom_call_target="tpu_custom_call" | custom-call | flops 754974720 | bytes 5373968 | tf_op jit(solution)/shard_map/input_send/pallas_call | solution.py:228
  115.1 6.3 %collective-permute-start.4 = (bf16[4,48,2560]{2,1,0:T(8,128)(2,1)S(1)}, bf16[4,48,2560]{2,1,0:T(8,128)(2,1)S(1)}, u32[]{:S(2)}, u32[]{:S(2)}) collective-permute-start(bf16[4,48,2560]{2,1,0:T(8,128)(2,1)S(1)} %input_send.1), channel_id=1, source_target_pairs={{0,1},{1,0},{2,3},{3,2},{4,5},{5,4},{6,7},{7,6},{8,9},{9,8},{10,11... | collective-permute-start | bytes 2949128 | tf_op jit(solution)/shard_map/ppermute | solution.py:291
  121.5 1.9 %input_keep.1.a_ref = bf16[4,48,2560]{2,1,0:T(8,128)(2,1)S(1)} custom-call(s32[4]{0:T(128)S(1)} %pad_add_fusion.pos_ref, f32[2,192,768]{2,1,0:T(8,128)S(1)} %copy-done.5, bf16[2,192,512]{2,1,0:T(8,128)(2,1)S(1)} %collective-permute-done.2.got_ref.refs_1_, bf16[2,192,256]{2,1,0:T(8,128)(2,1)S(1)} %collective-permute-done.3.refs_2_, ...), custom_call_target="tpu_custom_call" | custom-call | flops 754974720 | bytes 5373968 | tf_op jit(solution)/shard_map/input_keep/pallas_call | solution.py:228
  123.4 0.3 collective-permute-done.4.b_ref
  123.6 0.2 add.25
  123.9 0.0 copy-start.7
  123.9 16.4 %all_to_all.22.parts_ref = bf16[4,48,2560]{2,1,0:T(8,128)(2,1)S(1)} all-to-all(bf16[4,48,2560]{2,1,0:T(8,128)(2,1)S(1)} %add.25), channel_id=1, replica_groups={{0,8,16,24},{1,9,17,25},{2,10,18,26},{3,11,19,27},{4,12,20,28},{5,13,21..., dimensions={0} | all-to-all | bytes 1966080 | tf_op jit(solution)/shard_map/all_to_all | solution.py:294
  140.3 0.4 x_sum.1
  140.7 16.5 %all_to_all.23.parts_ref = bf16[8,24,640]{2,1,0:T(8,128)(2,1)S(1)} all-to-all(bf16[8,24,640]{2,1,0:T(8,128)(2,1)S(1)} %bitcast.13), channel_id=1, replica_groups={{0,2,4,6,256,258,260,262},{1,3,5,7,257,259,261,263},{8,10,12,14,264,266..., dimensions={0} | all-to-all | bytes 491520 | tf_op jit(solution)/shard_map/all_to_all | solution.py:296
  157.2 0.8 input_sum.1
  158.0 0.0 copy-done.7
  158.0 1.7 %convert_multiply_fusion = f32[320,256]{1,0:T(8,128)} fusion(f32[320,256]{1,0:T(8,128)S(1)} %copy-done.7, bf16[320,256]{1,0:T(8,128)(2,1)} %reduce-scatter.2.cloned.1.call-done), kind=kLoop, calls=%fused_computation | loop fusion | flops 163840 | bytes 819200 | tf_op jit(solution)/shard_map/mul | solution.py:298
  (4 shorter events, 0.0 us)
Async XLA Ops:
  7.2 65.0 %all-gather.3.cloned.1.call-start = ((), (), s32[]{:S(2)}) async-start(), calls=%async_computation.6 | async-start | bytes 4423680 | tf_op jit(solution)/shard_map/all_gather | solution.py:254
  10.0 148.0 %reduce-scatter.2.cloned.1.call-start = ((), (), s32[]{:S(2)}) async-start(), calls=%async_computation.5 | async-start | bytes 1474560 | tf_op jit(solution)/shard_map/reduce_scatter | solution.py:284
  11.0 13.8 %collective-permute-start = (bf16[160,384]{1,0:T(8,128)(2,1)S(1)}, bf16[160,384]{1,0:T(8,128)(2,1)S(1)}, u32[]{:S(2)}, u32[]{:S(2)}) collective-permute-start(bf16[160,384]{1,0:T(8,128)(2,1)S(1)} %maximum_maximum_fusion), channel_id=1, source_target_pairs={{0,16},{1,17},{2,18},{3,19},{4,20},{5,21},{6,22},{7,23},{8,24},{9,... | collective-permute-start | bytes 368648 | tf_op jit(solution)/shard_map/ppermute | solution.py:261
  72.2 8.7 %copy-start.2 = (bf16[4,4,160,384]{3,2,1,0:T(8,128)(2,1)}, bf16[4,4,160,384]{3,2,1,0:T(8,128)(2,1)S(1)}, u32[]{:S(2)}) copy-start(bf16[4,4,160,384]{3,2,1,0:T(8,128)(2,1)S(1)} %all_to_all.21.acts_ref.near_ref) | copy-start | bytes 5898244
  72.2 8.7 %collective-permute-start.1 = (bf16[4,4,160,384]{3,2,1,0:T(8,128)(2,1)S(1)}, bf16[4,4,160,384]{3,2,1,0:T(8,128)(2,1)}, u32[]{:S(2)}, u32[]{:S(2)}) collective-permute-start(bf16[4,4,160,384]{3,2,1,0:T(8,128)(2,1)S(1)} %all_to_all.21.acts_ref.near_ref), channel_id=1, source_target_pairs={{0,1},{1,0},{2,3},{3,2},{4,5},{5,4},{6,7},{7,6},{8,9},{9,8},{10,11... | collective-permute-start | bytes 5898248 | tf_op jit(solution)/shard_map/ppermute | solution.py:268
  76.7 2.1 %copy-start = (bf16[16,160,768]{2,1,0:T(8,128)(2,1)S(1)}, bf16[16,160,768]{2,1,0:T(8,128)(2,1)}, u32[]{:S(2)}) copy-start(bf16[16,160,768]{2,1,0:T(8,128)(2,1)} %all-gather.3.cloned.1.call-done) | copy-start | bytes 11796484
  78.9 2.1 %copy-start.1 = (bf16[16,160,768]{2,1,0:T(8,128)(2,1)S(1)}, bf16[16,160,768]{2,1,0:T(8,128)(2,1)}, u32[]{:S(2)}) copy-start(bf16[16,160,768]{2,1,0:T(8,128)(2,1)} %all-gather.3.cloned.1.call-done) | copy-start | bytes 11796484
  84.0 21.5 %copy-start.4 = (f32[2,192,768]{2,1,0:T(8,128)}, f32[2,192,768]{2,1,0:T(8,128)S(1)}, u32[]{:S(2)}) copy-start(f32[2,192,768]{2,1,0:T(8,128)S(1)} %get-tuple-element.16.own_ref.refs_0_) | copy-start | bytes 3538948
  84.0 21.5 %collective-permute-start.2 = (bf16[2,192,512]{2,1,0:T(8,128)(2,1)S(1)}, bf16[2,192,512]{2,1,0:T(8,128)(2,1)S(1)}, u32[]{:S(2)}, u32[]{:S(2)}) collective-permute-start(bf16[2,192,512]{2,1,0:T(8,128)(2,1)S(1)} %get-tuple-element.17), channel_id=1, source_target_pairs={{0,256},{32,288},{64,320},{96,352},{128,384},{160,416},{192,448},{... | collective-permute-start | bytes 1179656 | tf_op jit(solution)/shard_map/ppermute | solution.py:278
  92.0 19.9 %collective-permute-start.3 = (bf16[2,192,256]{2,1,0:T(8,128)(2,1)S(1)}, bf16[2,192,256]{2,1,0:T(8,128)(2,1)S(1)}, u32[]{:S(2)}, u32[]{:S(2)}) collective-permute-start(bf16[2,192,256]{2,1,0:T(8,128)(2,1)S(1)} %get-tuple-element.18), channel_id=1, source_target_pairs={{0,256},{32,288},{64,320},{96,352},{128,384},{160,416},{192,448},{... | collective-permute-start | bytes 589832 | tf_op jit(solution)/shard_map/ppermute | solution.py:279
  93.9 11.6 %copy-start.3 = (bf16[4,4,160,384]{3,2,1,0:T(8,128)(2,1)S(1)}, bf16[4,4,160,384]{3,2,1,0:T(8,128)(2,1)}, u32[]{:S(2)}) copy-start(bf16[4,4,160,384]{3,2,1,0:T(8,128)(2,1)} %copy-done.2) | copy-start | bytes 5898244
  108.3 1.1 copy-start.6
  112.0 1.3 copy-start.5
  115.1 8.5 %collective-permute-start.4 = (bf16[4,48,2560]{2,1,0:T(8,128)(2,1)S(1)}, bf16[4,48,2560]{2,1,0:T(8,128)(2,1)S(1)}, u32[]{:S(2)}, u32[]{:S(2)}) collective-permute-start(bf16[4,48,2560]{2,1,0:T(8,128)(2,1)S(1)} %input_send.1), channel_id=1, source_target_pairs={{0,1},{1,0},{2,3},{3,2},{4,5},{5,4},{6,7},{7,6},{8,9},{9,8},{10,11... | collective-permute-start | bytes 2949128 | tf_op jit(solution)/shard_map/ppermute | solution.py:291
  123.9 34.2 %copy-start.7 = (f32[320,256]{1,0:T(8,128)S(1)}, f32[320,256]{1,0:T(8,128)}, u32[]{:S(2)}) copy-start(f32[320,256]{1,0:T(8,128)} %get-tuple-element.23) | copy-start | bytes 983044
Sparse Core Ops, SparseCore 0:
  10.2 60.1 all-gather.2
  112.1 41.7 reduce-scatter.1

commit v4 on v3

--- a/solution.py
+++ b/solution.py
@@ -1,3 +1,4 @@
+import functools
 import math
 
 import jax
@@ -27,17 +28,17 @@
 NT = (((1,), (1,)), ((), ()))
 
 
-def _turn_pairs():
+def _turn_pairs(step):
     pairs = []
     for z in range(N_Z):
         for y in range(N_Y):
             for t in range(N_T):
-                x1, rest = t // 16, t % 16
+                x1, rest = t // 16, (t % 16) ^ (2 * step)
                 pairs.append(((z * N_Y + y) * N_T + t, (x1 * N_Y + y) * N_T + (1 - z) * 16 + rest))
     return pairs
 
 
-TURN = _turn_pairs()
+TURNS = [_turn_pairs(step) for step in range(N_ZL)]
 Z_SWAP = [(d, (d + N_Y) % (N_Z * N_Y)) for d in range(N_Z * N_Y)]
 CORE_SWAP = [(t, t ^ 1) for t in range(N_T)]
 ZL_GROUPS = [[x * 8 + zl * 2 + c for zl in range(N_ZL)] for x in range(N_X) for c in range(2)]
@@ -74,42 +75,37 @@
     down_w_ref[...] = value
 
 
-def forward(acts_ref, which, w_ref):
-    sums = [[None, None], [None, None]]
+def forward(acts_ref, which, my_zl, w_ref, kind):
+    cols = (slice(0, 2 * COLS), slice(2 * COLS, 3 * COLS))[kind]
+    sums = [None, None]
     for x0 in range(2):
-        for kind, cols in ((0, slice(0, 2 * COLS)), (1, slice(2 * COLS, 3 * COLS))):
-            rows = slice(kind * HALF_FEAT, (kind + 1) * HALF_FEAT)
-            acts = []
+        rows = slice(kind * HALF_FEAT, (kind + 1) * HALF_FEAT)
+        acts = []
+        for h in range(2):
+            part = jnp.concatenate([acts_ref[2 - 2 * h + x0, zl ^ my_zl, rows] for zl in range(N_ZL)], axis=0)
+            acts.append(part.T)
+        for half in range(2):
+            rows = slice(half * HALF_FEAT, (half + 1) * HALF_FEAT)
+            w = [w_ref[x0 * N_ZL + zl, which, rows, cols] for zl in range(N_ZL)]
+            w = jnp.concatenate(w, axis=0)
             for h in range(2):
-                part = jnp.concatenate([acts_ref[2 - 2 * h + x0, zl, rows] for zl in range(N_ZL)], axis=0)
-                acts.append(part.T)
-            for half in range(2):
-                rows = slice(half * HALF_FEAT, (half + 1) * HALF_FEAT)
-                w = [w_ref[x0 * N_ZL + zl, which, rows, cols] for zl in range(N_ZL)]
-                w = jnp.concatenate(w, axis=0)
-                for h in range(2):
-                    part = acts[h][half * TOK : (half + 1) * TOK]
-                    part = lax.dot_general(part, w, NN, preferred_element_type=jnp.float32)
-                    sums[h][kind] = part if sums[h][kind] is None else sums[h][kind] + part
+                part = acts[h][half * TOK : (half + 1) * TOK]
+                part = lax.dot_general(part, w, NN, preferred_element_type=jnp.float32)
+                sums[h] = part if sums[h] is None else sums[h] + part
     return sums
 
 
-def near_kernel(pos_ref, acts_ref, w_ref, out_ref):
-    sums = forward(acts_ref, pos_ref[1], w_ref)
-    for h in range(2):
-        out_ref[h, :, : 2 * COLS] = sums[h][0]
-        out_ref[h, :, 2 * COLS :] = sums[h][1]
-
-
-def far_kernel(pos_ref, acts_ref, w_ref, near_ref, own_ref, gate_up_ref, hidden_grad_ref):
-    sums = forward(acts_ref, 1 - pos_ref[1], w_ref)
-    for h in range(2):
-        gate_up = sums[h][0] + near_ref[h, :, : 2 * COLS]
-        hidden_grad = sums[h][1] + near_ref[h, :, 2 * COLS :]
-        own_ref[h, :, : 2 * COLS] = gate_up
-        own_ref[h, :, 2 * COLS :] = hidden_grad
-        gate_up_ref[h] = gate_up.astype(jnp.bfloat16)
-        hidden_grad_ref[h] = hidden_grad.astype(jnp.bfloat16)
+def near_kernel(pos_ref, acts_ref, w_ref, gate_up_ref, hidden_grad_ref):
+    for kind, out_ref in enumerate((gate_up_ref, hidden_grad_ref)):
+        for h, total in enumerate(forward(acts_ref, pos_ref[1], pos_ref[3], w_ref, kind)):
+            out_ref[h] = total
+
+
+def far_kernel(kind, pos_ref, acts_ref, w_ref, near_ref, own_ref, send_ref):
+    for h, total in enumerate(forward(acts_ref, 1 - pos_ref[1], pos_ref[3], w_ref, kind)):
+        total += near_ref[h]
+        own_ref[h] = total
+        send_ref[h] = total.astype(jnp.bfloat16)
 
 
 def copy_kernel(w_ref, out_ref):
@@ -121,7 +117,7 @@
     blank = jnp.zeros((TOK, COLS), jnp.bfloat16)
     rows = []
     for h in range(2):
-        total = own_ref[h, :, : 2 * COLS] + got_ref[h].astype(jnp.float32)
+        total = own_ref[h] + got_ref[h].astype(jnp.float32)
         gate, up = total[:, :COLS], total[:, COLS:]
         hidden = (gate * jax.nn.sigmoid(gate) * up).astype(jnp.bfloat16)
         rows += [jnp.concatenate([hidden, blank], axis=1), jnp.concatenate([blank, hidden], axis=1)]
@@ -129,7 +125,7 @@
     for x0 in range(2):
         for ref, which in ((near_ref, core), (far_ref, 1 - core)):
             grads = [
-                jnp.concatenate([ref[2 - 2 * h + x0, zl, HALF_FEAT:] for zl in range(N_ZL)], axis=0) for h in range(2)
+                jnp.concatenate([ref[2 - 2 * h + x0, zl ^ pos_ref[3], HALF_FEAT:] for zl in range(N_ZL)], axis=0) for h in range(2)
             ]
             acts = jnp.concatenate(grads, axis=1)
             part = lax.dot_general(acts, hidden, NN, preferred_element_type=jnp.float32).astype(jnp.bfloat16)
@@ -139,7 +135,7 @@
                 out_ref[x0 * N_ZL + zl, which, HALF_FEAT:] = rows[:, COLS:]
 
 
-def input_part(pos_ref, own_ref, gate_up_ref, hidden_grad_ref, w_ref, out_ref, side):
+def input_part(pos_ref, own_ref, got_ref, own_hg_ref, got_hg_ref, w_ref, out_ref, side):
     rows = N_X * 48
     row = lax.broadcasted_iota(jnp.int32, (rows, 2 * TOK), 0)
     col = lax.broadcasted_iota(jnp.int32, (rows, 2 * TOK), 1)
@@ -152,9 +148,9 @@
     pick = jnp.where(wanted == col, 1.0, 0.0).astype(jnp.bfloat16)
     grads = []
     for h in range(2):
-        total = own_ref[h, :, : 2 * COLS] + gate_up_ref[h].astype(jnp.float32)
+        total = own_ref[h] + got_ref[h].astype(jnp.float32)
         gate, up = total[:, :COLS], total[:, COLS:]
-        hidden_grad = own_ref[h, :, 2 * COLS :] + hidden_grad_ref[h].astype(jnp.float32)
+        hidden_grad = own_hg_ref[h] + got_hg_ref[h].astype(jnp.float32)
         sig = jax.nn.sigmoid(gate)
         gate_grad = (hidden_grad * up * sig * (1.0 + gate * (1.0 - sig))).astype(jnp.bfloat16)
         up_grad = (hidden_grad * gate * sig).astype(jnp.bfloat16)
@@ -258,41 +254,45 @@
         return jnp.concatenate([acts[:HALF_FEAT], acts[HALF_FEAT:]], axis=1)
 
     acts = jnp.concatenate([folded(inputs), folded(grad_out)], axis=0)
-    acts = lax.ppermute(acts, ("dp", "tensor"), TURN)
-    acts = jnp.broadcast_to(acts[None], (N_ZL, FEAT, 2 * TOK))
-    acts = lax.all_to_all(acts, "tensor", 0, 0, axis_index_groups=ZL_GROUPS, tiled=True)
-
+    acts = jnp.stack([lax.ppermute(acts, ("dp", "tensor"), turn) for turn in TURNS])
     acts = jnp.broadcast_to(acts[None], (N_X, N_ZL, FEAT, 2 * TOK))
     near = lax.all_to_all(acts, "tensor", 0, 0, axis_index_groups=X_GROUPS, tiled=True)
-    near, w = lax.optimization_barrier((near, w))
     far = lax.ppermute(near, "tensor", CORE_SWAP)
 
-    flops = HALF * 3 * COLS * 2 * TOK
-    sums = call(near_kernel, shaped((2, TOK, wide), f32), pos, near, w, name="forward_near", flops=flops)
-    own, gate_up, hidden_grad = call(
-        far_kernel,
-        (shaped((2, TOK, wide), f32), shaped((2, TOK, 2 * COLS)), shaped((2, TOK, COLS))),
-        pos, far, w, sums, name="forward_far",
-    )
-    w_own, _ = lax.optimization_barrier((w, own))
-    gate_up = lax.ppermute(gate_up, "dp", Z_SWAP)
-    hidden_grad = lax.ppermute(hidden_grad, "dp", Z_SWAP)
+    flops = HALF * COLS * 2 * TOK
+    gate_up_shape, hidden_grad_shape = (2, TOK, 2 * COLS), (2, TOK, COLS)
+    gate_up, hidden_grad = call(
+        near_kernel, (shaped(gate_up_shape, f32), shaped(hidden_grad_shape, f32)), pos, near, w,
+        name="forward_near", flops=3 * flops,
+    )
+    own, send = call(
+        functools.partial(far_kernel, 0), (shaped(gate_up_shape, f32), shaped(gate_up_shape)), pos, far, w, gate_up,
+        name="gate_up",
+    )
+    got = lax.ppermute(send, "dp", Z_SWAP)
+    own_hg, send = call(
+        functools.partial(far_kernel, 1), (shaped(hidden_grad_shape, f32), shaped(hidden_grad_shape)), pos, far, w,
+        hidden_grad, name="hidden_grad",
+    )
+    got_hg = lax.ppermute(send, "dp", Z_SWAP)
+    w_own, _ = lax.optimization_barrier((w, own_hg))
     w_gate_up = call(copy_kernel, shaped((N_Y, 2, FEAT, 2 * COLS)), w_own, name="copy", flops=flops)
 
-    down = call(down_kernel, shaped((N_Y, 2, FEAT, COLS)), pos, near, far, own, gate_up, name="down")
-    down, hidden_grad, w_gate_up = lax.optimization_barrier((down, hidden_grad, w_gate_up))
+    got, own_hg = lax.optimization_barrier((got, own_hg))
+    down = call(down_kernel, shaped((N_Y, 2, FEAT, COLS)), pos, near, far, own, got, name="down")
     down_grad = lax.psum_scatter(
         down.reshape(N_Y * ROWS, COLS), "dp", scatter_dimension=0, axis_index_groups=Y_GROUPS, tiled=True
     )
+    down, got_hg, w_gate_up = lax.optimization_barrier((down, got_hg, w_gate_up))
 
     out = shaped((N_X, 48, HALF))
-    grads = (own, gate_up, hidden_grad)
+    grads = (own, got, own_hg, got_hg)
     send = call(input_send_kernel, out, pos, *grads, w_gate_up, name="input_send", flops=flops)
     other = lax.ppermute(send, "tensor", CORE_SWAP)
     keep = call(input_keep_kernel, out, pos, *grads, w_gate_up, name="input_keep", flops=flops)
     parts = call(add_kernel, out, keep, other, name="add")
     parts = lax.all_to_all(parts, "tensor", 0, 0, axis_index_groups=X_GROUPS, tiled=True)
-    parts = call(x_sum_kernel, shaped((N_Y * 24, QUARTER)), parts, name="x_sum").reshape(N_Y, 24, QUARTER)
+    parts = call(x_sum_kernel, shaped((N_Y * 24, QUARTER)), parts, name="x_sum", flops=35 * 10**8).reshape(N_Y, 24, QUARTER)
     parts = lax.all_to_all(parts, ("dp", "tensor"), 0, 0, axis_index_groups=Z_GROUPS, tiled=True)
     input_grad = call(input_sum_kernel, shaped((6, D)), parts, name="input_sum")
     down_log_grad = down_grad.astype(f32) * down_w

time: 169 us -> 166 us (0.982)
  starting transfers between devices: 26.2 us -> 38.9 us
  waiting for transfers between devices: 22.6 us -> 11.5 us
  blocking collectives: 79.9 us -> 71.8 us
  Pallas kernels: 16 us -> 19.3 us
    all_to_all x1 -> x0, blocking collectives: 20.6 us -> none  [on_device(): lax.all_to_all(acts, 'tensor', 0, 0, axis_index_groups=ZL_GROUPS, tiled=T...]
    ppermute x3 -> x6, starting transfers between devices: 15.4 us -> 31.2 us  [the longest x4 22 us: on_device(): lax.ppermute(acts, ('dp', 'tensor'), turn)]
    ppermute x3 -> x6, waiting for transfers between devices: 22.3 us -> 11.4 us  [the longest x4 6.74 us: on_device(): lax.ppermute(acts, ('dp', 'tensor'), turn)]
    all_to_all x1, blocking collectives: 16.5 us -> 24.7 us  [on_device(): lax.all_to_all(parts, ('dp', 'tensor'), 0, 0, axis_index_groups=Z_GROUPS,...]
    all_to_all x1, blocking collectives: 26.4 us -> 30.4 us  [on_device(): lax.all_to_all(acts, 'tensor', 0, 0, axis_index_groups=X_GROUPS, tiled=True)]
    pallas_call x10 -> x11, Pallas kernels: 16 us -> 19.3 us  [call(): pl.pallas_call(kernel, out_shape=out_shapes, in_specs=specs, out_specs=ja...]
    ppermute x1, starting transfers between devices: 6.31 us -> 3.18 us  [on_device(): other = lax.ppermute(send, 'tensor', CORE_SWAP)]
    unnamed x16 -> x10, local copies, waits for them, and re-layouts: 4.6 us -> 5.39 us
  transfers between devices with their start and end apart: 7 -> 10, of which waited for: 4 -> 3; matrix products, arithmetic and copies ran while one was open for 1% -> 1% of each run, Pallas kernels for 6% -> 8%
where the time goes in v4:
time: 166 us; the launch traced here: 164 us
  blocking collectives  71.8 us (43%)
  starting transfers between devices  38.9 us (23%)
  Pallas kernels  19.3 us (12%)
  between operations  14.3 us (9%)
  waiting for transfers between devices  11.5 us (7%)
  local copies, waits for them, and re-layouts  6.44 us (4%)
  other arithmetic  1.92 us (1%)
    all_to_all x1, blocking collectives, on_device(): lax.all_to_all(acts, 'tensor', 0, 0, axis_index_groups=X_GROUPS, tiled=True)  30.4 us
    all_to_all x1, blocking collectives, on_device(): lax.all_to_all(parts, ('dp', 'tensor'), 0, 0, axis_index_groups=Z_GROUPS,...  24.7 us
    ppermute x4, starting transfers between devices, on_device(): lax.ppermute(acts, ('dp', 'tensor'), turn)  22 us
    pallas_call x11, Pallas kernels, call(): pl.pallas_call(kernel, out_shape=out_shapes, in_specs=specs, out_specs=ja...  19.3 us
    all_to_all x1, blocking collectives, on_device(): lax.all_to_all(parts, 'tensor', 0, 0, axis_index_groups=X_GROUPS, tiled=T...  16.7 us
    ppermute x4, waiting for transfers between devices, on_device(): lax.ppermute(acts, ('dp', 'tensor'), turn)  6.74 us
    ppermute x1, starting transfers between devices, on_device(): got_hg = lax.ppermute(send, 'dp', Z_SWAP)  6.21 us
    unnamed x10, local copies, waits for them, and re-layouts  5.39 us
  transfers between devices with their start and end apart: 10, of which 3 were waited for; matrix products, arithmetic and copies ran while one was open for 1% of the time, Pallas kernels for 8%

profile of v4, /device:TPU:1, one launch (start us, length us, event | category | flops | bytes accessed | tf_op | source)
XLA Modules:
  0.0 164.1 jit_solution(2562941347571239971)
XLA Ops:
  7.2 0.0 all-gather.3.cloned.1.call-start
  7.2 2.8 %decode.1 = (bf16[2,160,768]{2,1,0:T(8,128)(2,1)}, f32[320,256]{1,0:T(8,128)}) custom-call(s32[320,256]{1,0:T(8,128)} %gate_ref.1, s32[320,256]{1,0:T(8,128)} %up_ref.1, s32[320,256]{1,0:T(8,128)} %down_ref.1), custom_call_target="tpu_custom_call" | custom-call | flops 2621440 | bytes 1802240 | tf_op jit(solution)/shard_map/decode/pallas_call | solution.py:224
  10.0 0.0 all-gather.3.cloned.1.call-update
  10.0 0.0 reduce-scatter.2.cloned.1.call-start
  10.1 0.9 fusion
  10.9 0.1 maximum_maximum_fusion
  11.0 10.9 %collective-permute-start.3 = (bf16[160,384]{1,0:T(8,128)(2,1)S(1)}, bf16[160,384]{1,0:T(8,128)(2,1)S(1)}, u32[]{:S(2)}, u32[]{:S(2)}) collective-permute-start(bf16[160,384]{1,0:T(8,128)(2,1)S(1)} %maximum_maximum_fusion), channel_id=1, source_target_pairs={{0,22},{1,23},{2,20},{3,21},{4,18},{5,19},{6,16},{7,17},{8,30},{9,... | collective-permute-start | bytes 368648 | tf_op jit(solution)/shard_map/ppermute | solution.py:257
  21.9 6.1 %collective-permute-start.2 = (bf16[160,384]{1,0:T(8,128)(2,1)S(1)}, bf16[160,384]{1,0:T(8,128)(2,1)S(1)}, u32[]{:S(2)}, u32[]{:S(2)}) collective-permute-start(bf16[160,384]{1,0:T(8,128)(2,1)S(1)} %maximum_maximum_fusion), channel_id=1, source_target_pairs={{0,20},{1,21},{2,22},{3,23},{4,16},{5,17},{6,18},{7,19},{8,28},{9,... | collective-permute-start | bytes 368648 | tf_op jit(solution)/shard_map/ppermute | solution.py:257
  28.1 2.1 %collective-permute-start.1 = (bf16[160,384]{1,0:T(8,128)(2,1)S(1)}, bf16[160,384]{1,0:T(8,128)(2,1)S(1)}, u32[]{:S(2)}, u32[]{:S(2)}) collective-permute-start(bf16[160,384]{1,0:T(8,128)(2,1)S(1)} %maximum_maximum_fusion), channel_id=1, source_target_pairs={{0,18},{1,19},{2,16},{3,17},{4,22},{5,23},{6,20},{7,21},{8,26},{9,... | collective-permute-start | bytes 368648 | tf_op jit(solution)/shard_map/ppermute | solution.py:257
  30.2 2.9 %collective-permute-start = (bf16[160,384]{1,0:T(8,128)(2,1)S(1)}, bf16[160,384]{1,0:T(8,128)(2,1)S(1)}, u32[]{:S(2)}, u32[]{:S(2)}) collective-permute-start(bf16[160,384]{1,0:T(8,128)(2,1)S(1)} %maximum_maximum_fusion), channel_id=1, source_target_pairs={{0,16},{1,17},{2,18},{3,19},{4,20},{5,21},{6,22},{7,23},{8,24},{9,... | collective-permute-start | bytes 368648 | tf_op jit(solution)/shard_map/ppermute | solution.py:257
  33.1 0.0 collective-permute-done.3
  33.1 0.0 collective-permute-done.2
  33.1 3.9 %collective-permute-done.1 = bf16[160,384]{1,0:T(8,128)(2,1)S(1)} collective-permute-done((bf16[160,384]{1,0:T(8,128)(2,1)S(1)}, bf16[160,384]{1,0:T(8,128)(2,1)S(1)}, u32[]{:S(2)}, u32[]{:S(2)}) %collective-permute-start.1) | collective-permute-done | bytes 122912 | tf_op jit(solution)/shard_map/ppermute | solution.py:257
  37.0 2.9 %collective-permute-done = bf16[160,384]{1,0:T(8,128)(2,1)S(1)} collective-permute-done((bf16[160,384]{1,0:T(8,128)(2,1)S(1)}, bf16[160,384]{1,0:T(8,128)(2,1)S(1)}, u32[]{:S(2)}, u32[]{:S(2)}) %collective-permute-start) | collective-permute-done | bytes 122912 | tf_op jit(solution)/shard_map/ppermute | solution.py:257
  39.8 0.1 pad_maximum_fusion
  39.9 0.2 broadcast_in_dim.2
  40.1 30.4 %all_to_all.15.acts_ref.near_ref = bf16[4,4,160,384]{3,2,1,0:T(8,128)(2,1)S(1)} all-to-all(bf16[4,4,160,384]{3,2,1,0:T(8,128)(2,1)S(1)} %broadcast_in_dim.2), channel_id=1, replica_groups={{0,8,16,24},{1,9,17,25},{2,10,18,26},{3,11,19,27},{4,12,20,28},{5,13,21..., dimensions={0} | all-to-all | bytes 3932160 | tf_op jit(solution)/shard_map/all_to_all | solution.py:259
  70.5 4.5 %collective-permute-start.4 = (bf16[4,4,160,384]{3,2,1,0:T(8,128)(2,1)S(1)}, bf16[4,4,160,384]{3,2,1,0:T(8,128)(2,1)}, u32[]{:S(2)}, u32[]{:S(2)}) collective-permute-start(bf16[4,4,160,384]{3,2,1,0:T(8,128)(2,1)S(1)} %all_to_all.15.acts_ref.near_ref), channel_id=1, source_target_pairs={{0,1},{1,0},{2,3},{3,2},{4,5},{5,4},{6,7},{7,6},{8,9},{9,8},{10,11... | collective-permute-start | bytes 5898248 | tf_op jit(solution)/shard_map/ppermute | solution.py:260
  75.0 0.1 pad_add_fusion.pos_ref
  75.1 0.0 all-gather.3.cloned.1.call-done
  75.1 2.1 %copy-done = bf16[16,160,768]{2,1,0:T(8,128)(2,1)S(1)} copy-done((bf16[16,160,768]{2,1,0:T(8,128)(2,1)S(1)}, bf16[16,160,768]{2,1,0:T(8,128)(2,1)}, u32[]{:S(2)}) %copy-start) | copy-done | bytes 3932184
  77.2 2.0 %forward_near.1 = (f32[2,192,512]{2,1,0:T(8,128)S(1)}, f32[2,192,256]{2,1,0:T(8,128)S(1)}) custom-call(s32[4]{0:T(128)S(1)} %pad_add_fusion.pos_ref, bf16[4,4,160,384]{3,2,1,0:T(8,128)(2,1)S(1)} %all_to_all.15.acts_ref.near_ref, bf16[8,2,160,768]{3,2,1,0:T(8,128)(2,1)S(1)} %bitcast.13), custom_call_target="tpu_custom_call" | custom-call | flops 754974720 | bytes 7077904 | tf_op jit(solution)/shard_map/forward_near/pallas_call | solution.py:224
  79.2 0.0 collective-permute-done.4.acts_ref.far_ref
  79.2 0.1 copy-done.1
  79.3 2.6 %gate_up.1 = (f32[2,192,512]{2,1,0:T(8,128)S(1)}, bf16[2,192,512]{2,1,0:T(8,128)(2,1)S(1)}) custom-call(s32[4]{0:T(128)S(1)} %pad_add_fusion.pos_ref, bf16[4,4,160,384]{3,2,1,0:T(8,128)(2,1)} %collective-permute-done.4.acts_ref.far_ref, bf16[8,2,160,768]{3,2,1,0:T(8,128)(2,1)S(1)} %bitcast.14, f32[2,192,512]{2,1,0:T(8,128)S(1)} %get-tuple-element.16.near_ref), custom_call_target="tpu_custom_call" | custom-call | tf_op jit(solution)/shard_map/gate_up/pallas_call | solution.py:224
  81.9 3.0 %collective-permute-start.5 = (bf16[2,192,512]{2,1,0:T(8,128)(2,1)S(1)}, bf16[2,192,512]{2,1,0:T(8,128)(2,1)S(1)}, u32[]{:S(2)}, u32[]{:S(2)}) collective-permute-start(bf16[2,192,512]{2,1,0:T(8,128)(2,1)S(1)} %get-tuple-element.18), channel_id=1, source_target_pairs={{0,256},{32,288},{64,320},{96,352},{128,384},{160,416},{192,448},{... | collective-permute-start | bytes 1179656 | tf_op jit(solution)/shard_map/ppermute | solution.py:272
  84.9 2.9 %hidden_grad.1 = (f32[2,192,256]{2,1,0:T(8,128)S(1)}, bf16[2,192,256]{2,1,0:T(8,128)(2,1)}) custom-call(s32[4]{0:T(128)S(1)} %pad_add_fusion.pos_ref, bf16[4,4,160,384]{3,2,1,0:T(8,128)(2,1)} %collective-permute-done.4.acts_ref.far_ref, bf16[8,2,160,768]{3,2,1,0:T(8,128)(2,1)S(1)} %bitcast.15, f32[2,192,256]{2,1,0:T(8,128)S(1)} %get-tuple-element.19.near_ref), custom_call_target="tpu_custom_call" | custom-call | tf_op jit(solution)/shard_map/hidden_grad/pallas_call | solution.py:224
  87.8 6.2 %collective-permute-start.6 = (bf16[2,192,256]{2,1,0:T(8,128)(2,1)}, bf16[2,192,256]{2,1,0:T(8,128)(2,1)}, u32[]{:S(2)}, u32[]{:S(2)}) collective-permute-start(bf16[2,192,256]{2,1,0:T(8,128)(2,1)} %get-tuple-element.23), channel_id=1, source_target_pairs={{0,256},{32,288},{64,320},{96,352},{128,384},{160,416},{192,448},{... | collective-permute-start | bytes 589832 | tf_op jit(solution)/shard_map/ppermute | solution.py:277
  94.0 4.7 %collective-permute-done.5.got_ref.refs_1_ = bf16[2,192,512]{2,1,0:T(8,128)(2,1)S(1)} collective-permute-done((bf16[2,192,512]{2,1,0:T(8,128)(2,1)S(1)}, bf16[2,192,512]{2,1,0:T(8,128)(2,1)S(1)}, u32[]{:S(2)}, u32[]{:S(2)}) %collective-permute-start.5) | collective-permute-done | bytes 393248 | tf_op jit(solution)/shard_map/ppermute | solution.py:272
  98.7 2.8 %down.1 = bf16[8,2,160,256]{3,2,1,0:T(8,128)(2,1)S(1)} custom-call(s32[4]{0:T(128)S(1)} %pad_add_fusion.pos_ref, bf16[4,4,160,384]{3,2,1,0:T(8,128)(2,1)S(1)} %all_to_all.15.acts_ref.near_ref, bf16[4,4,160,384]{3,2,1,0:T(8,128)(2,1)} %collective-permute-done.4.acts_ref.far_ref, f32[2,192,512]{2,1,0:T(8,128)S(1)} %get-tuple-element.17.own_ref.refs_0_, ...), custom_call_target="tpu_custom_call" | custom-call | tf_op jit(solution)/shard_map/down/pallas_call | solution.py:224
  101.5 0.0 copy-start.3
  101.5 1.0 copy-done.3
  102.5 0.0 reduce-scatter.2.cloned.1.call-update
  102.6 0.0 copy-start.2
  102.6 2.1 %copy-done.2 = bf16[16,160,768]{2,1,0:T(8,128)(2,1)S(1)} copy-done((bf16[16,160,768]{2,1,0:T(8,128)(2,1)S(1)}, bf16[16,160,768]{2,1,0:T(8,128)(2,1)}, u32[]{:S(2)}) %copy-start.2) | copy-done | bytes 3932184
  104.7 0.2 copy.8.refs_4_
  104.9 0.0 collective-permute-done.6.refs_3_
  104.9 2.3 %input_send.1 = bf16[4,48,2560]{2,1,0:T(8,128)(2,1)S(1)} custom-call(s32[4]{0:T(128)S(1)} %pad_add_fusion.pos_ref, f32[2,192,512]{2,1,0:T(8,128)S(1)} %get-tuple-element.17.own_ref.refs_0_, bf16[2,192,512]{2,1,0:T(8,128)(2,1)S(1)} %collective-permute-done.5.got_ref.refs_1_, f32[2,192,256]{2,1,0:T(8,128)S(1)} %get-tuple-element.22.refs_2_, ...), custom_call_target="tpu_custom_call" | custom-call | flops 251658240 | bytes 5373968 | tf_op jit(solution)/shard_map/input_send/pallas_call | solution.py:224
  107.2 3.2 %collective-permute-start.7 = (bf16[4,48,2560]{2,1,0:T(8,128)(2,1)S(1)}, bf16[4,48,2560]{2,1,0:T(8,128)(2,1)S(1)}, u32[]{:S(2)}, u32[]{:S(2)}) collective-permute-start(bf16[4,48,2560]{2,1,0:T(8,128)(2,1)S(1)} %input_send.1), channel_id=1, source_target_pairs={{0,1},{1,0},{2,3},{3,2},{4,5},{5,4},{6,7},{7,6},{8,9},{9,8},{10,11... | collective-permute-start | bytes 2949128 | tf_op jit(solution)/shard_map/ppermute | solution.py:291
  110.4 2.3 %input_keep.1.a_ref = bf16[4,48,2560]{2,1,0:T(8,128)(2,1)S(1)} custom-call(s32[4]{0:T(128)S(1)} %pad_add_fusion.pos_ref, f32[2,192,512]{2,1,0:T(8,128)S(1)} %get-tuple-element.17.own_ref.refs_0_, bf16[2,192,512]{2,1,0:T(8,128)(2,1)S(1)} %collective-permute-done.5.got_ref.refs_1_, f32[2,192,256]{2,1,0:T(8,128)S(1)} %get-tuple-element.22.refs_2_, ...), custom_call_target="tpu_custom_call" | custom-call | flops 251658240 | bytes 5373968 | tf_op jit(solution)/shard_map/input_keep/pallas_call | solution.py:224
  112.7 0.0 collective-permute-done.7.b_ref
  112.7 0.2 add.25
  112.9 16.7 %all_to_all.16.parts_ref = bf16[4,48,2560]{2,1,0:T(8,128)(2,1)S(1)} all-to-all(bf16[4,48,2560]{2,1,0:T(8,128)(2,1)S(1)} %add.25), channel_id=1, replica_groups={{0,8,16,24},{1,9,17,25},{2,10,18,26},{3,11,19,27},{4,12,20,28},{5,13,21..., dimensions={0} | all-to-all | bytes 1966080 | tf_op jit(solution)/shard_map/all_to_all | solution.py:294
  129.6 0.4 x_sum.1
  130.1 24.7 %all_to_all.17.parts_ref = bf16[8,24,640]{2,1,0:T(8,128)(2,1)S(1)} all-to-all(bf16[8,24,640]{2,1,0:T(8,128)(2,1)S(1)} %bitcast.18), channel_id=1, replica_groups={{0,2,4,6,256,258,260,262},{1,3,5,7,257,259,261,263},{8,10,12,14,264,266..., dimensions={0} | all-to-all | bytes 491520 | tf_op jit(solution)/shard_map/all_to_all | solution.py:296
  154.8 0.8 input_sum.1
  155.6 0.0 copy-done.4
  155.6 1.7 %convert_multiply_fusion = f32[320,256]{1,0:T(8,128)} fusion(f32[320,256]{1,0:T(8,128)S(1)} %copy-done.4, bf16[320,256]{1,0:T(8,128)(2,1)} %reduce-scatter.2.cloned.1.call-done), kind=kLoop, calls=%fused_computation.1 | loop fusion | flops 163840 | bytes 819200 | tf_op jit(solution)/shard_map/mul | solution.py:298
  (4 shorter events, 0.0 us)
Async XLA Ops:
  7.2 67.9 %all-gather.3.cloned.1.call-start = ((), (), s32[]{:S(2)}) async-start(), calls=%async_computation.5 | async-start | bytes 4423680 | tf_op jit(solution)/shard_map/all_gather | solution.py:250
  10.0 145.6 %reduce-scatter.2.cloned.1.call-start = ((), (), s32[]{:S(2)}) async-start(), calls=%async_computation.4 | async-start | bytes 1474560 | tf_op jit(solution)/shard_map/reduce_scatter | solution.py:283
  11.0 22.0 %collective-permute-start.3 = (bf16[160,384]{1,0:T(8,128)(2,1)S(1)}, bf16[160,384]{1,0:T(8,128)(2,1)S(1)}, u32[]{:S(2)}, u32[]{:S(2)}) collective-permute-start(bf16[160,384]{1,0:T(8,128)(2,1)S(1)} %maximum_maximum_fusion), channel_id=1, source_target_pairs={{0,22},{1,23},{2,20},{3,21},{4,18},{5,19},{6,16},{7,17},{8,30},{9,... | collective-permute-start | bytes 368648 | tf_op jit(solution)/shard_map/ppermute | solution.py:257
  21.9 11.1 %collective-permute-start.2 = (bf16[160,384]{1,0:T(8,128)(2,1)S(1)}, bf16[160,384]{1,0:T(8,128)(2,1)S(1)}, u32[]{:S(2)}, u32[]{:S(2)}) collective-permute-start(bf16[160,384]{1,0:T(8,128)(2,1)S(1)} %maximum_maximum_fusion), channel_id=1, source_target_pairs={{0,20},{1,21},{2,22},{3,23},{4,16},{5,17},{6,18},{7,19},{8,28},{9,... | collective-permute-start | bytes 368648 | tf_op jit(solution)/shard_map/ppermute | solution.py:257
  28.1 8.9 %collective-permute-start.1 = (bf16[160,384]{1,0:T(8,128)(2,1)S(1)}, bf16[160,384]{1,0:T(8,128)(2,1)S(1)}, u32[]{:S(2)}, u32[]{:S(2)}) collective-permute-start(bf16[160,384]{1,0:T(8,128)(2,1)S(1)} %maximum_maximum_fusion), channel_id=1, source_target_pairs={{0,18},{1,19},{2,16},{3,17},{4,22},{5,23},{6,20},{7,21},{8,26},{9,... | collective-permute-start | bytes 368648 | tf_op jit(solution)/shard_map/ppermute | solution.py:257
  30.2 9.6 %collective-permute-start = (bf16[160,384]{1,0:T(8,128)(2,1)S(1)}, bf16[160,384]{1,0:T(8,128)(2,1)S(1)}, u32[]{:S(2)}, u32[]{:S(2)}) collective-permute-start(bf16[160,384]{1,0:T(8,128)(2,1)S(1)} %maximum_maximum_fusion), channel_id=1, source_target_pairs={{0,16},{1,17},{2,18},{3,19},{4,20},{5,21},{6,22},{7,23},{8,24},{9,... | collective-permute-start | bytes 368648 | tf_op jit(solution)/shard_map/ppermute | solution.py:257
  70.5 8.7 %collective-permute-start.4 = (bf16[4,4,160,384]{3,2,1,0:T(8,128)(2,1)S(1)}, bf16[4,4,160,384]{3,2,1,0:T(8,128)(2,1)}, u32[]{:S(2)}, u32[]{:S(2)}) collective-permute-start(bf16[4,4,160,384]{3,2,1,0:T(8,128)(2,1)S(1)} %all_to_all.15.acts_ref.near_ref), channel_id=1, source_target_pairs={{0,1},{1,0},{2,3},{3,2},{4,5},{5,4},{6,7},{7,6},{8,9},{9,8},{10,11... | collective-permute-start | bytes 5898248 | tf_op jit(solution)/shard_map/ppermute | solution.py:260
  75.1 2.1 %copy-start = (bf16[16,160,768]{2,1,0:T(8,128)(2,1)S(1)}, bf16[16,160,768]{2,1,0:T(8,128)(2,1)}, u32[]{:S(2)}) copy-start(bf16[16,160,768]{2,1,0:T(8,128)(2,1)} %all-gather.3.cloned.1.call-done) | copy-start | bytes 11796484
  77.2 2.1 %copy-start.1 = (bf16[16,160,768]{2,1,0:T(8,128)(2,1)S(1)}, bf16[16,160,768]{2,1,0:T(8,128)(2,1)}, u32[]{:S(2)}) copy-start(bf16[16,160,768]{2,1,0:T(8,128)(2,1)} %all-gather.3.cloned.1.call-done) | copy-start | bytes 11796484
  81.9 16.8 %collective-permute-start.5 = (bf16[2,192,512]{2,1,0:T(8,128)(2,1)S(1)}, bf16[2,192,512]{2,1,0:T(8,128)(2,1)S(1)}, u32[]{:S(2)}, u32[]{:S(2)}) collective-permute-start(bf16[2,192,512]{2,1,0:T(8,128)(2,1)S(1)} %get-tuple-element.18), channel_id=1, source_target_pairs={{0,256},{32,288},{64,320},{96,352},{128,384},{160,416},{192,448},{... | collective-permute-start | bytes 1179656 | tf_op jit(solution)/shard_map/ppermute | solution.py:272
  87.8 17.1 %collective-permute-start.6 = (bf16[2,192,256]{2,1,0:T(8,128)(2,1)}, bf16[2,192,256]{2,1,0:T(8,128)(2,1)}, u32[]{:S(2)}, u32[]{:S(2)}) collective-permute-start(bf16[2,192,256]{2,1,0:T(8,128)(2,1)} %get-tuple-element.23), channel_id=1, source_target_pairs={{0,256},{32,288},{64,320},{96,352},{128,384},{160,416},{192,448},{... | collective-permute-start | bytes 589832 | tf_op jit(solution)/shard_map/ppermute | solution.py:277
  101.5 1.1 copy-start.3
  102.6 2.1 %copy-start.2 = (bf16[16,160,768]{2,1,0:T(8,128)(2,1)S(1)}, bf16[16,160,768]{2,1,0:T(8,128)(2,1)}, u32[]{:S(2)}) copy-start(bf16[16,160,768]{2,1,0:T(8,128)(2,1)} %all-gather.3.cloned.1.call-done) | copy-start | bytes 11796484
  107.2 5.5 %collective-permute-start.7 = (bf16[4,48,2560]{2,1,0:T(8,128)(2,1)S(1)}, bf16[4,48,2560]{2,1,0:T(8,128)(2,1)S(1)}, u32[]{:S(2)}, u32[]{:S(2)}) collective-permute-start(bf16[4,48,2560]{2,1,0:T(8,128)(2,1)S(1)} %input_send.1), channel_id=1, source_target_pairs={{0,1},{1,0},{2,3},{3,2},{4,5},{5,4},{6,7},{7,6},{8,9},{9,8},{10,11... | collective-permute-start | bytes 2949128 | tf_op jit(solution)/shard_map/ppermute | solution.py:291
  129.6 26.0 %copy-start.4 = (f32[320,256]{1,0:T(8,128)S(1)}, f32[320,256]{1,0:T(8,128)}, u32[]{:S(2)}) copy-start(f32[320,256]{1,0:T(8,128)} %get-tuple-element.27) | copy-start | bytes 983044
Sparse Core Ops, SparseCore 0:
  10.2 60.1 all-gather.2
  102.7 46.0 reduce-scatter.1

commit v5 on v4

--- a/solution.py
+++ b/solution.py
@@ -1,4 +1,3 @@
-import functools
 import math
 
 import jax
@@ -62,57 +61,115 @@
     return jnp.where((packed & 1) != 0, -value, value)
 
 
-def decode_kernel(gate_ref, up_ref, down_ref, out_ref, down_w_ref, codes, sems):
-    copies = [
-        pltpu.make_async_copy(ref, codes.at[i], sems.at[i]) for i, ref in enumerate((gate_ref, up_ref, down_ref))
-    ]
+def decode_kernel(gate_ref, up_ref, down_ref, out_ref, codes, values, in_sems, out_sems):
+    pieces = [(i, core) for i in range(3) for core in range(2)]
+    reads, writes = [], []
+    for n, (i, core) in enumerate(pieces):
+        ref = (gate_ref, up_ref, down_ref)[i].at[core * FEAT : (core + 1) * FEAT]
+        reads.append(pltpu.make_async_copy(ref, codes.at[n], in_sems.at[n]))
+        writes.append(
+            pltpu.make_async_copy(values.at[n], out_ref.at[core, :, i * COLS : (i + 1) * COLS], out_sems.at[n])
+        )
+        reads[n].start()
+    for n, (i, core) in enumerate(pieces):
+        reads[n].wait()
+        values[n] = decode(codes[n], (D, D, FF_W)[i]).astype(jnp.bfloat16)
+        writes[n].start()
+    for write in writes:
+        write.wait()
+
+
+def decode_down_kernel(codes_ref, out_ref):
+    out_ref[...] = decode(codes_ref[...], FF_W)
+
+
+def fetch(w_ref, which, cols, w, sems):
+    copies = [pltpu.make_async_copy(w_ref.at[y, which, :, cols], w.at[y], sems.at[y]) for y in range(N_Y)]
     for copy in copies:
         copy.start()
-    for i, fan in enumerate((D, D, FF_W)):
-        copies[i].wait()
-        value = decode(codes[i], fan)
-        out_ref[:, :, i * COLS : (i + 1) * COLS] = value.astype(jnp.bfloat16).reshape(2, FEAT, COLS)
-    down_w_ref[...] = value
-
-
-def forward(acts_ref, which, my_zl, w_ref, kind):
-    cols = (slice(0, 2 * COLS), slice(2 * COLS, 3 * COLS))[kind]
+    return copies
+
+
+def fetch_acts(acts_ref, kind, acts, sems):
+    rows = slice(kind * HALF_FEAT, (kind + 1) * HALF_FEAT)
+    copies = [pltpu.make_async_copy(acts_ref.at[x, :, rows], acts.at[x], sems.at[x]) for x in range(N_X)]
+    for copy in copies:
+        copy.start()
+    return copies
+
+
+def block(acts_ref, x, my_zl, row):
+    return jnp.concatenate([acts_ref[x, zl ^ my_zl, row : row + HALF_FEAT] for zl in range(N_ZL)], axis=0)
+
+
+def forward(acts_ref, my_zl, row, w, ready):
     sums = [None, None]
     for x0 in range(2):
-        rows = slice(kind * HALF_FEAT, (kind + 1) * HALF_FEAT)
-        acts = []
-        for h in range(2):
-            part = jnp.concatenate([acts_ref[2 - 2 * h + x0, zl ^ my_zl, rows] for zl in range(N_ZL)], axis=0)
-            acts.append(part.T)
+        ready(x0)
+        acts = [block(acts_ref, 2 - 2 * h + x0, my_zl, row).T for h in range(2)]
         for half in range(2):
             rows = slice(half * HALF_FEAT, (half + 1) * HALF_FEAT)
-            w = [w_ref[x0 * N_ZL + zl, which, rows, cols] for zl in range(N_ZL)]
-            w = jnp.concatenate(w, axis=0)
+            weights = jnp.concatenate([w(x0 * N_ZL + zl, rows) for zl in range(N_ZL)], axis=0)
             for h in range(2):
                 part = acts[h][half * TOK : (half + 1) * TOK]
-                part = lax.dot_general(part, w, NN, preferred_element_type=jnp.float32)
+                part = lax.dot_general(part, weights, NN, preferred_element_type=jnp.float32)
                 sums[h] = part if sums[h] is None else sums[h] + part
     return sums
 
 
-def near_kernel(pos_ref, acts_ref, w_ref, gate_up_ref, hidden_grad_ref):
-    for kind, out_ref in enumerate((gate_up_ref, hidden_grad_ref)):
-        for h, total in enumerate(forward(acts_ref, pos_ref[1], pos_ref[3], w_ref, kind)):
-            out_ref[h] = total
-
-
-def far_kernel(kind, pos_ref, acts_ref, w_ref, near_ref, own_ref, send_ref):
-    for h, total in enumerate(forward(acts_ref, 1 - pos_ref[1], pos_ref[3], w_ref, kind)):
+GATE_UP, HIDDEN_GRAD = slice(0, 2 * COLS), slice(2 * COLS, 3 * COLS)
+
+
+def near_kernel(pos_ref, acts_ref, w_ref, out_ref, w_far_ref, w, sems):
+    core = pos_ref[1]
+    copies = fetch(w_ref, core, GATE_UP, w, sems.at[0])
+    others = fetch(w_ref, 1 - core, GATE_UP, w_far_ref, sems.at[1])
+
+    def ready(x0):
+        for copy in copies[x0 * N_ZL : (x0 + 1) * N_ZL]:
+            copy.wait()
+
+    for h, total in enumerate(forward(acts_ref, pos_ref[3], 0, lambda y, rows: w[y, rows], ready)):
+        out_ref[h] = total
+    for copy in others:
+        copy.wait()
+
+
+def gate_up_kernel(pos_ref, acts_ref, near_ref, w_far_ref, own_ref, send_ref, acts, sems):
+    copies = fetch_acts(acts_ref, 0, acts, sems)
+
+    def ready(x0):
+        copies[x0].wait()
+        copies[2 + x0].wait()
+
+    for h, total in enumerate(forward(acts, pos_ref[3], 0, lambda y, rows: w_far_ref[y, rows], ready)):
         total += near_ref[h]
         own_ref[h] = total
         send_ref[h] = total.astype(jnp.bfloat16)
 
 
+def hidden_grad_kernel(pos_ref, near_ref, far_ref, w_ref, own_ref, send_ref, grads_ref, acts, sems):
+    core, my_zl = pos_ref[1], pos_ref[3]
+    copies = fetch_acts(far_ref, 1, acts, sems)
+    totals = forward(near_ref, my_zl, HALF_FEAT, lambda y, rows: w_ref[y, core, rows, HIDDEN_GRAD], lambda x0: None)
+    for copy in copies:
+        copy.wait()
+    far = forward(acts, my_zl, 0, lambda y, rows: w_ref[y, 1 - core, rows, HIDDEN_GRAD], lambda x0: None)
+    for h in range(2):
+        total = totals[h] + far[h]
+        own_ref[h] = total
+        send_ref[h] = total.astype(jnp.bfloat16)
+    for side, (ref, row) in enumerate(((near_ref, HALF_FEAT), (acts, 0))):
+        for x0 in range(2):
+            for h in range(2):
+                grads_ref[side, x0, :, h * 2 * TOK : (h + 1) * 2 * TOK] = block(ref, 2 - 2 * h + x0, my_zl, row)
+
+
 def copy_kernel(w_ref, out_ref):
     out_ref[...] = w_ref[:, :, :, : 2 * COLS]
 
 
-def down_kernel(pos_ref, near_ref, far_ref, own_ref, got_ref, out_ref):
+def down_kernel(pos_ref, grads_ref, own_ref, got_ref, out_ref):
     core = pos_ref[1]
     blank = jnp.zeros((TOK, COLS), jnp.bfloat16)
     rows = []
@@ -123,11 +180,8 @@
         rows += [jnp.concatenate([hidden, blank], axis=1), jnp.concatenate([blank, hidden], axis=1)]
     hidden = jnp.concatenate(rows, axis=0)
     for x0 in range(2):
-        for ref, which in ((near_ref, core), (far_ref, 1 - core)):
-            grads = [
-                jnp.concatenate([ref[2 - 2 * h + x0, zl ^ pos_ref[3], HALF_FEAT:] for zl in range(N_ZL)], axis=0) for h in range(2)
-            ]
-            acts = jnp.concatenate(grads, axis=1)
+        for side, which in ((0, core), (1, 1 - core)):
+            acts = grads_ref[side, x0]
             part = lax.dot_general(acts, hidden, NN, preferred_element_type=jnp.float32).astype(jnp.bfloat16)
             for zl in range(N_ZL):
                 rows = part[zl * HALF_FEAT : (zl + 1) * HALF_FEAT]
@@ -215,7 +269,7 @@
 HBM = pl.BlockSpec(memory_space=pltpu.HBM)
 
 
-def call(kernel, out_shapes, *args, name, flops=0, scratch=(), hbm=(), limit=16):
+def call(kernel, out_shapes, *args, name, flops=0, scratch=(), hbm=(), limit=16, out_spec=VMEM):
     specs = [SMEM if a.dtype == jnp.int32 and a.ndim == 1 else HBM if i in hbm else VMEM for i, a in enumerate(args)]
     moved = 0
     if flops:
@@ -225,7 +279,7 @@
         kernel,
         out_shape=out_shapes,
         in_specs=specs,
-        out_specs=jax.tree.map(lambda _: VMEM, out_shapes),
+        out_specs=jax.tree.map(lambda _: out_spec, out_shapes),
         scratch_shapes=scratch,
         compiler_params=pltpu.CompilerParams(vmem_limit_bytes=limit * 2**20),
         cost_estimate=pl.CostEstimate(flops=flops, bytes_accessed=moved, transcendentals=0),
@@ -242,10 +296,14 @@
     pos = jnp.stack([dp // N_Y, tensor % 2, dp % N_Y, tensor // 2 % N_ZL]).astype(jnp.int32)
     wide, bf16, f32 = 3 * COLS, jnp.bfloat16, jnp.float32
 
-    w, down_w = call(
-        decode_kernel, (shaped((2, FEAT, wide)), shaped((ROWS, COLS), f32)), gate_codes, up_codes, down_codes,
+    w = call(
+        decode_kernel, shaped((2, FEAT, wide)), gate_codes, up_codes, down_codes,
         name="decode", flops=ROWS * COLS * 32,
-        scratch=[pltpu.VMEM((3, ROWS, COLS), jnp.int32), pltpu.SemaphoreType.DMA((3,))], hbm=(0, 1, 2), limit=60,
+        scratch=[
+            pltpu.VMEM((6, FEAT, COLS), jnp.int32), pltpu.VMEM((6, FEAT, COLS), bf16),
+            pltpu.SemaphoreType.DMA((6,)), pltpu.SemaphoreType.DMA((6,)),
+        ],
+        hbm=(0, 1, 2), limit=60, out_spec=HBM,
     )
     w = lax.all_gather(w, "dp", axis=0, axis_index_groups=Y_GROUPS)
 
@@ -261,29 +319,33 @@
 
     flops = HALF * COLS * 2 * TOK
     gate_up_shape, hidden_grad_shape = (2, TOK, 2 * COLS), (2, TOK, COLS)
-    gate_up, hidden_grad = call(
-        near_kernel, (shaped(gate_up_shape, f32), shaped(hidden_grad_shape, f32)), pos, near, w,
-        name="forward_near", flops=3 * flops,
+    w_shape = (N_Y, FEAT, 2 * COLS)
+    acts_space = [pltpu.VMEM((N_X, N_ZL, HALF_FEAT, 2 * TOK), bf16), pltpu.SemaphoreType.DMA((N_X,))]
+    gate_up, w_far = call(
+        near_kernel, (shaped(gate_up_shape, f32), shaped(w_shape)), pos, near, w, name="forward_near", flops=2 * flops,
+        hbm=(2,), limit=50, scratch=[pltpu.VMEM(w_shape, bf16), pltpu.SemaphoreType.DMA((2, N_Y))],
     )
     own, send = call(
-        functools.partial(far_kernel, 0), (shaped(gate_up_shape, f32), shaped(gate_up_shape)), pos, far, w, gate_up,
-        name="gate_up",
+        gate_up_kernel, (shaped(gate_up_shape, f32), shaped(gate_up_shape)), pos, far, gate_up, w_far, name="gate_up",
+        hbm=(1,), scratch=acts_space,
     )
     got = lax.ppermute(send, "dp", Z_SWAP)
-    own_hg, send = call(
-        functools.partial(far_kernel, 1), (shaped(hidden_grad_shape, f32), shaped(hidden_grad_shape)), pos, far, w,
-        hidden_grad, name="hidden_grad",
+    own_hg, send, grads = call(
+        hidden_grad_kernel,
+        (shaped(hidden_grad_shape, f32), shaped(hidden_grad_shape), shaped((2, 2, N_ZL * HALF_FEAT, 4 * TOK))),
+        pos, near, far, w, name="hidden_grad", hbm=(2,), scratch=acts_space,
     )
     got_hg = lax.ppermute(send, "dp", Z_SWAP)
-    w_own, _ = lax.optimization_barrier((w, own_hg))
+    w_own, codes, _ = lax.optimization_barrier((w, down_codes, own_hg))
+    down_w = call(decode_down_kernel, shaped((ROWS, COLS), f32), codes, name="decode_down", flops=ROWS * COLS * 32)
     w_gate_up = call(copy_kernel, shaped((N_Y, 2, FEAT, 2 * COLS)), w_own, name="copy", flops=flops)
 
     got, own_hg = lax.optimization_barrier((got, own_hg))
-    down = call(down_kernel, shaped((N_Y, 2, FEAT, COLS)), pos, near, far, own, got, name="down")
+    down = call(down_kernel, shaped((N_Y, 2, FEAT, COLS)), pos, grads, own, got, name="down")
     down_grad = lax.psum_scatter(
         down.reshape(N_Y * ROWS, COLS), "dp", scatter_dimension=0, axis_index_groups=Y_GROUPS, tiled=True
     )
-    down, got_hg, w_gate_up = lax.optimization_barrier((down, got_hg, w_gate_up))
+    down, got_hg, w_gate_up, down_w = lax.optimization_barrier((down, got_hg, w_gate_up, down_w))
 
     out = shaped((N_X, 48, HALF))
     grads = (own, got, own_hg, got_hg)

time: 166 us -> 164 us (0.988)
  local copies, waits for them, and re-layouts: 6.44 us -> 2.33 us
    unnamed x10, local copies, waits for them, and re-layouts: 5.39 us -> 2.12 us
    pallas_call x11 -> x12, Pallas kernels: 19.3 us -> 20.9 us  [call(): pl.pallas_call(kernel, out_shape=out_shapes, in_specs=specs, out_specs=ja...]
  transfers between devices with their start and end apart: 10 -> 10, of which waited for: 3 -> 5; matrix products, arithmetic and copies ran while one was open for 1% -> 0% of each run, Pallas kernels for 8% -> 9%
where the time goes in v5:
time: 164 us; the launch traced here: 161 us
  blocking collectives  71 us (43%)
  starting transfers between devices  39.8 us (24%)
  Pallas kernels  20.9 us (13%)
  between operations  14.3 us (9%)
  waiting for transfers between devices  11.2 us (7%)
  local copies, waits for them, and re-layouts  2.33 us (1%)
  other arithmetic  1.92 us (1%)
    all_to_all x1, blocking collectives, on_device(): lax.all_to_all(acts, 'tensor', 0, 0, axis_index_groups=X_GROUPS, tiled=True)  30.4 us
    all_to_all x1, blocking collectives, on_device(): lax.all_to_all(parts, ('dp', 'tensor'), 0, 0, axis_index_groups=Z_GROUPS,...  24.4 us
    ppermute x4, starting transfers between devices, on_device(): lax.ppermute(acts, ('dp', 'tensor'), turn)  22 us
    pallas_call x12, Pallas kernels, call(): pl.pallas_call(kernel, out_shape=out_shapes, in_specs=specs, out_specs=ja...  20.9 us
    all_to_all x1, blocking collectives, on_device(): lax.all_to_all(parts, 'tensor', 0, 0, axis_index_groups=X_GROUPS, tiled=T...  16.3 us
    ppermute x4, waiting for transfers between devices, on_device(): lax.ppermute(acts, ('dp', 'tensor'), turn)  6.74 us
    ppermute x1, starting transfers between devices, on_device(): got_hg = lax.ppermute(send, 'dp', Z_SWAP)  5.9 us
    ppermute x1, starting transfers between devices, on_device(): far = lax.ppermute(near, 'tensor', CORE_SWAP)  4.5 us
  transfers between devices with their start and end apart: 10, of which 5 were waited for; matrix products, arithmetic and copies ran while one was open for 0% of the time, Pallas kernels for 9%

profile of v5, /device:TPU:1, one launch (start us, length us, event | category | flops | bytes accessed | tf_op | source)
XLA Modules:
  0.0 161.5 jit_solution(16047733380928348877)
XLA Ops:
  7.2 0.0 copy-start.3
  7.2 0.0 copy-start.4
  7.2 0.0 all-gather.3.cloned.1.call-start
  7.2 2.6 %decode.1 = bf16[2,160,768]{2,1,0:T(8,128)(2,1)} custom-call(s32[320,256]{1,0:T(8,128)} %gate_ref.1, s32[320,256]{1,0:T(8,128)} %up_ref.1, s32[320,256]{1,0:T(8,128)} %codes_ref), custom_call_target="tpu_custom_call" | custom-call | flops 2621440 | bytes 1474560 | tf_op jit(solution)/shard_map/decode/pallas_call | solution.py:278
  9.9 0.0 all-gather.3.cloned.1.call-update
  9.9 0.0 reduce-scatter.2.cloned.1.call-start
  9.9 0.0 copy-done.3
  9.9 0.0 copy-done.4
  10.0 0.1 maximum_maximum_fusion
  10.1 10.9 %collective-permute-start.3 = (bf16[160,384]{1,0:T(8,128)(2,1)S(1)}, bf16[160,384]{1,0:T(8,128)(2,1)S(1)}, u32[]{:S(2)}, u32[]{:S(2)}) collective-permute-start(bf16[160,384]{1,0:T(8,128)(2,1)S(1)} %maximum_maximum_fusion), channel_id=1, source_target_pairs={{0,22},{1,23},{2,20},{3,21},{4,18},{5,19},{6,16},{7,17},{8,30},{9,... | collective-permute-start | bytes 368648 | tf_op jit(solution)/shard_map/ppermute | solution.py:315
  21.0 6.1 %collective-permute-start.2 = (bf16[160,384]{1,0:T(8,128)(2,1)S(1)}, bf16[160,384]{1,0:T(8,128)(2,1)S(1)}, u32[]{:S(2)}, u32[]{:S(2)}) collective-permute-start(bf16[160,384]{1,0:T(8,128)(2,1)S(1)} %maximum_maximum_fusion), channel_id=1, source_target_pairs={{0,20},{1,21},{2,22},{3,23},{4,16},{5,17},{6,18},{7,19},{8,28},{9,... | collective-permute-start | bytes 368648 | tf_op jit(solution)/shard_map/ppermute | solution.py:315
  27.1 2.1 %collective-permute-start.1 = (bf16[160,384]{1,0:T(8,128)(2,1)S(1)}, bf16[160,384]{1,0:T(8,128)(2,1)S(1)}, u32[]{:S(2)}, u32[]{:S(2)}) collective-permute-start(bf16[160,384]{1,0:T(8,128)(2,1)S(1)} %maximum_maximum_fusion), channel_id=1, source_target_pairs={{0,18},{1,19},{2,16},{3,17},{4,22},{5,23},{6,20},{7,21},{8,26},{9,... | collective-permute-start | bytes 368648 | tf_op jit(solution)/shard_map/ppermute | solution.py:315
  29.2 2.9 %collective-permute-start = (bf16[160,384]{1,0:T(8,128)(2,1)S(1)}, bf16[160,384]{1,0:T(8,128)(2,1)S(1)}, u32[]{:S(2)}, u32[]{:S(2)}) collective-permute-start(bf16[160,384]{1,0:T(8,128)(2,1)S(1)} %maximum_maximum_fusion), channel_id=1, source_target_pairs={{0,16},{1,17},{2,18},{3,19},{4,20},{5,21},{6,22},{7,23},{8,24},{9,... | collective-permute-start | bytes 368648 | tf_op jit(solution)/shard_map/ppermute | solution.py:315
  32.1 0.0 collective-permute-done.3
  32.1 0.0 collective-permute-done.2
  32.1 3.9 %collective-permute-done.1 = bf16[160,384]{1,0:T(8,128)(2,1)S(1)} collective-permute-done((bf16[160,384]{1,0:T(8,128)(2,1)S(1)}, bf16[160,384]{1,0:T(8,128)(2,1)S(1)}, u32[]{:S(2)}, u32[]{:S(2)}) %collective-permute-start.1) | collective-permute-done | bytes 122912 | tf_op jit(solution)/shard_map/ppermute | solution.py:315
  36.0 2.9 %collective-permute-done = bf16[160,384]{1,0:T(8,128)(2,1)S(1)} collective-permute-done((bf16[160,384]{1,0:T(8,128)(2,1)S(1)}, bf16[160,384]{1,0:T(8,128)(2,1)S(1)}, u32[]{:S(2)}, u32[]{:S(2)}) %collective-permute-start) | collective-permute-done | bytes 122912 | tf_op jit(solution)/shard_map/ppermute | solution.py:315
  38.9 0.1 pad_maximum_fusion
  38.9 0.2 broadcast_in_dim.2
  39.1 30.4 %all_to_all.15.acts_ref.near_ref = bf16[4,4,160,384]{3,2,1,0:T(8,128)(2,1)S(1)} all-to-all(bf16[4,4,160,384]{3,2,1,0:T(8,128)(2,1)S(1)} %broadcast_in_dim.2), channel_id=1, replica_groups={{0,8,16,24},{1,9,17,25},{2,10,18,26},{3,11,19,27},{4,12,20,28},{5,13,21..., dimensions={0} | all-to-all | bytes 3932160 | tf_op jit(solution)/shard_map/all_to_all | solution.py:317
  69.5 4.5 %collective-permute-start.4 = (bf16[4,4,160,384]{3,2,1,0:T(8,128)(2,1)S(1)}, bf16[4,4,160,384]{3,2,1,0:T(8,128)(2,1)}, u32[]{:S(2)}, u32[]{:S(2)}) collective-permute-start(bf16[4,4,160,384]{3,2,1,0:T(8,128)(2,1)S(1)} %all_to_all.15.acts_ref.near_ref), channel_id=1, source_target_pairs={{0,1},{1,0},{2,3},{3,2},{4,5},{5,4},{6,7},{7,6},{8,9},{9,8},{10,11... | collective-permute-start | bytes 5898248 | tf_op jit(solution)/shard_map/ppermute | solution.py:318
  74.1 0.1 pad_add_fusion.pos_ref
  74.1 3.0 %forward_near.1 = (f32[2,192,512]{2,1,0:T(8,128)S(1)}, bf16[8,160,512]{2,1,0:T(8,128)(2,1)S(1)}) custom-call(s32[4]{0:T(128)S(1)} %pad_add_fusion.pos_ref, bf16[4,4,160,384]{3,2,1,0:T(8,128)(2,1)S(1)} %all_to_all.15.acts_ref.near_ref, bf16[8,2,160,768]{3,2,1,0:T(8,128)(2,1)} %bitcast.13), custom_call_target="tpu_custom_call" | custom-call | flops 503316480 | bytes 7995408 | tf_op jit(solution)/shard_map/forward_near/pallas_call | solution.py:278
  77.1 0.6 collective-permute-done.4.acts_ref.far_ref
  77.7 3.1 %gate_up.1 = (f32[2,192,512]{2,1,0:T(8,128)S(1)}, bf16[2,192,512]{2,1,0:T(8,128)(2,1)S(1)}) custom-call(s32[4]{0:T(128)S(1)} %pad_add_fusion.pos_ref, bf16[4,4,160,384]{3,2,1,0:T(8,128)(2,1)} %collective-permute-done.4.acts_ref.far_ref, f32[2,192,512]{2,1,0:T(8,128)S(1)} %get-tuple-element.16.near_ref, bf16[8,160,512]{2,1,0:T(8,128)(2,1)S(1)} %get-tuple-element.17.w_far_ref), custom_call_target="tpu_custom_call" | custom-call | tf_op jit(solution)/shard_map/gate_up/pallas_call | solution.py:278
  80.9 3.3 %collective-permute-start.5 = (bf16[2,192,512]{2,1,0:T(8,128)(2,1)S(1)}, bf16[2,192,512]{2,1,0:T(8,128)(2,1)S(1)}, u32[]{:S(2)}, u32[]{:S(2)}) collective-permute-start(bf16[2,192,512]{2,1,0:T(8,128)(2,1)S(1)} %get-tuple-element.19), channel_id=1, source_target_pairs={{0,256},{32,288},{64,320},{96,352},{128,384},{160,416},{192,448},{... | collective-permute-start | bytes 1179656 | tf_op jit(solution)/shard_map/ppermute | solution.py:332
  84.2 0.0 copy-done
  84.2 3.6 %hidden_grad.1 = (f32[2,192,256]{2,1,0:T(8,128)S(1)}, bf16[2,192,256]{2,1,0:T(8,128)(2,1)}, bf16[2,2,320,768]{3,2,1,0:T(8,128)(2,1)S(1)}) custom-call(s32[4]{0:T(128)S(1)} %pad_add_fusion.pos_ref, bf16[4,4,160,384]{3,2,1,0:T(8,128)(2,1)S(1)} %all_to_all.15.acts_ref.near_ref, bf16[4,4,160,384]{3,2,1,0:T(8,128)(2,1)} %collective-permute-done.4.acts_ref.far_ref, ...), custom_call_target="tpu_custom_call" | custom-call | tf_op jit(solution)/shard_map/hidden_grad/pallas_call | solution.py:278
  87.8 5.9 %collective-permute-start.6 = (bf16[2,192,256]{2,1,0:T(8,128)(2,1)}, bf16[2,192,256]{2,1,0:T(8,128)(2,1)S(1)}, u32[]{:S(2)}, u32[]{:S(2)}) collective-permute-start(bf16[2,192,256]{2,1,0:T(8,128)(2,1)} %get-tuple-element.24), channel_id=1, source_target_pairs={{0,256},{32,288},{64,320},{96,352},{128,384},{160,416},{192,448},{... | collective-permute-start | bytes 589832 | tf_op jit(solution)/shard_map/ppermute | solution.py:338
  93.7 3.5 %collective-permute-done.5.got_ref.refs_1_ = bf16[2,192,512]{2,1,0:T(8,128)(2,1)S(1)} collective-permute-done((bf16[2,192,512]{2,1,0:T(8,128)(2,1)S(1)}, bf16[2,192,512]{2,1,0:T(8,128)(2,1)S(1)}, u32[]{:S(2)}, u32[]{:S(2)}) %collective-permute-start.5) | collective-permute-done | bytes 393248 | tf_op jit(solution)/shard_map/ppermute | solution.py:332
  97.2 2.8 %down.1 = bf16[8,2,160,256]{3,2,1,0:T(8,128)(2,1)} custom-call(s32[4]{0:T(128)S(1)} %pad_add_fusion.pos_ref, bf16[2,2,320,768]{3,2,1,0:T(8,128)(2,1)S(1)} %get-tuple-element.23.grads_ref, f32[2,192,512]{2,1,0:T(8,128)S(1)} %get-tuple-element.18.own_ref.refs_0_, bf16[2,192,512]{2,1,0:T(8,128)(2,1)S(1)} %collective-permute-done.5.got_ref.refs_1_), custom_call_target="tpu_custom_call" | custom-call | tf_op jit(solution)/shard_map/down/pallas_call | solution.py:278
  100.1 0.0 reduce-scatter.2.cloned.1.call-update
  100.1 0.0 copy-done.2
  100.1 0.3 decode_down.1
  100.4 0.0 copy-start.1
  100.4 2.1 %copy-done.1 = bf16[16,160,768]{2,1,0:T(8,128)(2,1)S(1)} copy-done((bf16[16,160,768]{2,1,0:T(8,128)(2,1)S(1)}, bf16[16,160,768]{2,1,0:T(8,128)(2,1)}, u32[]{:S(2)}) %copy-start.1) | copy-done | bytes 3932184
  102.5 0.2 copy.8.refs_4_
  102.7 0.0 collective-permute-done.6.refs_3_
  102.7 1.9 %input_send.1 = bf16[4,48,2560]{2,1,0:T(8,128)(2,1)S(1)} custom-call(s32[4]{0:T(128)S(1)} %pad_add_fusion.pos_ref, f32[2,192,512]{2,1,0:T(8,128)S(1)} %get-tuple-element.18.own_ref.refs_0_, bf16[2,192,512]{2,1,0:T(8,128)(2,1)S(1)} %collective-permute-done.5.got_ref.refs_1_, f32[2,192,256]{2,1,0:T(8,128)S(1)} %get-tuple-element.22.refs_2_, ...), custom_call_target="tpu_custom_call" | custom-call | flops 251658240 | bytes 5373968 | tf_op jit(solution)/shard_map/input_send/pallas_call | solution.py:278
  104.6 4.0 %collective-permute-start.7 = (bf16[4,48,2560]{2,1,0:T(8,128)(2,1)S(1)}, bf16[4,48,2560]{2,1,0:T(8,128)(2,1)S(1)}, u32[]{:S(2)}, u32[]{:S(2)}) collective-permute-start(bf16[4,48,2560]{2,1,0:T(8,128)(2,1)S(1)} %input_send.1), channel_id=1, source_target_pairs={{0,1},{1,0},{2,3},{3,2},{4,5},{5,4},{6,7},{7,6},{8,9},{9,8},{10,11... | collective-permute-start | bytes 2949128 | tf_op jit(solution)/shard_map/ppermute | solution.py:353
  108.6 1.9 %input_keep.1.a_ref = bf16[4,48,2560]{2,1,0:T(8,128)(2,1)S(1)} custom-call(s32[4]{0:T(128)S(1)} %pad_add_fusion.pos_ref, f32[2,192,512]{2,1,0:T(8,128)S(1)} %get-tuple-element.18.own_ref.refs_0_, bf16[2,192,512]{2,1,0:T(8,128)(2,1)S(1)} %collective-permute-done.5.got_ref.refs_1_, f32[2,192,256]{2,1,0:T(8,128)S(1)} %get-tuple-element.22.refs_2_, ...), custom_call_target="tpu_custom_call" | custom-call | flops 251658240 | bytes 5373968 | tf_op jit(solution)/shard_map/input_keep/pallas_call | solution.py:278
  110.5 0.2 collective-permute-done.7.b_ref
  110.8 0.2 add.25
  111.0 16.3 %all_to_all.16.parts_ref = bf16[4,48,2560]{2,1,0:T(8,128)(2,1)S(1)} all-to-all(bf16[4,48,2560]{2,1,0:T(8,128)(2,1)S(1)} %add.25), channel_id=1, replica_groups={{0,8,16,24},{1,9,17,25},{2,10,18,26},{3,11,19,27},{4,12,20,28},{5,13,21..., dimensions={0} | all-to-all | bytes 1966080 | tf_op jit(solution)/shard_map/all_to_all | solution.py:356
  127.3 0.4 x_sum.1
  127.7 24.4 %all_to_all.17.parts_ref = bf16[8,24,640]{2,1,0:T(8,128)(2,1)S(1)} all-to-all(bf16[8,24,640]{2,1,0:T(8,128)(2,1)S(1)} %bitcast.16), channel_id=1, replica_groups={{0,2,4,6,256,258,260,262},{1,3,5,7,257,259,261,263},{8,10,12,14,264,266..., dimensions={0} | all-to-all | bytes 491520 | tf_op jit(solution)/shard_map/all_to_all | solution.py:358
  152.1 0.8 input_sum.1
  153.0 1.7 %convert_multiply_fusion = f32[320,256]{1,0:T(8,128)} fusion(f32[320,256]{1,0:T(8,128)S(1)} %decode_down.1, bf16[320,256]{1,0:T(8,128)(2,1)} %reduce-scatter.2.cloned.1.call-done), kind=kLoop, calls=%fused_computation.1 | loop fusion | flops 163840 | bytes 819200 | tf_op jit(solution)/shard_map/mul | solution.py:360
  (5 shorter events, 0.0 us)
Async XLA Ops:
  7.2 2.8 %copy-start.3 = (bf16[192,160]{0,1:T(8,128)(2,1)S(1)}, bf16[192,160]{0,1:T(8,128)(2,1)}, u32[]{:S(2)}) copy-start(bf16[192,160]{0,1:T(8,128)(2,1)} %param.5) | copy-start | bytes 184324
  7.2 2.8 %copy-start.4 = (bf16[192,160]{0,1:T(8,128)(2,1)S(1)}, bf16[192,160]{0,1:T(8,128)(2,1)}, u32[]{:S(2)}) copy-start(bf16[192,160]{0,1:T(8,128)(2,1)} %param.6) | copy-start | bytes 184324
  7.2 67.0 %all-gather.3.cloned.1.call-start = ((), (), s32[]{:S(2)}) async-start(), calls=%async_computation.5 | async-start | bytes 4423680 | tf_op jit(solution)/shard_map/all_gather | solution.py:308
  9.9 143.1 %reduce-scatter.2.cloned.1.call-start = ((), (), s32[]{:S(2)}) async-start(), calls=%async_computation.4 | async-start | bytes 1474560 | tf_op jit(solution)/shard_map/reduce_scatter | solution.py:345
  10.1 22.0 %collective-permute-start.3 = (bf16[160,384]{1,0:T(8,128)(2,1)S(1)}, bf16[160,384]{1,0:T(8,128)(2,1)S(1)}, u32[]{:S(2)}, u32[]{:S(2)}) collective-permute-start(bf16[160,384]{1,0:T(8,128)(2,1)S(1)} %maximum_maximum_fusion), channel_id=1, source_target_pairs={{0,22},{1,23},{2,20},{3,21},{4,18},{5,19},{6,16},{7,17},{8,30},{9,... | collective-permute-start | bytes 368648 | tf_op jit(solution)/shard_map/ppermute | solution.py:315
  21.0 11.1 %collective-permute-start.2 = (bf16[160,384]{1,0:T(8,128)(2,1)S(1)}, bf16[160,384]{1,0:T(8,128)(2,1)S(1)}, u32[]{:S(2)}, u32[]{:S(2)}) collective-permute-start(bf16[160,384]{1,0:T(8,128)(2,1)S(1)} %maximum_maximum_fusion), channel_id=1, source_target_pairs={{0,20},{1,21},{2,22},{3,23},{4,16},{5,17},{6,18},{7,19},{8,28},{9,... | collective-permute-start | bytes 368648 | tf_op jit(solution)/shard_map/ppermute | solution.py:315
  27.1 8.9 %collective-permute-start.1 = (bf16[160,384]{1,0:T(8,128)(2,1)S(1)}, bf16[160,384]{1,0:T(8,128)(2,1)S(1)}, u32[]{:S(2)}, u32[]{:S(2)}) collective-permute-start(bf16[160,384]{1,0:T(8,128)(2,1)S(1)} %maximum_maximum_fusion), channel_id=1, source_target_pairs={{0,18},{1,19},{2,16},{3,17},{4,22},{5,23},{6,20},{7,21},{8,26},{9,... | collective-permute-start | bytes 368648 | tf_op jit(solution)/shard_map/ppermute | solution.py:315
  29.2 9.6 %collective-permute-start = (bf16[160,384]{1,0:T(8,128)(2,1)S(1)}, bf16[160,384]{1,0:T(8,128)(2,1)S(1)}, u32[]{:S(2)}, u32[]{:S(2)}) collective-permute-start(bf16[160,384]{1,0:T(8,128)(2,1)S(1)} %maximum_maximum_fusion), channel_id=1, source_target_pairs={{0,16},{1,17},{2,18},{3,19},{4,20},{5,21},{6,22},{7,23},{8,24},{9,... | collective-permute-start | bytes 368648 | tf_op jit(solution)/shard_map/ppermute | solution.py:315
  69.5 8.2 %collective-permute-start.4 = (bf16[4,4,160,384]{3,2,1,0:T(8,128)(2,1)S(1)}, bf16[4,4,160,384]{3,2,1,0:T(8,128)(2,1)}, u32[]{:S(2)}, u32[]{:S(2)}) collective-permute-start(bf16[4,4,160,384]{3,2,1,0:T(8,128)(2,1)S(1)} %all_to_all.15.acts_ref.near_ref), channel_id=1, source_target_pairs={{0,1},{1,0},{2,3},{3,2},{4,5},{5,4},{6,7},{7,6},{8,9},{9,8},{10,11... | collective-permute-start | bytes 5898248 | tf_op jit(solution)/shard_map/ppermute | solution.py:318
  77.7 6.5 %copy-start = (bf16[16,160,768]{2,1,0:T(8,128)(2,1)S(1)}, bf16[16,160,768]{2,1,0:T(8,128)(2,1)}, u32[]{:S(2)}) copy-start(bf16[16,160,768]{2,1,0:T(8,128)(2,1)} %all-gather.3.cloned.1.call-done) | copy-start | bytes 11796484
  80.9 16.4 %collective-permute-start.5 = (bf16[2,192,512]{2,1,0:T(8,128)(2,1)S(1)}, bf16[2,192,512]{2,1,0:T(8,128)(2,1)S(1)}, u32[]{:S(2)}, u32[]{:S(2)}) collective-permute-start(bf16[2,192,512]{2,1,0:T(8,128)(2,1)S(1)} %get-tuple-element.19), channel_id=1, source_target_pairs={{0,256},{32,288},{64,320},{96,352},{128,384},{160,416},{192,448},{... | collective-permute-start | bytes 1179656 | tf_op jit(solution)/shard_map/ppermute | solution.py:332
  87.8 14.9 %collective-permute-start.6 = (bf16[2,192,256]{2,1,0:T(8,128)(2,1)}, bf16[2,192,256]{2,1,0:T(8,128)(2,1)S(1)}, u32[]{:S(2)}, u32[]{:S(2)}) collective-permute-start(bf16[2,192,256]{2,1,0:T(8,128)(2,1)} %get-tuple-element.24), channel_id=1, source_target_pairs={{0,256},{32,288},{64,320},{96,352},{128,384},{160,416},{192,448},{... | collective-permute-start | bytes 589832 | tf_op jit(solution)/shard_map/ppermute | solution.py:338
  97.2 2.8 %copy-start.2 = (s32[320,256]{1,0:T(8,128)S(1)}, s32[320,256]{1,0:T(8,128)}, u32[]{:S(2)}) copy-start(s32[320,256]{1,0:T(8,128)} %codes_ref) | copy-start | bytes 983044
  100.4 2.1 %copy-start.1 = (bf16[16,160,768]{2,1,0:T(8,128)(2,1)S(1)}, bf16[16,160,768]{2,1,0:T(8,128)(2,1)}, u32[]{:S(2)}) copy-start(bf16[16,160,768]{2,1,0:T(8,128)(2,1)} %all-gather.3.cloned.1.call-done) | copy-start | bytes 11796484
  104.6 6.2 %collective-permute-start.7 = (bf16[4,48,2560]{2,1,0:T(8,128)(2,1)S(1)}, bf16[4,48,2560]{2,1,0:T(8,128)(2,1)S(1)}, u32[]{:S(2)}, u32[]{:S(2)}) collective-permute-start(bf16[4,48,2560]{2,1,0:T(8,128)(2,1)S(1)} %input_send.1), channel_id=1, source_target_pairs={{0,1},{1,0},{2,3},{3,2},{4,5},{5,4},{6,7},{7,6},{8,9},{9,8},{10,11... | collective-permute-start | bytes 2949128 | tf_op jit(solution)/shard_map/ppermute | solution.py:353
Sparse Core Ops, SparseCore 0:
  10.1 60.1 all-gather.2
  100.2 46.9 reduce-scatter.1

commit v6 on v5

--- a/solution.py
+++ b/solution.py
@@ -52,13 +52,11 @@
 
 
 def decode(packed, fan):
-    frac = ((packed >> 1) & 7).astype(jnp.float32) * 0.125
-    power = jnp.where((packed & 16) != 0, 0.5, 1.0)
-    power = power * jnp.where((packed & 32) != 0, 0.25, 1.0)
-    power = power * jnp.where((packed & 64) != 0, 0.0625, 1.0)
-    poly = 1.0 - frac * (coef_one - frac * (coef_two - coef_three * frac))
-    value = power * poly * (3.0 / math.sqrt(fan))
-    return jnp.where((packed & 1) != 0, -value, value)
+    frac = (packed & 14).astype(jnp.float32)
+    poly = 1.0 - frac * (coef_one / 16 - frac * (coef_two / 256 - coef_three / 4096 * frac))
+    power = lax.shift_right_logical(jnp.full_like(packed, 128), packed >> 4)
+    power = jnp.where((packed & 1) != 0, -power, power).astype(jnp.float32)
+    return power * (3.0 / math.sqrt(fan) / 128) * poly
 
 
 def decode_kernel(gate_ref, up_ref, down_ref, out_ref, codes, values, in_sems, out_sems):
@@ -102,11 +100,14 @@
     return jnp.concatenate([acts_ref[x, zl ^ my_zl, row : row + HALF_FEAT] for zl in range(N_ZL)], axis=0)
 
 
-def forward(acts_ref, my_zl, row, w, ready):
+def forward(acts_ref, my_zl, row, w, acts_ready=None, w_ready=None):
     sums = [None, None]
     for x0 in range(2):
-        ready(x0)
+        if acts_ready is not None:
+            acts_ready(x0)
         acts = [block(acts_ref, 2 - 2 * h + x0, my_zl, row).T for h in range(2)]
+        if w_ready is not None:
+            w_ready(x0)
         for half in range(2):
             rows = slice(half * HALF_FEAT, (half + 1) * HALF_FEAT)
             weights = jnp.concatenate([w(x0 * N_ZL + zl, rows) for zl in range(N_ZL)], axis=0)
@@ -129,7 +130,7 @@
         for copy in copies[x0 * N_ZL : (x0 + 1) * N_ZL]:
             copy.wait()
 
-    for h, total in enumerate(forward(acts_ref, pos_ref[3], 0, lambda y, rows: w[y, rows], ready)):
+    for h, total in enumerate(forward(acts_ref, pos_ref[3], 0, lambda y, rows: w[y, rows], w_ready=ready)):
         out_ref[h] = total
     for copy in others:
         copy.wait()
@@ -142,7 +143,7 @@
         copies[x0].wait()
         copies[2 + x0].wait()
 
-    for h, total in enumerate(forward(acts, pos_ref[3], 0, lambda y, rows: w_far_ref[y, rows], ready)):
+    for h, total in enumerate(forward(acts, pos_ref[3], 0, lambda y, rows: w_far_ref[y, rows], acts_ready=ready)):
         total += near_ref[h]
         own_ref[h] = total
         send_ref[h] = total.astype(jnp.bfloat16)
@@ -151,10 +152,10 @@
 def hidden_grad_kernel(pos_ref, near_ref, far_ref, w_ref, own_ref, send_ref, grads_ref, acts, sems):
     core, my_zl = pos_ref[1], pos_ref[3]
     copies = fetch_acts(far_ref, 1, acts, sems)
-    totals = forward(near_ref, my_zl, HALF_FEAT, lambda y, rows: w_ref[y, core, rows, HIDDEN_GRAD], lambda x0: None)
+    totals = forward(near_ref, my_zl, HALF_FEAT, lambda y, rows: w_ref[y, core, rows, HIDDEN_GRAD])
     for copy in copies:
         copy.wait()
-    far = forward(acts, my_zl, 0, lambda y, rows: w_ref[y, 1 - core, rows, HIDDEN_GRAD], lambda x0: None)
+    far = forward(acts, my_zl, 0, lambda y, rows: w_ref[y, 1 - core, rows, HIDDEN_GRAD])
     for h in range(2):
         total = totals[h] + far[h]
         own_ref[h] = total
@@ -189,7 +190,7 @@
                 out_ref[x0 * N_ZL + zl, which, HALF_FEAT:] = rows[:, COLS:]
 
 
-def input_part(pos_ref, own_ref, got_ref, own_hg_ref, got_hg_ref, w_ref, out_ref, side):
+def input_part(grads, w_ref, out_ref, side):
     rows = N_X * 48
     row = lax.broadcasted_iota(jnp.int32, (rows, 2 * TOK), 0)
     col = lax.broadcasted_iota(jnp.int32, (rows, 2 * TOK), 1)
@@ -200,6 +201,15 @@
     zl = (left * 10923) >> 16
     wanted = h * TOK + x * 48 + zl * 12 + side * 6 + left - 6 * zl
     pick = jnp.where(wanted == col, 1.0, 0.0).astype(jnp.bfloat16)
+    grads = lax.dot_general(pick, grads, NN, preferred_element_type=jnp.float32).astype(jnp.bfloat16)
+    for q in range(4):
+        pair = w_ref[2 * q : 2 * q + 2].reshape(2 * ROWS, 2 * COLS)
+        part = lax.dot_general(grads, pair, NT, preferred_element_type=jnp.float32)
+        at = slice(q * 2 * ROWS, (q + 1) * 2 * ROWS)
+        out_ref[:, :, at] = part.astype(jnp.bfloat16).reshape(N_X, 48, 2 * ROWS)
+
+
+def input_send_kernel(pos_ref, own_ref, got_ref, own_hg_ref, got_hg_ref, w_ref, out_ref, grads_ref):
     grads = []
     for h in range(2):
         total = own_ref[h] + got_ref[h].astype(jnp.float32)
@@ -210,20 +220,12 @@
         up_grad = (hidden_grad * gate * sig).astype(jnp.bfloat16)
         grads.append(jnp.concatenate([gate_grad, up_grad], axis=1))
     grads = jnp.concatenate(grads, axis=0)
-    grads = lax.dot_general(pick, grads, NN, preferred_element_type=jnp.float32).astype(jnp.bfloat16)
-    for q in range(4):
-        pair = w_ref[2 * q : 2 * q + 2].reshape(2 * ROWS, 2 * COLS)
-        part = lax.dot_general(grads, pair, NT, preferred_element_type=jnp.float32)
-        at = slice(q * 2 * ROWS, (q + 1) * 2 * ROWS)
-        out_ref[:, :, at] = part.astype(jnp.bfloat16).reshape(N_X, 48, 2 * ROWS)
-
-
-def input_send_kernel(pos_ref, *refs):
-    input_part(pos_ref, *refs, 1 - pos_ref[1])
-
-
-def input_keep_kernel(pos_ref, *refs):
-    input_part(pos_ref, *refs, pos_ref[1])
+    grads_ref[...] = grads
+    input_part(grads, w_ref, out_ref, 1 - pos_ref[1])
+
+
+def input_keep_kernel(pos_ref, grads_ref, w_ref, out_ref):
+    input_part(grads_ref[...], w_ref, out_ref, pos_ref[1])
 
 
 def add_kernel(a_ref, b_ref, out_ref):
@@ -348,10 +350,12 @@
     down, got_hg, w_gate_up, down_w = lax.optimization_barrier((down, got_hg, w_gate_up, down_w))
 
     out = shaped((N_X, 48, HALF))
-    grads = (own, got, own_hg, got_hg)
-    send = call(input_send_kernel, out, pos, *grads, w_gate_up, name="input_send", flops=flops)
+    send, grads = call(
+        input_send_kernel, (out, shaped((2 * TOK, 2 * COLS))), pos, own, got, own_hg, got_hg, w_gate_up,
+        name="input_send", flops=4 * flops,
+    )
     other = lax.ppermute(send, "tensor", CORE_SWAP)
-    keep = call(input_keep_kernel, out, pos, *grads, w_gate_up, name="input_keep", flops=flops)
+    keep = call(input_keep_kernel, out, pos, grads, w_gate_up, name="input_keep", flops=4 * flops)
     parts = call(add_kernel, out, keep, other, name="add")
     parts = lax.all_to_all(parts, "tensor", 0, 0, axis_index_groups=X_GROUPS, tiled=True)
     parts = call(x_sum_kernel, shaped((N_Y * 24, QUARTER)), parts, name="x_sum", flops=35 * 10**8).reshape(N_Y, 24, QUARTER)

time: 164 us -> 163 us (level)
  no operation moved by 1% of the time
where the time goes in v6:
time: 163 us; the launch traced here: 162 us
  blocking collectives  71.5 us (44%)
  starting transfers between devices  39.8 us (24%)
  Pallas kernels  20.3 us (12%)
  between operations  14.3 us (9%)
  waiting for transfers between devices  11.4 us (7%)
  local copies, waits for them, and re-layouts  2.33 us (1%)
  other arithmetic  1.92 us (1%)
    all_to_all x1, blocking collectives, on_device(): lax.all_to_all(acts, 'tensor', 0, 0, axis_index_groups=X_GROUPS, tiled=True)  30.4 us
    all_to_all x1, blocking collectives, on_device(): lax.all_to_all(parts, ('dp', 'tensor'), 0, 0, axis_index_groups=Z_GROUPS,...  24.9 us
    ppermute x4, starting transfers between devices, on_device(): lax.ppermute(acts, ('dp', 'tensor'), turn)  22 us
    pallas_call x12, Pallas kernels, call(): pl.pallas_call(kernel, out_shape=out_shapes, in_specs=specs, out_specs=ja...  20.3 us
    all_to_all x1, blocking collectives, on_device(): lax.all_to_all(parts, 'tensor', 0, 0, axis_index_groups=X_GROUPS, tiled=T...  16.3 us
    ppermute x4, waiting for transfers between devices, on_device(): lax.ppermute(acts, ('dp', 'tensor'), turn)  6.74 us
    ppermute x1, starting transfers between devices, on_device(): got_hg = lax.ppermute(send, 'dp', Z_SWAP)  5.62 us
    ppermute x1, starting transfers between devices, on_device(): far = lax.ppermute(near, 'tensor', CORE_SWAP)  4.5 us
  transfers between devices with their start and end apart: 10, of which 5 were waited for; matrix products, arithmetic and copies ran while one was open for 0% of the time, Pallas kernels for 9%

profile of v6, /device:TPU:1, one launch (start us, length us, event | category | flops | bytes accessed | tf_op | source)
XLA Modules:
  0.0 161.5 jit_solution(6050605449050762986)
XLA Ops:
  7.2 0.0 copy-start.3
  7.2 0.0 copy-start.4
  7.2 0.0 all-gather.3.cloned.1.call-start
  7.2 2.3 %decode.1 = bf16[2,160,768]{2,1,0:T(8,128)(2,1)} custom-call(s32[320,256]{1,0:T(8,128)} %gate_ref.1, s32[320,256]{1,0:T(8,128)} %up_ref.1, s32[320,256]{1,0:T(8,128)} %codes_ref), custom_call_target="tpu_custom_call" | custom-call | flops 2621440 | bytes 1474560 | tf_op jit(solution)/shard_map/decode/pallas_call | solution.py:280
  9.5 0.0 all-gather.3.cloned.1.call-update
  9.5 0.0 reduce-scatter.2.cloned.1.call-start
  9.6 0.0 copy-done.3
  9.6 0.0 copy-done.4
  9.6 0.1 maximum_maximum_fusion
  9.7 10.9 %collective-permute-start.3 = (bf16[160,384]{1,0:T(8,128)(2,1)S(1)}, bf16[160,384]{1,0:T(8,128)(2,1)S(1)}, u32[]{:S(2)}, u32[]{:S(2)}) collective-permute-start(bf16[160,384]{1,0:T(8,128)(2,1)S(1)} %maximum_maximum_fusion), channel_id=1, source_target_pairs={{0,22},{1,23},{2,20},{3,21},{4,18},{5,19},{6,16},{7,17},{8,30},{9,... | collective-permute-start | bytes 368648 | tf_op jit(solution)/shard_map/ppermute | solution.py:317
  20.7 6.1 %collective-permute-start.2 = (bf16[160,384]{1,0:T(8,128)(2,1)S(1)}, bf16[160,384]{1,0:T(8,128)(2,1)S(1)}, u32[]{:S(2)}, u32[]{:S(2)}) collective-permute-start(bf16[160,384]{1,0:T(8,128)(2,1)S(1)} %maximum_maximum_fusion), channel_id=1, source_target_pairs={{0,20},{1,21},{2,22},{3,23},{4,16},{5,17},{6,18},{7,19},{8,28},{9,... | collective-permute-start | bytes 368648 | tf_op jit(solution)/shard_map/ppermute | solution.py:317
  26.8 2.1 %collective-permute-start.1 = (bf16[160,384]{1,0:T(8,128)(2,1)S(1)}, bf16[160,384]{1,0:T(8,128)(2,1)S(1)}, u32[]{:S(2)}, u32[]{:S(2)}) collective-permute-start(bf16[160,384]{1,0:T(8,128)(2,1)S(1)} %maximum_maximum_fusion), channel_id=1, source_target_pairs={{0,18},{1,19},{2,16},{3,17},{4,22},{5,23},{6,20},{7,21},{8,26},{9,... | collective-permute-start | bytes 368648 | tf_op jit(solution)/shard_map/ppermute | solution.py:317
  28.9 2.9 %collective-permute-start = (bf16[160,384]{1,0:T(8,128)(2,1)S(1)}, bf16[160,384]{1,0:T(8,128)(2,1)S(1)}, u32[]{:S(2)}, u32[]{:S(2)}) collective-permute-start(bf16[160,384]{1,0:T(8,128)(2,1)S(1)} %maximum_maximum_fusion), channel_id=1, source_target_pairs={{0,16},{1,17},{2,18},{3,19},{4,20},{5,21},{6,22},{7,23},{8,24},{9,... | collective-permute-start | bytes 368648 | tf_op jit(solution)/shard_map/ppermute | solution.py:317
  31.8 0.0 collective-permute-done.3
  31.8 0.0 collective-permute-done.2
  31.8 3.9 %collective-permute-done.1 = bf16[160,384]{1,0:T(8,128)(2,1)S(1)} collective-permute-done((bf16[160,384]{1,0:T(8,128)(2,1)S(1)}, bf16[160,384]{1,0:T(8,128)(2,1)S(1)}, u32[]{:S(2)}, u32[]{:S(2)}) %collective-permute-start.1) | collective-permute-done | bytes 122912 | tf_op jit(solution)/shard_map/ppermute | solution.py:317
  35.7 2.9 %collective-permute-done = bf16[160,384]{1,0:T(8,128)(2,1)S(1)} collective-permute-done((bf16[160,384]{1,0:T(8,128)(2,1)S(1)}, bf16[160,384]{1,0:T(8,128)(2,1)S(1)}, u32[]{:S(2)}, u32[]{:S(2)}) %collective-permute-start) | collective-permute-done | bytes 122912 | tf_op jit(solution)/shard_map/ppermute | solution.py:317
  38.5 0.1 pad_maximum_fusion
  38.6 0.2 broadcast_in_dim.2
  38.8 30.4 %all_to_all.15.acts_ref.near_ref = bf16[4,4,160,384]{3,2,1,0:T(8,128)(2,1)S(1)} all-to-all(bf16[4,4,160,384]{3,2,1,0:T(8,128)(2,1)S(1)} %broadcast_in_dim.2), channel_id=1, replica_groups={{0,8,16,24},{1,9,17,25},{2,10,18,26},{3,11,19,27},{4,12,20,28},{5,13,21..., dimensions={0} | all-to-all | bytes 3932160 | tf_op jit(solution)/shard_map/all_to_all | solution.py:319
  69.2 4.5 %collective-permute-start.4 = (bf16[4,4,160,384]{3,2,1,0:T(8,128)(2,1)S(1)}, bf16[4,4,160,384]{3,2,1,0:T(8,128)(2,1)}, u32[]{:S(2)}, u32[]{:S(2)}) collective-permute-start(bf16[4,4,160,384]{3,2,1,0:T(8,128)(2,1)S(1)} %all_to_all.15.acts_ref.near_ref), channel_id=1, source_target_pairs={{0,1},{1,0},{2,3},{3,2},{4,5},{5,4},{6,7},{7,6},{8,9},{9,8},{10,11... | collective-permute-start | bytes 5898248 | tf_op jit(solution)/shard_map/ppermute | solution.py:320
  73.7 0.1 pad_add_fusion.pos_ref
  73.8 2.9 %forward_near.1 = (f32[2,192,512]{2,1,0:T(8,128)S(1)}, bf16[8,160,512]{2,1,0:T(8,128)(2,1)S(1)}) custom-call(s32[4]{0:T(128)S(1)} %pad_add_fusion.pos_ref, bf16[4,4,160,384]{3,2,1,0:T(8,128)(2,1)S(1)} %all_to_all.15.acts_ref.near_ref, bf16[8,2,160,768]{3,2,1,0:T(8,128)(2,1)} %bitcast.13), custom_call_target="tpu_custom_call" | custom-call | flops 503316480 | bytes 7995408 | tf_op jit(solution)/shard_map/forward_near/pallas_call | solution.py:280
  76.7 0.7 collective-permute-done.4.acts_ref.far_ref
  77.4 3.1 %gate_up.1 = (f32[2,192,512]{2,1,0:T(8,128)S(1)}, bf16[2,192,512]{2,1,0:T(8,128)(2,1)S(1)}) custom-call(s32[4]{0:T(128)S(1)} %pad_add_fusion.pos_ref, bf16[4,4,160,384]{3,2,1,0:T(8,128)(2,1)} %collective-permute-done.4.acts_ref.far_ref, f32[2,192,512]{2,1,0:T(8,128)S(1)} %get-tuple-element.18.near_ref, bf16[8,160,512]{2,1,0:T(8,128)(2,1)S(1)} %get-tuple-element.19.w_far_ref), custom_call_target="tpu_custom_call" | custom-call | tf_op jit(solution)/shard_map/gate_up/pallas_call | solution.py:280
  80.5 3.6 %collective-permute-start.5 = (bf16[2,192,512]{2,1,0:T(8,128)(2,1)S(1)}, bf16[2,192,512]{2,1,0:T(8,128)(2,1)S(1)}, u32[]{:S(2)}, u32[]{:S(2)}) collective-permute-start(bf16[2,192,512]{2,1,0:T(8,128)(2,1)S(1)} %get-tuple-element.21), channel_id=1, source_target_pairs={{0,256},{32,288},{64,320},{96,352},{128,384},{160,416},{192,448},{... | collective-permute-start | bytes 1179656 | tf_op jit(solution)/shard_map/ppermute | solution.py:334
  84.1 0.0 copy-done
  84.1 3.6 %hidden_grad.1 = (f32[2,192,256]{2,1,0:T(8,128)S(1)}, bf16[2,192,256]{2,1,0:T(8,128)(2,1)}, bf16[2,2,320,768]{3,2,1,0:T(8,128)(2,1)S(1)}) custom-call(s32[4]{0:T(128)S(1)} %pad_add_fusion.pos_ref, bf16[4,4,160,384]{3,2,1,0:T(8,128)(2,1)S(1)} %all_to_all.15.acts_ref.near_ref, bf16[4,4,160,384]{3,2,1,0:T(8,128)(2,1)} %collective-permute-done.4.acts_ref.far_ref, ...), custom_call_target="tpu_custom_call" | custom-call | tf_op jit(solution)/shard_map/hidden_grad/pallas_call | solution.py:280
  87.8 5.6 %collective-permute-start.6 = (bf16[2,192,256]{2,1,0:T(8,128)(2,1)}, bf16[2,192,256]{2,1,0:T(8,128)(2,1)S(1)}, u32[]{:S(2)}, u32[]{:S(2)}) collective-permute-start(bf16[2,192,256]{2,1,0:T(8,128)(2,1)} %get-tuple-element.26), channel_id=1, source_target_pairs={{0,256},{32,288},{64,320},{96,352},{128,384},{160,416},{192,448},{... | collective-permute-start | bytes 589832 | tf_op jit(solution)/shard_map/ppermute | solution.py:340
  93.4 3.5 %collective-permute-done.5.got_ref = bf16[2,192,512]{2,1,0:T(8,128)(2,1)S(1)} collective-permute-done((bf16[2,192,512]{2,1,0:T(8,128)(2,1)S(1)}, bf16[2,192,512]{2,1,0:T(8,128)(2,1)S(1)}, u32[]{:S(2)}, u32[]{:S(2)}) %collective-permute-start.5) | collective-permute-done | bytes 393248 | tf_op jit(solution)/shard_map/ppermute | solution.py:334
  96.9 2.8 %down.1 = bf16[8,2,160,256]{3,2,1,0:T(8,128)(2,1)} custom-call(s32[4]{0:T(128)S(1)} %pad_add_fusion.pos_ref, bf16[2,2,320,768]{3,2,1,0:T(8,128)(2,1)S(1)} %get-tuple-element.25.grads_ref, f32[2,192,512]{2,1,0:T(8,128)S(1)} %get-tuple-element.20.own_ref, bf16[2,192,512]{2,1,0:T(8,128)(2,1)S(1)} %collective-permute-done.5.got_ref), custom_call_target="tpu_custom_call" | custom-call | tf_op jit(solution)/shard_map/down/pallas_call | solution.py:280
  99.7 0.0 reduce-scatter.2.cloned.1.call-update
  99.8 0.0 copy-done.2
  99.8 0.2 decode_down.1
  100.0 0.0 copy-start.1
  100.0 2.1 %copy-done.1 = bf16[16,160,768]{2,1,0:T(8,128)(2,1)S(1)} copy-done((bf16[16,160,768]{2,1,0:T(8,128)(2,1)S(1)}, bf16[16,160,768]{2,1,0:T(8,128)(2,1)}, u32[]{:S(2)}) %copy-start.1) | copy-done | bytes 3932184
  102.1 0.2 copy.8.w_ref
  102.2 0.0 collective-permute-done.6.got_hg_ref
  102.3 1.9 %input_send.1 = (bf16[4,48,2560]{2,1,0:T(8,128)(2,1)S(1)}, bf16[384,512]{1,0:T(8,128)(2,1)S(1)}) custom-call(s32[4]{0:T(128)S(1)} %pad_add_fusion.pos_ref, f32[2,192,512]{2,1,0:T(8,128)S(1)} %get-tuple-element.20.own_ref, bf16[2,192,512]{2,1,0:T(8,128)(2,1)S(1)} %collective-permute-done.5.got_ref, f32[2,192,256]{2,1,0:T(8,128)S(1)} %get-tuple-element.24.own_hg_ref, ...), custom_call_target="tpu_custom_call" | custom-call | flops 1006632960 | bytes 5767184 | tf_op jit(solution)/shard_map/input_send/pallas_call | solution.py:280
  104.2 4.0 %collective-permute-start.7 = (bf16[4,48,2560]{2,1,0:T(8,128)(2,1)S(1)}, bf16[4,48,2560]{2,1,0:T(8,128)(2,1)S(1)}, u32[]{:S(2)}, u32[]{:S(2)}) collective-permute-start(bf16[4,48,2560]{2,1,0:T(8,128)(2,1)S(1)} %get-tuple-element.32), channel_id=1, source_target_pairs={{0,1},{1,0},{2,3},{3,2},{4,5},{5,4},{6,7},{7,6},{8,9},{9,8},{10,11... | collective-permute-start | bytes 2949128 | tf_op jit(solution)/shard_map/ppermute | solution.py:357
  108.2 1.7 %input_keep.1.a_ref = bf16[4,48,2560]{2,1,0:T(8,128)(2,1)S(1)} custom-call(s32[4]{0:T(128)S(1)} %pad_add_fusion.pos_ref, bf16[384,512]{1,0:T(8,128)(2,1)S(1)} %get-tuple-element.31.grads_ref, bf16[8,2,160,512]{3,2,1,0:T(8,128)(2,1)S(1)} %copy.8.w_ref), custom_call_target="tpu_custom_call" | custom-call | flops 1006632960 | bytes 3997712 | tf_op jit(solution)/shard_map/input_keep/pallas_call | solution.py:280
  109.9 0.5 collective-permute-done.7.b_ref
  110.4 0.2 add.25
  110.6 16.3 %all_to_all.16.parts_ref = bf16[4,48,2560]{2,1,0:T(8,128)(2,1)S(1)} all-to-all(bf16[4,48,2560]{2,1,0:T(8,128)(2,1)S(1)} %add.25), channel_id=1, replica_groups={{0,8,16,24},{1,9,17,25},{2,10,18,26},{3,11,19,27},{4,12,20,28},{5,13,21..., dimensions={0} | all-to-all | bytes 1966080 | tf_op jit(solution)/shard_map/all_to_all | solution.py:360
  126.8 0.4 x_sum.1
  127.3 24.9 %all_to_all.17.parts_ref = bf16[8,24,640]{2,1,0:T(8,128)(2,1)S(1)} all-to-all(bf16[8,24,640]{2,1,0:T(8,128)(2,1)S(1)} %bitcast.16), channel_id=1, replica_groups={{0,2,4,6,256,258,260,262},{1,3,5,7,257,259,261,263},{8,10,12,14,264,266..., dimensions={0} | all-to-all | bytes 491520 | tf_op jit(solution)/shard_map/all_to_all | solution.py:362
  152.2 0.8 input_sum.1
  153.0 1.7 %convert_multiply_fusion = f32[320,256]{1,0:T(8,128)} fusion(f32[320,256]{1,0:T(8,128)S(1)} %decode_down.1, bf16[320,256]{1,0:T(8,128)(2,1)} %reduce-scatter.2.cloned.1.call-done), kind=kLoop, calls=%fused_computation.1 | loop fusion | flops 163840 | bytes 819200 | tf_op jit(solution)/shard_map/mul | solution.py:364
  (5 shorter events, 0.0 us)
Async XLA Ops:
  7.2 2.4 %copy-start.3 = (bf16[192,160]{0,1:T(8,128)(2,1)S(1)}, bf16[192,160]{0,1:T(8,128)(2,1)}, u32[]{:S(2)}) copy-start(bf16[192,160]{0,1:T(8,128)(2,1)} %param.5) | copy-start | bytes 184324
  7.2 2.4 %copy-start.4 = (bf16[192,160]{0,1:T(8,128)(2,1)S(1)}, bf16[192,160]{0,1:T(8,128)(2,1)}, u32[]{:S(2)}) copy-start(bf16[192,160]{0,1:T(8,128)(2,1)} %param.6) | copy-start | bytes 184324
  7.2 66.6 %all-gather.3.cloned.1.call-start = ((), (), s32[]{:S(2)}) async-start(), calls=%async_computation.5 | async-start | bytes 4423680 | tf_op jit(solution)/shard_map/all_gather | solution.py:310
  9.5 143.5 %reduce-scatter.2.cloned.1.call-start = ((), (), s32[]{:S(2)}) async-start(), calls=%async_computation.4 | async-start | bytes 1474560 | tf_op jit(solution)/shard_map/reduce_scatter | solution.py:347
  9.7 22.0 %collective-permute-start.3 = (bf16[160,384]{1,0:T(8,128)(2,1)S(1)}, bf16[160,384]{1,0:T(8,128)(2,1)S(1)}, u32[]{:S(2)}, u32[]{:S(2)}) collective-permute-start(bf16[160,384]{1,0:T(8,128)(2,1)S(1)} %maximum_maximum_fusion), channel_id=1, source_target_pairs={{0,22},{1,23},{2,20},{3,21},{4,18},{5,19},{6,16},{7,17},{8,30},{9,... | collective-permute-start | bytes 368648 | tf_op jit(solution)/shard_map/ppermute | solution.py:317
  20.7 11.1 %collective-permute-start.2 = (bf16[160,384]{1,0:T(8,128)(2,1)S(1)}, bf16[160,384]{1,0:T(8,128)(2,1)S(1)}, u32[]{:S(2)}, u32[]{:S(2)}) collective-permute-start(bf16[160,384]{1,0:T(8,128)(2,1)S(1)} %maximum_maximum_fusion), channel_id=1, source_target_pairs={{0,20},{1,21},{2,22},{3,23},{4,16},{5,17},{6,18},{7,19},{8,28},{9,... | collective-permute-start | bytes 368648 | tf_op jit(solution)/shard_map/ppermute | solution.py:317
  26.8 8.9 %collective-permute-start.1 = (bf16[160,384]{1,0:T(8,128)(2,1)S(1)}, bf16[160,384]{1,0:T(8,128)(2,1)S(1)}, u32[]{:S(2)}, u32[]{:S(2)}) collective-permute-start(bf16[160,384]{1,0:T(8,128)(2,1)S(1)} %maximum_maximum_fusion), channel_id=1, source_target_pairs={{0,18},{1,19},{2,16},{3,17},{4,22},{5,23},{6,20},{7,21},{8,26},{9,... | collective-permute-start | bytes 368648 | tf_op jit(solution)/shard_map/ppermute | solution.py:317
  28.9 9.6 %collective-permute-start = (bf16[160,384]{1,0:T(8,128)(2,1)S(1)}, bf16[160,384]{1,0:T(8,128)(2,1)S(1)}, u32[]{:S(2)}, u32[]{:S(2)}) collective-permute-start(bf16[160,384]{1,0:T(8,128)(2,1)S(1)} %maximum_maximum_fusion), channel_id=1, source_target_pairs={{0,16},{1,17},{2,18},{3,19},{4,20},{5,21},{6,22},{7,23},{8,24},{9,... | collective-permute-start | bytes 368648 | tf_op jit(solution)/shard_map/ppermute | solution.py:317
  69.2 8.2 %collective-permute-start.4 = (bf16[4,4,160,384]{3,2,1,0:T(8,128)(2,1)S(1)}, bf16[4,4,160,384]{3,2,1,0:T(8,128)(2,1)}, u32[]{:S(2)}, u32[]{:S(2)}) collective-permute-start(bf16[4,4,160,384]{3,2,1,0:T(8,128)(2,1)S(1)} %all_to_all.15.acts_ref.near_ref), channel_id=1, source_target_pairs={{0,1},{1,0},{2,3},{3,2},{4,5},{5,4},{6,7},{7,6},{8,9},{9,8},{10,11... | collective-permute-start | bytes 5898248 | tf_op jit(solution)/shard_map/ppermute | solution.py:320
  77.4 6.7 %copy-start = (bf16[16,160,768]{2,1,0:T(8,128)(2,1)S(1)}, bf16[16,160,768]{2,1,0:T(8,128)(2,1)}, u32[]{:S(2)}) copy-start(bf16[16,160,768]{2,1,0:T(8,128)(2,1)} %all-gather.3.cloned.1.call-done) | copy-start | bytes 11796484
  80.5 16.4 %collective-permute-start.5 = (bf16[2,192,512]{2,1,0:T(8,128)(2,1)S(1)}, bf16[2,192,512]{2,1,0:T(8,128)(2,1)S(1)}, u32[]{:S(2)}, u32[]{:S(2)}) collective-permute-start(bf16[2,192,512]{2,1,0:T(8,128)(2,1)S(1)} %get-tuple-element.21), channel_id=1, source_target_pairs={{0,256},{32,288},{64,320},{96,352},{128,384},{160,416},{192,448},{... | collective-permute-start | bytes 1179656 | tf_op jit(solution)/shard_map/ppermute | solution.py:334
  87.8 14.5 %collective-permute-start.6 = (bf16[2,192,256]{2,1,0:T(8,128)(2,1)}, bf16[2,192,256]{2,1,0:T(8,128)(2,1)S(1)}, u32[]{:S(2)}, u32[]{:S(2)}) collective-permute-start(bf16[2,192,256]{2,1,0:T(8,128)(2,1)} %get-tuple-element.26), channel_id=1, source_target_pairs={{0,256},{32,288},{64,320},{96,352},{128,384},{160,416},{192,448},{... | collective-permute-start | bytes 589832 | tf_op jit(solution)/shard_map/ppermute | solution.py:340
  96.9 2.8 %copy-start.2 = (s32[320,256]{1,0:T(8,128)S(1)}, s32[320,256]{1,0:T(8,128)}, u32[]{:S(2)}) copy-start(s32[320,256]{1,0:T(8,128)} %codes_ref) | copy-start | bytes 983044
  100.0 2.1 %copy-start.1 = (bf16[16,160,768]{2,1,0:T(8,128)(2,1)S(1)}, bf16[16,160,768]{2,1,0:T(8,128)(2,1)}, u32[]{:S(2)}) copy-start(bf16[16,160,768]{2,1,0:T(8,128)(2,1)} %all-gather.3.cloned.1.call-done) | copy-start | bytes 11796484
  104.2 6.2 %collective-permute-start.7 = (bf16[4,48,2560]{2,1,0:T(8,128)(2,1)S(1)}, bf16[4,48,2560]{2,1,0:T(8,128)(2,1)S(1)}, u32[]{:S(2)}, u32[]{:S(2)}) collective-permute-start(bf16[4,48,2560]{2,1,0:T(8,128)(2,1)S(1)} %get-tuple-element.32), channel_id=1, source_target_pairs={{0,1},{1,0},{2,3},{3,2},{4,5},{5,4},{6,7},{7,6},{8,9},{9,8},{10,11... | collective-permute-start | bytes 2949128 | tf_op jit(solution)/shard_map/ppermute | solution.py:357
Sparse Core Ops, SparseCore 0:
  10.1 60.1 all-gather.2
  99.9 46.9 reduce-scatter.1

commit v7 on v5

--- a/solution.py
+++ b/solution.py
@@ -335,9 +335,10 @@
         (shaped(hidden_grad_shape, f32), shaped(hidden_grad_shape), shaped((2, 2, N_ZL * HALF_FEAT, 4 * TOK))),
         pos, near, far, w, name="hidden_grad", hbm=(2,), scratch=acts_space,
     )
-    got_hg = lax.ppermute(send, "dp", Z_SWAP)
     w_own, codes, _ = lax.optimization_barrier((w, down_codes, own_hg))
     down_w = call(decode_down_kernel, shaped((ROWS, COLS), f32), codes, name="decode_down", flops=ROWS * COLS * 32)
+    send, down_w = lax.optimization_barrier((send, down_w))
+    got_hg = lax.ppermute(send, "dp", Z_SWAP)
     w_gate_up = call(copy_kernel, shaped((N_Y, 2, FEAT, 2 * COLS)), w_own, name="copy", flops=flops)
 
     got, own_hg = lax.optimization_barrier((got, own_hg))

time: 164 us -> 163 us (level)
  transfers between devices with their start and end apart: 10 -> 10, of which waited for: 5 -> 6; matrix products, arithmetic and copies ran while one was open for 0% -> 0% of each run, Pallas kernels for 9% -> 9%
where the time goes in v7:
time: 163 us; the launch traced here: 161 us
  blocking collectives  71 us (44%)
  starting transfers between devices  39.3 us (24%)
  Pallas kernels  21 us (13%)
  between operations  14.3 us (9%)
  waiting for transfers between devices  11.5 us (7%)
  local copies, waits for them, and re-layouts  2.34 us (1%)
  other arithmetic  1.92 us (1%)
    all_to_all x1, blocking collectives, on_device(): lax.all_to_all(acts, 'tensor', 0, 0, axis_index_groups=X_GROUPS, tiled=True)  30.4 us
    all_to_all x1, blocking collectives, on_device(): lax.all_to_all(parts, ('dp', 'tensor'), 0, 0, axis_index_groups=Z_GROUPS,...  24.4 us
    ppermute x4, starting transfers between devices, on_device(): lax.ppermute(acts, ('dp', 'tensor'), turn)  22 us
    pallas_call x12, Pallas kernels, call(): pl.pallas_call(kernel, out_shape=out_shapes, in_specs=specs, out_specs=ja...  21 us
    all_to_all x1, blocking collectives, on_device(): lax.all_to_all(parts, 'tensor', 0, 0, axis_index_groups=X_GROUPS, tiled=T...  16.3 us
    ppermute x4, waiting for transfers between devices, on_device(): lax.ppermute(acts, ('dp', 'tensor'), turn)  6.74 us
    ppermute x1, starting transfers between devices, on_device(): got_hg = lax.ppermute(send, 'dp', Z_SWAP)  5.9 us
    ppermute x1, starting transfers between devices, on_device(): far = lax.ppermute(near, 'tensor', CORE_SWAP)  4.5 us
  transfers between devices with their start and end apart: 10, of which 6 were waited for; matrix products, arithmetic and copies ran while one was open for 0% of the time, Pallas kernels for 9%

profile of v7, /device:TPU:1, one launch (start us, length us, event | category | flops | bytes accessed | tf_op | source)
XLA Modules:
  0.0 161.3 jit_solution(16676422745547190122)
XLA Ops:
  7.2 0.0 copy-start.3
  7.2 0.0 copy-start.4
  7.2 0.0 all-gather.3.cloned.1.call-start
  7.2 2.6 %decode.1 = bf16[2,160,768]{2,1,0:T(8,128)(2,1)} custom-call(s32[320,256]{1,0:T(8,128)} %gate_ref.1, s32[320,256]{1,0:T(8,128)} %up_ref.1, s32[320,256]{1,0:T(8,128)} %codes_ref), custom_call_target="tpu_custom_call" | custom-call | flops 2621440 | bytes 1474560 | tf_op jit(solution)/shard_map/decode/pallas_call | solution.py:278
  9.9 0.0 all-gather.3.cloned.1.call-update
  9.9 0.0 reduce-scatter.2.cloned.1.call-start
  9.9 0.0 copy-done.3
  9.9 0.0 copy-done.4
  10.0 0.1 maximum_maximum_fusion
  10.1 10.9 %collective-permute-start.3 = (bf16[160,384]{1,0:T(8,128)(2,1)S(1)}, bf16[160,384]{1,0:T(8,128)(2,1)S(1)}, u32[]{:S(2)}, u32[]{:S(2)}) collective-permute-start(bf16[160,384]{1,0:T(8,128)(2,1)S(1)} %maximum_maximum_fusion), channel_id=1, source_target_pairs={{0,22},{1,23},{2,20},{3,21},{4,18},{5,19},{6,16},{7,17},{8,30},{9,... | collective-permute-start | bytes 368648 | tf_op jit(solution)/shard_map/ppermute | solution.py:315
  21.0 6.1 %collective-permute-start.2 = (bf16[160,384]{1,0:T(8,128)(2,1)S(1)}, bf16[160,384]{1,0:T(8,128)(2,1)S(1)}, u32[]{:S(2)}, u32[]{:S(2)}) collective-permute-start(bf16[160,384]{1,0:T(8,128)(2,1)S(1)} %maximum_maximum_fusion), channel_id=1, source_target_pairs={{0,20},{1,21},{2,22},{3,23},{4,16},{5,17},{6,18},{7,19},{8,28},{9,... | collective-permute-start | bytes 368648 | tf_op jit(solution)/shard_map/ppermute | solution.py:315
  27.1 2.1 %collective-permute-start.1 = (bf16[160,384]{1,0:T(8,128)(2,1)S(1)}, bf16[160,384]{1,0:T(8,128)(2,1)S(1)}, u32[]{:S(2)}, u32[]{:S(2)}) collective-permute-start(bf16[160,384]{1,0:T(8,128)(2,1)S(1)} %maximum_maximum_fusion), channel_id=1, source_target_pairs={{0,18},{1,19},{2,16},{3,17},{4,22},{5,23},{6,20},{7,21},{8,26},{9,... | collective-permute-start | bytes 368648 | tf_op jit(solution)/shard_map/ppermute | solution.py:315
  29.2 2.9 %collective-permute-start = (bf16[160,384]{1,0:T(8,128)(2,1)S(1)}, bf16[160,384]{1,0:T(8,128)(2,1)S(1)}, u32[]{:S(2)}, u32[]{:S(2)}) collective-permute-start(bf16[160,384]{1,0:T(8,128)(2,1)S(1)} %maximum_maximum_fusion), channel_id=1, source_target_pairs={{0,16},{1,17},{2,18},{3,19},{4,20},{5,21},{6,22},{7,23},{8,24},{9,... | collective-permute-start | bytes 368648 | tf_op jit(solution)/shard_map/ppermute | solution.py:315
  32.1 0.0 collective-permute-done.3
  32.1 0.0 collective-permute-done.2
  32.1 3.9 %collective-permute-done.1 = bf16[160,384]{1,0:T(8,128)(2,1)S(1)} collective-permute-done((bf16[160,384]{1,0:T(8,128)(2,1)S(1)}, bf16[160,384]{1,0:T(8,128)(2,1)S(1)}, u32[]{:S(2)}, u32[]{:S(2)}) %collective-permute-start.1) | collective-permute-done | bytes 122912 | tf_op jit(solution)/shard_map/ppermute | solution.py:315
  36.0 2.9 %collective-permute-done = bf16[160,384]{1,0:T(8,128)(2,1)S(1)} collective-permute-done((bf16[160,384]{1,0:T(8,128)(2,1)S(1)}, bf16[160,384]{1,0:T(8,128)(2,1)S(1)}, u32[]{:S(2)}, u32[]{:S(2)}) %collective-permute-start) | collective-permute-done | bytes 122912 | tf_op jit(solution)/shard_map/ppermute | solution.py:315
  38.9 0.1 pad_maximum_fusion
  38.9 0.2 broadcast_in_dim.2
  39.1 30.4 %all_to_all.15.acts_ref.near_ref = bf16[4,4,160,384]{3,2,1,0:T(8,128)(2,1)S(1)} all-to-all(bf16[4,4,160,384]{3,2,1,0:T(8,128)(2,1)S(1)} %broadcast_in_dim.2), channel_id=1, replica_groups={{0,8,16,24},{1,9,17,25},{2,10,18,26},{3,11,19,27},{4,12,20,28},{5,13,21..., dimensions={0} | all-to-all | bytes 3932160 | tf_op jit(solution)/shard_map/all_to_all | solution.py:317
  69.5 4.5 %collective-permute-start.4 = (bf16[4,4,160,384]{3,2,1,0:T(8,128)(2,1)S(1)}, bf16[4,4,160,384]{3,2,1,0:T(8,128)(2,1)}, u32[]{:S(2)}, u32[]{:S(2)}) collective-permute-start(bf16[4,4,160,384]{3,2,1,0:T(8,128)(2,1)S(1)} %all_to_all.15.acts_ref.near_ref), channel_id=1, source_target_pairs={{0,1},{1,0},{2,3},{3,2},{4,5},{5,4},{6,7},{7,6},{8,9},{9,8},{10,11... | collective-permute-start | bytes 5898248 | tf_op jit(solution)/shard_map/ppermute | solution.py:318
  74.1 0.1 pad_add_fusion.pos_ref
  74.1 3.0 %forward_near.1 = (f32[2,192,512]{2,1,0:T(8,128)S(1)}, bf16[8,160,512]{2,1,0:T(8,128)(2,1)S(1)}) custom-call(s32[4]{0:T(128)S(1)} %pad_add_fusion.pos_ref, bf16[4,4,160,384]{3,2,1,0:T(8,128)(2,1)S(1)} %all_to_all.15.acts_ref.near_ref, bf16[8,2,160,768]{3,2,1,0:T(8,128)(2,1)} %bitcast.13), custom_call_target="tpu_custom_call" | custom-call | flops 503316480 | bytes 7995408 | tf_op jit(solution)/shard_map/forward_near/pallas_call | solution.py:278
  77.1 0.6 collective-permute-done.4.acts_ref.far_ref
  77.7 3.1 %gate_up.1 = (f32[2,192,512]{2,1,0:T(8,128)S(1)}, bf16[2,192,512]{2,1,0:T(8,128)(2,1)S(1)}) custom-call(s32[4]{0:T(128)S(1)} %pad_add_fusion.pos_ref, bf16[4,4,160,384]{3,2,1,0:T(8,128)(2,1)} %collective-permute-done.4.acts_ref.far_ref, f32[2,192,512]{2,1,0:T(8,128)S(1)} %get-tuple-element.18.near_ref, bf16[8,160,512]{2,1,0:T(8,128)(2,1)S(1)} %get-tuple-element.19.w_far_ref), custom_call_target="tpu_custom_call" | custom-call | tf_op jit(solution)/shard_map/gate_up/pallas_call | solution.py:278
  80.9 0.0 copy-start.2
  80.9 3.4 %collective-permute-start.5 = (bf16[2,192,512]{2,1,0:T(8,128)(2,1)S(1)}, bf16[2,192,512]{2,1,0:T(8,128)(2,1)S(1)}, u32[]{:S(2)}, u32[]{:S(2)}) collective-permute-start(bf16[2,192,512]{2,1,0:T(8,128)(2,1)S(1)} %get-tuple-element.21), channel_id=1, source_target_pairs={{0,256},{32,288},{64,320},{96,352},{128,384},{160,416},{192,448},{... | collective-permute-start | bytes 1179656 | tf_op jit(solution)/shard_map/ppermute | solution.py:332
  84.3 0.0 copy-done
  84.3 3.6 %hidden_grad.1 = (f32[2,192,256]{2,1,0:T(8,128)S(1)}, bf16[2,192,256]{2,1,0:T(8,128)(2,1)}, bf16[2,2,320,768]{3,2,1,0:T(8,128)(2,1)S(1)}) custom-call(s32[4]{0:T(128)S(1)} %pad_add_fusion.pos_ref, bf16[4,4,160,384]{3,2,1,0:T(8,128)(2,1)S(1)} %all_to_all.15.acts_ref.near_ref, bf16[4,4,160,384]{3,2,1,0:T(8,128)(2,1)} %collective-permute-done.4.acts_ref.far_ref, ...), custom_call_target="tpu_custom_call" | custom-call | tf_op jit(solution)/shard_map/hidden_grad/pallas_call | solution.py:278
  88.0 0.0 copy-done.2
  88.0 0.3 decode_down.1
  88.3 5.9 %collective-permute-start.6 = (bf16[2,192,256]{2,1,0:T(8,128)(2,1)}, bf16[2,192,256]{2,1,0:T(8,128)(2,1)S(1)}, u32[]{:S(2)}, u32[]{:S(2)}) collective-permute-start(bf16[2,192,256]{2,1,0:T(8,128)(2,1)} %get-tuple-element.28), channel_id=1, source_target_pairs={{0,256},{32,288},{64,320},{96,352},{128,384},{160,416},{192,448},{... | collective-permute-start | bytes 589832 | tf_op jit(solution)/shard_map/ppermute | solution.py:341
  94.2 3.2 %collective-permute-done.5.got_ref.refs_1_ = bf16[2,192,512]{2,1,0:T(8,128)(2,1)S(1)} collective-permute-done((bf16[2,192,512]{2,1,0:T(8,128)(2,1)S(1)}, bf16[2,192,512]{2,1,0:T(8,128)(2,1)S(1)}, u32[]{:S(2)}, u32[]{:S(2)}) %collective-permute-start.5) | collective-permute-done | bytes 393248 | tf_op jit(solution)/shard_map/ppermute | solution.py:332
  97.4 2.8 %down.1 = bf16[8,2,160,256]{3,2,1,0:T(8,128)(2,1)} custom-call(s32[4]{0:T(128)S(1)} %pad_add_fusion.pos_ref, bf16[2,2,320,768]{3,2,1,0:T(8,128)(2,1)S(1)} %get-tuple-element.25.grads_ref, f32[2,192,512]{2,1,0:T(8,128)S(1)} %get-tuple-element.20.own_ref.refs_0_, bf16[2,192,512]{2,1,0:T(8,128)(2,1)S(1)} %collective-permute-done.5.got_ref.refs_1_), custom_call_target="tpu_custom_call" | custom-call | tf_op jit(solution)/shard_map/down/pallas_call | solution.py:278
  100.2 0.0 reduce-scatter.2.cloned.1.call-update
  100.2 2.1 %copy-done.1 = bf16[16,160,768]{2,1,0:T(8,128)(2,1)S(1)} copy-done((bf16[16,160,768]{2,1,0:T(8,128)(2,1)S(1)}, bf16[16,160,768]{2,1,0:T(8,128)(2,1)}, u32[]{:S(2)}) %copy-start.1) | copy-done | bytes 3932184
  102.3 0.2 copy.8.refs_4_
  102.5 0.6 collective-permute-done.6.refs_3_
  103.2 1.9 %input_send.1 = bf16[4,48,2560]{2,1,0:T(8,128)(2,1)S(1)} custom-call(s32[4]{0:T(128)S(1)} %pad_add_fusion.pos_ref, f32[2,192,512]{2,1,0:T(8,128)S(1)} %get-tuple-element.20.own_ref.refs_0_, bf16[2,192,512]{2,1,0:T(8,128)(2,1)S(1)} %collective-permute-done.5.got_ref.refs_1_, f32[2,192,256]{2,1,0:T(8,128)S(1)} %get-tuple-element.24.refs_2_, ...), custom_call_target="tpu_custom_call" | custom-call | flops 251658240 | bytes 5373968 | tf_op jit(solution)/shard_map/input_send/pallas_call | solution.py:278
  105.1 3.4 %collective-permute-start.7 = (bf16[4,48,2560]{2,1,0:T(8,128)(2,1)S(1)}, bf16[4,48,2560]{2,1,0:T(8,128)(2,1)S(1)}, u32[]{:S(2)}, u32[]{:S(2)}) collective-permute-start(bf16[4,48,2560]{2,1,0:T(8,128)(2,1)S(1)} %input_send.1), channel_id=1, source_target_pairs={{0,1},{1,0},{2,3},{3,2},{4,5},{5,4},{6,7},{7,6},{8,9},{9,8},{10,11... | collective-permute-start | bytes 2949128 | tf_op jit(solution)/shard_map/ppermute | solution.py:354
  108.4 1.9 %input_keep.1.a_ref = bf16[4,48,2560]{2,1,0:T(8,128)(2,1)S(1)} custom-call(s32[4]{0:T(128)S(1)} %pad_add_fusion.pos_ref, f32[2,192,512]{2,1,0:T(8,128)S(1)} %get-tuple-element.20.own_ref.refs_0_, bf16[2,192,512]{2,1,0:T(8,128)(2,1)S(1)} %collective-permute-done.5.got_ref.refs_1_, f32[2,192,256]{2,1,0:T(8,128)S(1)} %get-tuple-element.24.refs_2_, ...), custom_call_target="tpu_custom_call" | custom-call | flops 251658240 | bytes 5373968 | tf_op jit(solution)/shard_map/input_keep/pallas_call | solution.py:278
  110.4 0.2 collective-permute-done.7.b_ref
  110.6 0.2 add.25
  110.8 16.3 %all_to_all.16.parts_ref = bf16[4,48,2560]{2,1,0:T(8,128)(2,1)S(1)} all-to-all(bf16[4,48,2560]{2,1,0:T(8,128)(2,1)S(1)} %add.25), channel_id=1, replica_groups={{0,8,16,24},{1,9,17,25},{2,10,18,26},{3,11,19,27},{4,12,20,28},{5,13,21..., dimensions={0} | all-to-all | bytes 1966080 | tf_op jit(solution)/shard_map/all_to_all | solution.py:357
  127.1 0.4 x_sum.1
  127.5 24.4 %all_to_all.17.parts_ref = bf16[8,24,640]{2,1,0:T(8,128)(2,1)S(1)} all-to-all(bf16[8,24,640]{2,1,0:T(8,128)(2,1)S(1)} %bitcast.16), channel_id=1, replica_groups={{0,2,4,6,256,258,260,262},{1,3,5,7,257,259,261,263},{8,10,12,14,264,266..., dimensions={0} | all-to-all | bytes 491520 | tf_op jit(solution)/shard_map/all_to_all | solution.py:359
  151.9 0.8 input_sum.1
  152.8 1.7 %convert_multiply_fusion = f32[320,256]{1,0:T(8,128)} fusion(f32[320,256]{1,0:T(8,128)S(1)} %decode_down.1, bf16[320,256]{1,0:T(8,128)(2,1)} %reduce-scatter.2.cloned.1.call-done), kind=kLoop, calls=%fused_computation.1 | loop fusion | flops 163840 | bytes 819200 | tf_op jit(solution)/shard_map/mul | solution.py:361
  (5 shorter events, 0.0 us)
Async XLA Ops:
  7.2 2.8 %copy-start.3 = (bf16[192,160]{0,1:T(8,128)(2,1)S(1)}, bf16[192,160]{0,1:T(8,128)(2,1)}, u32[]{:S(2)}) copy-start(bf16[192,160]{0,1:T(8,128)(2,1)} %param.5) | copy-start | bytes 184324
  7.2 2.8 %copy-start.4 = (bf16[192,160]{0,1:T(8,128)(2,1)S(1)}, bf16[192,160]{0,1:T(8,128)(2,1)}, u32[]{:S(2)}) copy-start(bf16[192,160]{0,1:T(8,128)(2,1)} %param.6) | copy-start | bytes 184324
  7.2 67.0 %all-gather.3.cloned.1.call-start = ((), (), s32[]{:S(2)}) async-start(), calls=%async_computation.5 | async-start | bytes 4423680 | tf_op jit(solution)/shard_map/all_gather | solution.py:308
  9.9 142.9 %reduce-scatter.2.cloned.1.call-start = ((), (), s32[]{:S(2)}) async-start(), calls=%async_computation.4 | async-start | bytes 1474560 | tf_op jit(solution)/shard_map/reduce_scatter | solution.py:346
  10.1 22.0 %collective-permute-start.3 = (bf16[160,384]{1,0:T(8,128)(2,1)S(1)}, bf16[160,384]{1,0:T(8,128)(2,1)S(1)}, u32[]{:S(2)}, u32[]{:S(2)}) collective-permute-start(bf16[160,384]{1,0:T(8,128)(2,1)S(1)} %maximum_maximum_fusion), channel_id=1, source_target_pairs={{0,22},{1,23},{2,20},{3,21},{4,18},{5,19},{6,16},{7,17},{8,30},{9,... | collective-permute-start | bytes 368648 | tf_op jit(solution)/shard_map/ppermute | solution.py:315
  21.0 11.1 %collective-permute-start.2 = (bf16[160,384]{1,0:T(8,128)(2,1)S(1)}, bf16[160,384]{1,0:T(8,128)(2,1)S(1)}, u32[]{:S(2)}, u32[]{:S(2)}) collective-permute-start(bf16[160,384]{1,0:T(8,128)(2,1)S(1)} %maximum_maximum_fusion), channel_id=1, source_target_pairs={{0,20},{1,21},{2,22},{3,23},{4,16},{5,17},{6,18},{7,19},{8,28},{9,... | collective-permute-start | bytes 368648 | tf_op jit(solution)/shard_map/ppermute | solution.py:315
  27.1 8.9 %collective-permute-start.1 = (bf16[160,384]{1,0:T(8,128)(2,1)S(1)}, bf16[160,384]{1,0:T(8,128)(2,1)S(1)}, u32[]{:S(2)}, u32[]{:S(2)}) collective-permute-start(bf16[160,384]{1,0:T(8,128)(2,1)S(1)} %maximum_maximum_fusion), channel_id=1, source_target_pairs={{0,18},{1,19},{2,16},{3,17},{4,22},{5,23},{6,20},{7,21},{8,26},{9,... | collective-permute-start | bytes 368648 | tf_op jit(solution)/shard_map/ppermute | solution.py:315
  29.2 9.6 %collective-permute-start = (bf16[160,384]{1,0:T(8,128)(2,1)S(1)}, bf16[160,384]{1,0:T(8,128)(2,1)S(1)}, u32[]{:S(2)}, u32[]{:S(2)}) collective-permute-start(bf16[160,384]{1,0:T(8,128)(2,1)S(1)} %maximum_maximum_fusion), channel_id=1, source_target_pairs={{0,16},{1,17},{2,18},{3,19},{4,20},{5,21},{6,22},{7,23},{8,24},{9,... | collective-permute-start | bytes 368648 | tf_op jit(solution)/shard_map/ppermute | solution.py:315
  69.5 8.2 %collective-permute-start.4 = (bf16[4,4,160,384]{3,2,1,0:T(8,128)(2,1)S(1)}, bf16[4,4,160,384]{3,2,1,0:T(8,128)(2,1)}, u32[]{:S(2)}, u32[]{:S(2)}) collective-permute-start(bf16[4,4,160,384]{3,2,1,0:T(8,128)(2,1)S(1)} %all_to_all.15.acts_ref.near_ref), channel_id=1, source_target_pairs={{0,1},{1,0},{2,3},{3,2},{4,5},{5,4},{6,7},{7,6},{8,9},{9,8},{10,11... | collective-permute-start | bytes 5898248 | tf_op jit(solution)/shard_map/ppermute | solution.py:318
  77.7 6.6 %copy-start = (bf16[16,160,768]{2,1,0:T(8,128)(2,1)S(1)}, bf16[16,160,768]{2,1,0:T(8,128)(2,1)}, u32[]{:S(2)}) copy-start(bf16[16,160,768]{2,1,0:T(8,128)(2,1)} %all-gather.3.cloned.1.call-done) | copy-start | bytes 11796484
  80.9 7.1 %copy-start.2 = (s32[320,256]{1,0:T(8,128)S(1)}, s32[320,256]{1,0:T(8,128)}, u32[]{:S(2)}) copy-start(s32[320,256]{1,0:T(8,128)} %codes_ref) | copy-start | bytes 983044
  80.9 16.5 %collective-permute-start.5 = (bf16[2,192,512]{2,1,0:T(8,128)(2,1)S(1)}, bf16[2,192,512]{2,1,0:T(8,128)(2,1)S(1)}, u32[]{:S(2)}, u32[]{:S(2)}) collective-permute-start(bf16[2,192,512]{2,1,0:T(8,128)(2,1)S(1)} %get-tuple-element.21), channel_id=1, source_target_pairs={{0,256},{32,288},{64,320},{96,352},{128,384},{160,416},{192,448},{... | collective-permute-start | bytes 1179656 | tf_op jit(solution)/shard_map/ppermute | solution.py:332
  88.3 14.9 %collective-permute-start.6 = (bf16[2,192,256]{2,1,0:T(8,128)(2,1)}, bf16[2,192,256]{2,1,0:T(8,128)(2,1)S(1)}, u32[]{:S(2)}, u32[]{:S(2)}) collective-permute-start(bf16[2,192,256]{2,1,0:T(8,128)(2,1)} %get-tuple-element.28), channel_id=1, source_target_pairs={{0,256},{32,288},{64,320},{96,352},{128,384},{160,416},{192,448},{... | collective-permute-start | bytes 589832 | tf_op jit(solution)/shard_map/ppermute | solution.py:341
  100.2 2.1 %copy-start.1 = (bf16[16,160,768]{2,1,0:T(8,128)(2,1)S(1)}, bf16[16,160,768]{2,1,0:T(8,128)(2,1)}, u32[]{:S(2)}) copy-start(bf16[16,160,768]{2,1,0:T(8,128)(2,1)} %all-gather.3.cloned.1.call-done) | copy-start | bytes 11796484
  105.1 5.5 %collective-permute-start.7 = (bf16[4,48,2560]{2,1,0:T(8,128)(2,1)S(1)}, bf16[4,48,2560]{2,1,0:T(8,128)(2,1)S(1)}, u32[]{:S(2)}, u32[]{:S(2)}) collective-permute-start(bf16[4,48,2560]{2,1,0:T(8,128)(2,1)S(1)} %input_send.1), channel_id=1, source_target_pairs={{0,1},{1,0},{2,3},{3,2},{4,5},{5,4},{6,7},{7,6},{8,9},{9,8},{10,11... | collective-permute-start | bytes 2949128 | tf_op jit(solution)/shard_map/ppermute | solution.py:354
Sparse Core Ops, SparseCore 0:
  10.1 60.1 all-gather.2
  100.3 46.8 reduce-scatter.1
